TPU v7x, 128 devices: a whole 4x4x4 slice. The times are simulated.
128 devices in a mesh: section: 2 (over x_lo), dp: 2 (over x_hi), seq: 32 (over y, z, core).
Axes of the slice: x: 4 (x_hi: 2, x_lo: 2; x = x_hi * 2 + x_lo), y: 4, z: 4, core: 2. Of those that a mesh axis runs over, the one named last changes fastest.
Arguments:
- inputs: bfloat16 [4, 2048, 1536], P('dp', 'seq'), may hold values from -6 to 6
- prefix: int32 [4], P('dp'), may hold values from 204 to 1024
- cotangent: bfloat16 [4, 2048, 1536], P('dp', 'seq'), may hold values from -6 to 6
- attn_gain: bfloat16 [2, 1536], P('section', ('dp', 'seq')), may hold values from 0.5 to 1.5
- w_query: bfloat16 [2, 1536, 1536], P('section', ('dp', 'seq')), may hold values from -0.15625 to 0.15625
- w_key: bfloat16 [2, 1536, 768], P('section', ('dp', 'seq')), may hold values from -0.15625 to 0.15625
- w_value: bfloat16 [2, 1536, 768], P('section', ('dp', 'seq')), may hold values from -0.15625 to 0.15625
- w_out: bfloat16 [2, 1536, 1536], P('section', ('dp', 'seq')), may hold values from -1.75 to 1.75
- mlp_gain: bfloat16 [2, 1536], P('section', ('dp', 'seq')), may hold values from 0.5 to 1.5
- w_gate: bfloat16 [2, 1536, 4096], P('section', ('dp', 'seq')), may hold values from -0.15625 to 0.15625
- w_up: bfloat16 [2, 1536, 4096], P('section', ('dp', 'seq')), may hold values from -0.15625 to 0.15625
- w_down: bfloat16 [2, 4096, 1536], P('section', ('dp', 'seq')), may hold values from -0.09375 to 0.09375
Outputs:
- layer_outs: bfloat16 [2, 4, 2048, 1536], P('section', 'dp', 'seq')
- layer_grads: bfloat16 [2, 4, 2048, 1536], P('section', 'dp', 'seq')
- grad_attn_gain: float32 [2, 1536], P('section', ('dp', 'seq'))
- grad_w_query: float32 [2, 1536, 1536], P('section', ('dp', 'seq'))
- grad_w_key: float32 [2, 1536, 768], P('section', ('dp', 'seq'))
- grad_w_value: float32 [2, 1536, 768], P('section', ('dp', 'seq'))
- grad_w_out: float32 [2, 1536, 1536], P('section', ('dp', 'seq'))
- grad_mlp_gain: float32 [2, 1536], P('section', ('dp', 'seq'))
- grad_w_gate: float32 [2, 1536, 4096], P('section', ('dp', 'seq'))
- grad_w_up: float32 [2, 1536, 4096], P('section', ('dp', 'seq'))
- grad_w_down: float32 [2, 4096, 1536], P('section', ('dp', 'seq'))
All inputs are finite; a program needn't handle non-finite values.
Results may differ from a plain program's by a relative error of at most 0.039.
Values may be sent and summed in bfloat16 or wider, within the bound.
A program may use at most 320 MiB of HBM per device.

v0:
```python
import math

import jax
import jax.numpy as jnp
from jax import lax
from jax.sharding import PartitionSpec as P

HEADS = 16
KV_HEADS = 8
HEAD = 96


eps_norm = 1e-05
rope_base = 100000.0
neg_fill = -1e30


def passed_along(x, axis, by):
    peers = lax.axis_size(axis)
    pairs = [(i, i + by) for i in range(peers) if 0 <= i + by < peers]
    return lax.ppermute(x, axis, pairs)


def rms_scale(hidden, gain):
    inverse = lax.rsqrt(jnp.mean(hidden * hidden, axis=-1, keepdims=True) + eps_norm)
    return hidden * inverse * gain


def rotate(heads_in, positions):
    half_size = heads_in.shape[-1] // 2
    frequency = rope_base ** (-jnp.arange(half_size, dtype=jnp.float32) * 2.0 / heads_in.shape[-1])
    angles = positions.astype(jnp.float32)[:, None] * frequency[None, :]
    cosine = jnp.concatenate([jnp.cos(angles), jnp.cos(angles)], -1)[:, None, :]
    sine_table = jnp.concatenate([jnp.sin(angles), jnp.sin(angles)], -1)[:, None, :]
    first_half = heads_in[..., :half_size]
    second_half = heads_in[..., half_size:]
    turned = jnp.concatenate([-second_half, first_half], -1)
    return heads_in * cosine + turned * sine_table


def swiglu(gate_in, up_in):
    return jax.nn.silu(gate_in) * up_in


def weight_grads_of(parts):
    (
        mixed_act,
        grad_low,
        normed_two,
        grad_gate,
        grad_upact,
        attended,
        branch_low,
        normed,
        grad_query,
        grad_key,
        grad_value,
    ) = parts
    grad_wdown = jnp.einsum("rf,rd->fd", mixed_act, grad_low, preferred_element_type=jnp.float32)
    grad_wgate = jnp.einsum("rd,rf->df", normed_two, grad_gate, preferred_element_type=jnp.float32)
    grad_wup = jnp.einsum("rd,rf->df", normed_two, grad_upact, preferred_element_type=jnp.float32)
    grad_wout = jnp.einsum("rq,rd->qd", attended, branch_low, preferred_element_type=jnp.float32)
    grad_wquery = jnp.einsum("rd,rq->dq", normed, grad_query, preferred_element_type=jnp.float32)
    grad_wkey = jnp.einsum("rd,rq->dq", normed, grad_key, preferred_element_type=jnp.float32)
    grad_wvalue = jnp.einsum("rd,rq->dq", normed, grad_value, preferred_element_type=jnp.float32)
    return (grad_wquery, grad_wkey, grad_wvalue, grad_wout, grad_wgate, grad_wup, grad_wdown)


def body(
    inputs,
    prefix,
    cotangent,
    attn_gain,
    w_query,
    w_key,
    w_value,
    w_out,
    mlp_gain,
    w_gate,
    w_up,
    w_down,
):
    micro_count, row_count, model_width = inputs.shape
    section_rank = lax.axis_index("section")
    seq_rank = lax.axis_index("seq")
    last_section = lax.axis_size("section") - 1
    tick_count = micro_count + last_section
    length = row_count * lax.axis_size("seq")
    head_group = HEADS // KV_HEADS
    score_scale = 1.0 / math.sqrt(HEAD)
    positions = seq_rank * row_count + jnp.arange(row_count, dtype=jnp.int32)
    key_pos = jnp.arange(length, dtype=jnp.int32)
    gathered = (
        lax.all_gather(attn_gain, ("dp", "seq"), axis=1, tiled=True),
        lax.all_gather(w_query, ("dp", "seq"), axis=1, tiled=True),
        lax.all_gather(w_key, ("dp", "seq"), axis=1, tiled=True),
        lax.all_gather(w_value, ("dp", "seq"), axis=1, tiled=True),
        lax.all_gather(w_out, ("dp", "seq"), axis=1, tiled=True),
        lax.all_gather(mlp_gain, ("dp", "seq"), axis=1, tiled=True),
        lax.all_gather(w_gate, ("dp", "seq"), axis=1, tiled=True),
        lax.all_gather(w_up, ("dp", "seq"), axis=1, tiled=True),
        lax.all_gather(w_down, ("dp", "seq"), axis=1, tiled=True),
    )
    weights_fwd = tuple((gathered_piece[0] for gathered_piece in gathered))

    def masked_scores(queries_rot, keys_all, prefix_len):
        scores = (
            jnp.einsum(
                "qgrd,kgd->grqk",
                queries_rot.reshape(row_count, KV_HEADS, head_group, HEAD),
                keys_all.reshape(length, KV_HEADS, HEAD),
                preferred_element_type=jnp.float32,
            )
            * score_scale
        )
        allowed = (key_pos[None, :] <= positions[:, None]) | (key_pos[None, :] < prefix_len)
        return jnp.where(allowed, scores, neg_fill)

    def backward(grad_out, kept_state, prefix_len, weight_set, is_valid):
        (
            gain_attn,
            weight_query,
            weight_key,
            weight_value,
            weight_out,
            gain_mlp,
            weight_gate,
            weight_up,
            weight_down,
        ) = weight_set
        (
            hidden_low,
            normed,
            queries_rot,
            keys_all,
            values_all,
            log_total,
            attended,
            middle,
            normed_two,
            gate_act,
            up_act,
            mixed_act,
        ) = kept_state
        grad_low = grad_out.astype(jnp.bfloat16)
        grad_mixed = jnp.einsum(
            "rd,fd->rf", grad_low, weight_down, preferred_element_type=jnp.float32
        )
        _, swiglu_back = jax.vjp(swiglu, gate_act, up_act)
        grad_gate, grad_upact = swiglu_back(grad_mixed)
        grad_gate = grad_gate.astype(jnp.bfloat16)
        grad_upact = grad_upact.astype(jnp.bfloat16)
        grad_normed_two = jnp.einsum(
            "rf,df->rd", grad_gate, weight_gate, preferred_element_type=jnp.float32
        ) + jnp.einsum("rf,df->rd", grad_upact, weight_up, preferred_element_type=jnp.float32)
        _, norm_back_two = jax.vjp(rms_scale, middle, gain_mlp.astype(jnp.float32))
        grad_mid_part, grad_gain_mlp = norm_back_two(grad_normed_two)
        grad_middle = grad_out + grad_mid_part
        branch_low = grad_middle.astype(jnp.bfloat16)
        grad_att = jnp.einsum(
            "rd,qd->rq", branch_low, weight_out, preferred_element_type=jnp.float32
        ).astype(jnp.bfloat16)
        queries_four = queries_rot.reshape(row_count, KV_HEADS, head_group, HEAD)
        keys_three = keys_all.reshape(length, KV_HEADS, HEAD)
        values_three = values_all.reshape(length, KV_HEADS, HEAD)
        grad_att_four = grad_att.reshape(row_count, KV_HEADS, head_group, HEAD)
        scores = masked_scores(queries_rot, keys_all, prefix_len)
        soft_probs = jnp.exp(scores - log_total)
        grad_probs = jnp.einsum(
            "qgrd,kgd->grqk", grad_att_four, values_three, preferred_element_type=jnp.float32
        )
        row_delta = jnp.sum(soft_probs * grad_probs, axis=-1, keepdims=True)
        grad_scores = (soft_probs * (grad_probs - row_delta)).astype(jnp.bfloat16)
        grad_vpart = jnp.einsum(
            "grqk,qgrd->kgd",
            soft_probs.astype(jnp.bfloat16),
            grad_att_four,
            preferred_element_type=jnp.float32,
        ).reshape(length, KV_HEADS * HEAD)
        grad_kpart = (
            jnp.einsum(
                "grqk,qgrd->kgd", grad_scores, queries_four, preferred_element_type=jnp.float32
            )
            * score_scale
        ).reshape(length, KV_HEADS * HEAD)
        grad_qrot = (
            jnp.einsum(
                "grqk,kgd->qgrd", grad_scores, keys_three, preferred_element_type=jnp.float32
            )
            * score_scale
        ).reshape(row_count, HEADS, HEAD)
        grad_keys_own, grad_values_own = (
            lax.psum_scatter(
                grad_kpart.astype(jnp.bfloat16), "seq", scatter_dimension=0, tiled=True
            ).astype(jnp.float32),
            lax.psum_scatter(
                grad_vpart.astype(jnp.bfloat16), "seq", scatter_dimension=0, tiled=True
            ).astype(jnp.float32),
        )
        _, rope_back_query = jax.vjp(
            lambda field_in: rotate(field_in, positions),
            jnp.zeros((row_count, HEADS, HEAD), jnp.float32),
        )
        _, rope_back_key = jax.vjp(
            lambda field_in: rotate(field_in, positions),
            jnp.zeros((row_count, KV_HEADS, HEAD), jnp.float32),
        )
        grad_query = (
            rope_back_query(grad_qrot)[0].reshape(row_count, HEADS * HEAD).astype(jnp.bfloat16)
        )
        grad_key = (
            rope_back_key(grad_keys_own.reshape(row_count, KV_HEADS, HEAD))[0]
            .reshape(row_count, KV_HEADS * HEAD)
            .astype(jnp.bfloat16)
        )
        grad_value = grad_values_own.astype(jnp.bfloat16)
        grad_normed = (
            jnp.einsum("rq,dq->rd", grad_query, weight_query, preferred_element_type=jnp.float32)
            + jnp.einsum("rq,dq->rd", grad_key, weight_key, preferred_element_type=jnp.float32)
            + jnp.einsum("rq,dq->rd", grad_value, weight_value, preferred_element_type=jnp.float32)
        )
        _, norm_back_one = jax.vjp(
            rms_scale, hidden_low.astype(jnp.float32), gain_attn.astype(jnp.float32)
        )
        grad_hid_part, grad_gain_attn = norm_back_one(grad_normed)
        grad_hidden = grad_middle + grad_hid_part

        def keep_valid(field):
            return jnp.where(is_valid, field, jnp.zeros_like(field))

        parts = (
            mixed_act,
            keep_valid(grad_low),
            normed_two,
            keep_valid(grad_gate),
            keep_valid(grad_upact),
            attended,
            keep_valid(branch_low),
            normed,
            keep_valid(grad_query),
            keep_valid(grad_key),
            keep_valid(grad_value),
        )
        gains = (keep_valid(grad_gain_attn), keep_valid(grad_gain_mlp))
        return (grad_hidden.astype(jnp.bfloat16), gains, parts)

    recv_act = jnp.zeros((row_count, model_width), jnp.bfloat16)
    outs_buffer = jnp.zeros((micro_count, row_count, model_width), jnp.bfloat16)
    kept_list = []
    for tick_index in range(tick_count):
        batch_index = tick_index - section_rank
        is_valid = (batch_index >= 0) & (batch_index < micro_count)
        clipped = jnp.clip(batch_index, 0, micro_count - 1)
        own_input = lax.dynamic_index_in_dim(inputs, clipped, 0, keepdims=False)
        layer_input = jnp.where(section_rank == 0, own_input, recv_act)
        prefix_len = lax.dynamic_index_in_dim(prefix, clipped, 0, keepdims=False)
        (
            forward_gain_attn,
            forward_weight_query,
            forward_weight_key,
            forward_weight_value,
            forward_weight_out,
            forward_gain_mlp,
            forward_weight_gate,
            forward_weight_up,
            forward_weight_down,
        ) = weights_fwd
        hidden = layer_input.astype(jnp.float32)
        forward_normed = rms_scale(hidden, forward_gain_attn.astype(jnp.float32)).astype(
            jnp.bfloat16
        )
        queries = jnp.dot(forward_normed, forward_weight_query, preferred_element_type=jnp.float32)
        keys_pre = jnp.dot(forward_normed, forward_weight_key, preferred_element_type=jnp.float32)
        values_low = jnp.dot(
            forward_normed, forward_weight_value, preferred_element_type=jnp.float32
        ).astype(jnp.bfloat16)
        forward_queries_rot = (
            rotate(queries.reshape(row_count, HEADS, HEAD), positions)
            .astype(jnp.bfloat16)
            .reshape(row_count, HEADS * HEAD)
        )
        keys_rot = (
            rotate(keys_pre.reshape(row_count, KV_HEADS, HEAD), positions)
            .astype(jnp.bfloat16)
            .reshape(row_count, KV_HEADS * HEAD)
        )
        forward_keys_all = lax.all_gather(keys_rot, "seq", axis=0, tiled=True)
        forward_values_all = lax.all_gather(values_low, "seq", axis=0, tiled=True)
        forward_scores = masked_scores(forward_queries_rot, forward_keys_all, prefix_len)
        row_top = jnp.max(forward_scores, axis=-1, keepdims=True)
        forward_log_total = row_top + jnp.log(
            jnp.sum(jnp.exp(forward_scores - row_top), axis=-1, keepdims=True)
        )
        forward_soft_probs = jnp.exp(forward_scores - forward_log_total).astype(jnp.bfloat16)
        forward_attended = (
            jnp.einsum(
                "grqk,kgd->qgrd",
                forward_soft_probs,
                forward_values_all.reshape(length, KV_HEADS, HEAD),
                preferred_element_type=jnp.float32,
            )
            .reshape(row_count, HEADS * HEAD)
            .astype(jnp.bfloat16)
        )
        forward_middle = hidden + jnp.dot(
            forward_attended, forward_weight_out, preferred_element_type=jnp.float32
        )
        forward_normed_two = rms_scale(forward_middle, forward_gain_mlp.astype(jnp.float32)).astype(
            jnp.bfloat16
        )
        forward_gate_act = jnp.dot(
            forward_normed_two, forward_weight_gate, preferred_element_type=jnp.float32
        )
        forward_up_act = jnp.dot(
            forward_normed_two, forward_weight_up, preferred_element_type=jnp.float32
        )
        forward_mixed_act = swiglu(forward_gate_act, forward_up_act).astype(jnp.bfloat16)
        result = forward_middle + jnp.dot(
            forward_mixed_act, forward_weight_down, preferred_element_type=jnp.float32
        )
        forward_kept_state = (
            layer_input,
            forward_normed,
            forward_queries_rot,
            forward_keys_all,
            forward_values_all,
            forward_log_total,
            forward_attended,
            forward_middle,
            forward_normed_two,
            forward_gate_act,
            forward_up_act,
            forward_mixed_act,
        )
        layer_output = result.astype(jnp.bfloat16)
        kept_state = forward_kept_state
        kept_list.append(kept_state)
        previous = lax.dynamic_index_in_dim(outs_buffer, clipped, 0, keepdims=False)
        outs_buffer = lax.dynamic_update_index_in_dim(
            outs_buffer, jnp.where(is_valid, layer_output, previous), clipped, 0
        )
        if tick_index < tick_count - 1:
            recv_act = passed_along(layer_output, "section", 1)
    stacked = tuple(
        (
            jnp.stack([kept_entry[slot] for kept_entry in kept_list])
            for slot in range(len(kept_list[0]))
        )
    )
    regathered = (
        lax.all_gather(attn_gain, ("dp", "seq"), axis=1, tiled=True),
        lax.all_gather(w_query, ("dp", "seq"), axis=1, tiled=True),
        lax.all_gather(w_key, ("dp", "seq"), axis=1, tiled=True),
        lax.all_gather(w_value, ("dp", "seq"), axis=1, tiled=True),
        lax.all_gather(w_out, ("dp", "seq"), axis=1, tiled=True),
        lax.all_gather(mlp_gain, ("dp", "seq"), axis=1, tiled=True),
        lax.all_gather(w_gate, ("dp", "seq"), axis=1, tiled=True),
        lax.all_gather(w_up, ("dp", "seq"), axis=1, tiled=True),
        lax.all_gather(w_down, ("dp", "seq"), axis=1, tiled=True),
    )
    weights_bwd = tuple((gathered_piece[0] for gathered_piece in regathered))
    gain_totals = (jnp.zeros((model_width,), jnp.float32), jnp.zeros((model_width,), jnp.float32))
    parts_list = []
    recv_grad = jnp.zeros((row_count, model_width), jnp.bfloat16)
    grads_buffer = jnp.zeros((micro_count, row_count, model_width), jnp.bfloat16)
    for tick_index in range(tick_count):
        batch_index = tick_index - (last_section - section_rank)
        is_valid = (batch_index >= 0) & (batch_index < micro_count)
        clipped = jnp.clip(batch_index, 0, micro_count - 1)
        fwd_tick = jnp.clip(batch_index + section_rank, 0, tick_count - 1)
        kept_state = tuple(
            (
                lax.dynamic_index_in_dim(stacked_field, fwd_tick, 0, keepdims=False)
                for stacked_field in stacked
            )
        )
        own_cot = lax.dynamic_index_in_dim(cotangent, clipped, 0, keepdims=False)
        grad_input = jnp.where(
            section_rank == last_section, own_cot.astype(jnp.float32), recv_grad.astype(jnp.float32)
        )
        prefix_len = lax.dynamic_index_in_dim(prefix, clipped, 0, keepdims=False)
        grad_low_in, gains, parts = backward(
            grad_input, kept_state, prefix_len, weights_bwd, is_valid
        )
        parts_list.append(parts)
        gain_totals = (gain_totals[0] + gains[0], gain_totals[1] + gains[1])
        previous = lax.dynamic_index_in_dim(grads_buffer, clipped, 0, keepdims=False)
        grads_buffer = lax.dynamic_update_index_in_dim(
            grads_buffer, jnp.where(is_valid, grad_low_in, previous), clipped, 0
        )
        if tick_index < tick_count - 1:
            recv_grad = passed_along(grad_low_in, "section", -1)
    joined = tuple(
        (
            jnp.concatenate([part_entry[slot] for part_entry in parts_list], 0)
            for slot in range(len(parts_list[0]))
        )
    )
    wq, wk, wv, wo, wg, wu, wd = weight_grads_of(joined)
    full_set = (gain_totals[0], wq, wk, wv, wo, gain_totals[1], wg, wu, wd)
    sums = (
        lax.psum_scatter(full_set[0][None], ("dp", "seq"), scatter_dimension=1, tiled=True),
        lax.psum_scatter(full_set[1][None], ("dp", "seq"), scatter_dimension=1, tiled=True),
        lax.psum_scatter(full_set[2][None], ("dp", "seq"), scatter_dimension=1, tiled=True),
        lax.psum_scatter(full_set[3][None], ("dp", "seq"), scatter_dimension=1, tiled=True),
        lax.psum_scatter(full_set[4][None], ("dp", "seq"), scatter_dimension=1, tiled=True),
        lax.psum_scatter(full_set[5][None], ("dp", "seq"), scatter_dimension=1, tiled=True),
        lax.psum_scatter(full_set[6][None], ("dp", "seq"), scatter_dimension=1, tiled=True),
        lax.psum_scatter(full_set[7][None], ("dp", "seq"), scatter_dimension=1, tiled=True),
        lax.psum_scatter(full_set[8][None], ("dp", "seq"), scatter_dimension=1, tiled=True),
    )
    return (
        outs_buffer[None],
        grads_buffer[None],
        sums[0],
        sums[1],
        sums[2],
        sums[3],
        sums[4],
        sums[5],
        sums[6],
        sums[7],
        sums[8],
    )


def solution(mesh):
    return jax.shard_map(
        body,
        mesh=mesh,
        in_specs=(
            P("dp", "seq", None),
            P("dp"),
            P("dp", "seq", None),
            P("section", ("dp", "seq")),
            P("section", ("dp", "seq"), None),
            P("section", ("dp", "seq"), None),
            P("section", ("dp", "seq"), None),
            P("section", ("dp", "seq"), None),
            P("section", ("dp", "seq")),
            P("section", ("dp", "seq"), None),
            P("section", ("dp", "seq"), None),
            P("section", ("dp", "seq"), None),
        ),
        out_specs=(
            P("section", "dp", "seq", None),
            P("section", "dp", "seq", None),
            P("section", ("dp", "seq")),
            P("section", ("dp", "seq"), None),
            P("section", ("dp", "seq"), None),
            P("section", ("dp", "seq"), None),
            P("section", ("dp", "seq"), None),
            P("section", ("dp", "seq")),
            P("section", ("dp", "seq"), None),
            P("section", ("dp", "seq"), None),
            P("section", ("dp", "seq"), None),
        ),
        check_vma=False,
    )
```

profile of v0, /device:TPU:1, one launch (start us, length us, event | category | flops | bytes accessed | tf_op | source)
XLA Modules:
  0.0 3050.3 jit_solution(4998061939986792980)
XLA Ops:
  13.1 167.6 %all-reduce.17 = (bf16[1536]{0:T(1024)(128)(2,1)S(1)}, bf16[1536]{0:T(1024)(128)(2,1)S(1)}) all-reduce(bf16[1536]{0:T(1024)(128)(2,1)S(1)} %dynamic-update-slice, bf16[1536]{0:T(1024)(128)(2,1)S(1)} %dynamic-update-slice.1), channel_id=1, replica_groups=mesh['section'=2,'dp'=2,'seq'=32] {'dp','seq'}, use_global_device_ids=true, to_apply=%add.12 | all-reduce | flops 3072 | bytes 12288
  199.2 26.5 all-gather.22.cloned.1.call-done
  237.7 34.5 %all-gather.20.cloned.1.call-done = bf16[2048,768]{1,0:T(8,128)(2,1)} async-done(((bf16[64,768]{1,0:T(8,128)(2,1)}), bf16[2048,768]{1,0:T(8,128)(2,1)}) %all-gather.20.cloned.1.call-update) | async-done | bytes 3145744 | tf_op jit(solution)/shard_map/all_gather | solution.py:287
  275.3 44.0 %all-gather.16.cloned.1.call-done = bf16[2048,768]{1,0:T(8,128)(2,1)} async-done(((bf16[64,768]{1,0:T(8,128)(2,1)}), bf16[2048,768]{1,0:T(8,128)(2,1)}) %all-gather.16.cloned.1.call-update) | async-done | bytes 3145744 | tf_op jit(solution)/shard_map/all_gather | solution.py:288
  332.1 62.5 %all-gather.24.cloned.1.call-done = bf16[1,1536,1536]{2,1,0:T(8,128)(2,1)} async-done(((bf16[1,24,1536]{2,1,0:T(8,128)(2,1)}), bf16[1,1536,1536]{2,1,0:T(8,128)(2,1)}) %all-gather.24.cloned.1.call-update) | async-done | bytes 4718608 | tf_op jit(solution)/shard_map/all_gather | solution.py:98
  398.0 91.3 %all-gather.26.cloned.1.call-done = bf16[1,1536,4096]{2,1,0:T(8,128)(2,1)} async-done(((bf16[1,24,4096]{2,1,0:T(8,128)(2,1)}), bf16[1,1536,4096]{2,1,0:T(8,128)(2,1)}) %all-gather.26.cloned.1.call-update) | async-done | bytes 12582928 | tf_op jit(solution)/shard_map/all_gather | solution.py:100
  496.2 87.2 %all-gather.28.cloned.1.call-done = bf16[1,1536,4096]{2,1,0:T(8,128)(2,1)} async-done(((bf16[1,24,4096]{2,1,0:T(8,128)(2,1)}), bf16[1,1536,4096]{2,1,0:T(8,128)(2,1)}) %all-gather.28.cloned.1.call-update) | async-done | bytes 12582928 | tf_op jit(solution)/shard_map/all_gather | solution.py:101
  591.4 86.2 %all-gather.30.cloned.1.call-done = bf16[1,4096,1536]{2,1,0:T(8,128)(2,1)} async-done(((bf16[1,64,1536]{2,1,0:T(8,128)(2,1)}), bf16[1,4096,1536]{2,1,0:T(8,128)(2,1)}) %all-gather.30.cloned.1.call-update) | async-done | bytes 12582928 | tf_op jit(solution)/shard_map/all_gather | solution.py:102
  701.8 37.6 %all-gather.34.cloned.1.call-done = bf16[2048,768]{1,0:T(8,128)(2,1)} async-done(((bf16[64,768]{1,0:T(8,128)(2,1)}), bf16[2048,768]{1,0:T(8,128)(2,1)}) %all-gather.34.cloned.1.call-update) | async-done | bytes 3145744 | tf_op jit(solution)/shard_map/all_gather | solution.py:287
  753.8 33.0 %all-gather.32.cloned.1.call-done = bf16[2048,768]{1,0:T(8,128)(2,1)} async-done(((bf16[64,768]{1,0:T(8,128)(2,1)}), bf16[2048,768]{1,0:T(8,128)(2,1)}) %all-gather.32.cloned.1.call-update) | async-done | bytes 3145744 | tf_op jit(solution)/shard_map/all_gather | solution.py:288
  840.1 34.5 %all-gather.38.cloned.1.call-done = bf16[2048,768]{1,0:T(8,128)(2,1)} async-done(((bf16[64,768]{1,0:T(8,128)(2,1)}), bf16[2048,768]{1,0:T(8,128)(2,1)}) %all-gather.38.cloned.1.call-update) | async-done | bytes 3145744 | tf_op jit(solution)/shard_map/all_gather | solution.py:287
  888.4 33.5 %all-gather.36.cloned.1.call-done = bf16[2048,768]{1,0:T(8,128)(2,1)} async-done(((bf16[64,768]{1,0:T(8,128)(2,1)}), bf16[2048,768]{1,0:T(8,128)(2,1)}) %all-gather.36.cloned.1.call-update) | async-done | bytes 3145744 | tf_op jit(solution)/shard_map/all_gather | solution.py:288
  1068.6 38.3 %reduce-scatter.22.cloned.1.call-done = bf16[64,768]{1,0:T(8,128)(2,1)} async-done(((bf16[2048,768]{1,0:T(8,128)(2,1)}), bf16[64,768]{1,0:T(8,128)(2,1)}) %reduce-scatter.22.cloned.1.call-update) | async-done | bytes 98320 | tf_op jit(solution)/shard_map/reduce_scatter | solution.py:193
  1115.7 75.0 %reduce-scatter.42.cloned.1.call-done = bf16[64,768]{1,0:T(8,128)(2,1)} async-done(((bf16[2048,768]{1,0:T(8,128)(2,1)}), bf16[64,768]{1,0:T(8,128)(2,1)}) %reduce-scatter.42.cloned.1.call-update) | async-done | bytes 98320
  1278.0 52.5 %reduce-scatter.24.cloned.1.call-done = bf16[64,768]{1,0:T(8,128)(2,1)} async-done(((bf16[2048,768]{1,0:T(8,128)(2,1)}), bf16[64,768]{1,0:T(8,128)(2,1)}) %reduce-scatter.24.cloned.1.call-update) | async-done | bytes 98320 | tf_op jit(solution)/shard_map/reduce_scatter | solution.py:193
  1335.2 79.0 %reduce-scatter.44.cloned.1.call-done = bf16[64,768]{1,0:T(8,128)(2,1)} async-done(((bf16[2048,768]{1,0:T(8,128)(2,1)}), bf16[64,768]{1,0:T(8,128)(2,1)}) %reduce-scatter.44.cloned.1.call-update) | async-done | bytes 98320
  1506.5 45.6 %reduce-scatter.46.cloned.1.call-done = bf16[64,768]{1,0:T(8,128)(2,1)} async-done(((bf16[2048,768]{1,0:T(8,128)(2,1)}), bf16[64,768]{1,0:T(8,128)(2,1)}) %reduce-scatter.46.cloned.1.call-update) | async-done | bytes 98320
  1553.9 82.2 %reduce-scatter.26.cloned.1.call-done = bf16[64,768]{1,0:T(8,128)(2,1)} async-done(((bf16[2048,768]{1,0:T(8,128)(2,1)}), bf16[64,768]{1,0:T(8,128)(2,1)}) %reduce-scatter.26.cloned.1.call-update) | async-done | bytes 98320 | tf_op jit(solution)/shard_map/reduce_scatter | solution.py:193
  1717.9 320.9 %all-reduce.16 = (f32[1,1536]{1,0:T(1,128)S(1)}, f32[1,1536]{1,0:T(1,128)S(1)}) all-reduce(f32[1,1536]{1,0:T(1,128)S(1)} %add.514, f32[1,1536]{1,0:T(1,128)S(1)} %add.517), channel_id=8, replica_groups=mesh['section'=2,'dp'=2,'seq'=32] {'dp','seq'}, use_global_device_ids=true, to_apply=%region_36.37.clone | all-reduce | flops 3072 | bytes 24576
  2040.2 103.2 %reduce-scatter.34.cloned.1.call-done = f32[1,24,1536]{2,1,0:T(8,128)} async-done(((f32[1,1536,1536]{2,1,0:T(8,128)}), f32[1,24,1536]{2,1,0:T(8,128)}) %reduce-scatter.34.cloned.1.call-update) | async-done | bytes 147472 | tf_op jit(solution)/shard_map/reduce_scatter | solution.py:406
  2143.4 179.3 %reduce-scatter.28.cloned.1.call-done = f32[1,24,1536]{2,1,0:T(8,128)} async-done(((f32[1,1536,1536]{2,1,0:T(8,128)}), f32[1,24,1536]{2,1,0:T(8,128)}) %reduce-scatter.28.cloned.1.call-update) | async-done | bytes 147472 | tf_op jit(solution)/shard_map/reduce_scatter | solution.py:403
  2322.7 240.2 %reduce-scatter.40.cloned.1.call-done = f32[1,64,1536]{2,1,0:T(8,128)} async-done(((f32[1,4096,1536]{2,1,0:T(8,128)}), f32[1,64,1536]{2,1,0:T(8,128)}) %reduce-scatter.40.cloned.1.call-update) | async-done | bytes 393232 | tf_op jit(solution)/shard_map/reduce_scatter | solution.py:410
  2562.9 241.0 %reduce-scatter.36.cloned.1.call-done = f32[1,24,4096]{2,1,0:T(8,128)} async-done(((f32[1,1536,4096]{2,1,0:T(8,128)}), f32[1,24,4096]{2,1,0:T(8,128)}) %reduce-scatter.36.cloned.1.call-update) | async-done | bytes 393232 | tf_op jit(solution)/shard_map/reduce_scatter | solution.py:408
  2803.9 239.7 %reduce-scatter.38.cloned.1.call-done = f32[1,24,4096]{2,1,0:T(8,128)} async-done(((f32[1,1536,4096]{2,1,0:T(8,128)}), f32[1,24,4096]{2,1,0:T(8,128)}) %reduce-scatter.38.cloned.1.call-update) | async-done | bytes 393232 | tf_op jit(solution)/shard_map/reduce_scatter | solution.py:409
  (697 shorter events, 596.8 us)
Async XLA Ops:
  7.2 175.2 %all-gather.18.cloned.1.call-start = ((), (), s32[]{:S(2)}) async-start(), calls=%async_computation.15 | async-start | bytes 2396160 | tf_op jit(solution)/shard_map/all_gather | solution.py:96
  7.9 179.7 %all-gather.14.cloned.1.call-start = ((), (), s32[]{:S(2)}) async-start(), calls=%async_computation.13 | async-start | bytes 2396160 | tf_op jit(solution)/shard_map/all_gather | solution.py:97
  8.7 217.1 %all-gather.22.cloned.1.call-start = ((), (), s32[]{:S(2)}) async-start(), calls=%async_computation.17 | async-start | bytes 4792320 | tf_op jit(solution)/shard_map/all_gather | solution.py:95
  9.4 262.8 %all-gather.20.cloned.1.call-start = ((), (), s32[]{:S(2)}) async-start(), calls=%async_computation.16 | async-start | bytes 3244032 | tf_op jit(solution)/shard_map/all_gather | solution.py:287
  187.5 131.8 %all-gather.16.cloned.1.call-start = ((), (), s32[]{:S(2)}) async-start(), calls=%async_computation.14 | async-start | bytes 3244032 | tf_op jit(solution)/shard_map/all_gather | solution.py:288
  190.5 204.1 %all-gather.24.cloned.1.call-start = ((), (), s32[]{:S(2)}) async-start(), calls=%async_computation.18 | async-start | bytes 4792320 | tf_op jit(solution)/shard_map/all_gather | solution.py:98
  191.0 298.3 %all-gather.26.cloned.1.call-start = ((), (), s32[]{:S(2)}) async-start(), calls=%async_computation.19 | async-start | bytes 12779520 | tf_op jit(solution)/shard_map/all_gather | solution.py:100
  191.8 391.6 %all-gather.28.cloned.1.call-start = ((), (), s32[]{:S(2)}) async-start(), calls=%async_computation.20 | async-start | bytes 12779520 | tf_op jit(solution)/shard_map/all_gather | solution.py:101
  192.5 485.0 %all-gather.30.cloned.1.call-start = ((), (), s32[]{:S(2)}) async-start(), calls=%async_computation.21 | async-start | bytes 12779520 | tf_op jit(solution)/shard_map/all_gather | solution.py:102
  193.3 546.2 %all-gather.34.cloned.1.call-start = ((), (), s32[]{:S(2)}) async-start(), calls=%async_computation.23 | async-start | bytes 3244032 | tf_op jit(solution)/shard_map/all_gather | solution.py:287
  695.5 179.1 %all-gather.38.cloned.1.call-start = ((), (), s32[]{:S(2)}) async-start(), calls=%async_computation.25 | async-start | bytes 3244032 | tf_op jit(solution)/shard_map/all_gather | solution.py:287
  830.3 276.6 %reduce-scatter.22.cloned.1.call-start = ((), (), s32[]{:S(2)}) async-start(), calls=%async_computation.26 | async-start | bytes 3244032 | tf_op jit(solution)/shard_map/reduce_scatter | solution.py:193
  1028.9 161.7 %reduce-scatter.42.cloned.1.call-start = ((), (), s32[]{:S(2)}) async-start(), calls=%async_computation.36 | async-start | bytes 3244032
  1038.1 292.4 %reduce-scatter.24.cloned.1.call-start = ((), (), s32[]{:S(2)}) async-start(), calls=%async_computation.27 | async-start | bytes 3244032 | tf_op jit(solution)/shard_map/reduce_scatter | solution.py:193
  1249.3 164.9 %reduce-scatter.44.cloned.1.call-start = ((), (), s32[]{:S(2)}) async-start(), calls=%async_computation.37 | async-start | bytes 3244032
  1258.1 294.0 %reduce-scatter.46.cloned.1.call-start = ((), (), s32[]{:S(2)}) async-start(), calls=%async_computation.38 | async-start | bytes 3244032
  1471.0 165.0 %reduce-scatter.26.cloned.1.call-start = ((), (), s32[]{:S(2)}) async-start(), calls=%async_computation.28 | async-start | bytes 3244032 | tf_op jit(solution)/shard_map/reduce_scatter | solution.py:193
  1493.1 547.0 %reduce-scatter.32.cloned.1.call-start = ((), (), s32[]{:S(2)}) async-start(), calls=%async_computation.31 | async-start | bytes 4792320 | tf_op jit(solution)/shard_map/reduce_scatter | solution.py:405
  1651.8 388.3 %reduce-scatter.30.cloned.1.call-start = ((), (), s32[]{:S(2)}) async-start(), calls=%async_computation.30 | async-start | bytes 4792320 | tf_op jit(solution)/shard_map/reduce_scatter | solution.py:404
  1655.6 487.8 %reduce-scatter.34.cloned.1.call-start = ((), (), s32[]{:S(2)}) async-start(), calls=%async_computation.32 | async-start | bytes 9584640 | tf_op jit(solution)/shard_map/reduce_scatter | solution.py:406
  1663.0 659.7 %reduce-scatter.28.cloned.1.call-start = ((), (), s32[]{:S(2)}) async-start(), calls=%async_computation.29 | async-start | bytes 9584640 | tf_op jit(solution)/shard_map/reduce_scatter | solution.py:403
  1670.4 892.5 %reduce-scatter.40.cloned.1.call-start = ((), (), s32[]{:S(2)}) async-start(), calls=%async_computation.35 | async-start | bytes 25559040 | tf_op jit(solution)/shard_map/reduce_scatter | solution.py:410
  1682.7 1121.2 %reduce-scatter.36.cloned.1.call-start = ((), (), s32[]{:S(2)}) async-start(), calls=%async_computation.33 | async-start | bytes 25559040 | tf_op jit(solution)/shard_map/reduce_scatter | solution.py:408
  1696.0 1347.6 %reduce-scatter.38.cloned.1.call-start = ((), (), s32[]{:S(2)}) async-start(), calls=%async_computation.34 | async-start | bytes 25559040 | tf_op jit(solution)/shard_map/reduce_scatter | solution.py:409
  (181 other events, 7673.4 us)
Sparse Core Ops, SparseCore 0:
  11.2 72.1 all-gather.17
  86.6 65.7 all-gather.13
  155.6 70.1 all-gather.21
  274.8 44.4 all-gather.15
  322.4 72.1 all-gather.23
  397.8 91.4 all-gather.25
  492.5 90.9 all-gather.27
  586.6 90.9 all-gather.29
  693.6 45.7 all-gather.33
  742.3 44.4 all-gather.31
  828.5 45.9 all-gather.37
  1029.1 77.8 reduce-scatter.21
  1110.8 79.8 reduce-scatter.41
  1249.5 80.9 reduce-scatter.23
  1334.4 79.8 reduce-scatter.43
  1471.1 80.9 reduce-scatter.45
  1556.2 79.8 reduce-scatter.25
  1652.0 154.5 reduce-scatter.31
  1812.5 152.6 reduce-scatter.29
  1971.6 171.7 reduce-scatter.33
  2150.7 171.9 reduce-scatter.27
  2329.1 233.6 reduce-scatter.39
  2570.5 233.3 reduce-scatter.35
  2810.3 233.2 reduce-scatter.37
  (2 shorter events, 88.0 us)
where the time goes:
time: 3060 us; the launch traced here: 3050 us
  waiting for transfers between devices  1970 us (64%)
  blocking collectives  488 us (16%)
  matrix products  343 us (11%)
  local copies, waits for them, and re-layouts  157 us (5%)
  other arithmetic  63.3 us (2%)
    unnamed x2, blocking collectives  488 us
    reduce_scatter x1, waiting for transfers between devices, body(): lax.psum_scatter(full_set[6][None], ('dp', 'seq'), scatter_dimension=1, t...  241 us
    reduce_scatter x1, waiting for transfers between devices, body(): lax.psum_scatter(full_set[8][None], ('dp', 'seq'), scatter_dimension=1, t...  240 us
    reduce_scatter x1, waiting for transfers between devices, body(): lax.psum_scatter(full_set[7][None], ('dp', 'seq'), scatter_dimension=1, t...  240 us
    unnamed x29, waiting for transfers between devices  205 us
    reduce_scatter x1, waiting for transfers between devices, body(): lax.psum_scatter(full_set[1][None], ('dp', 'seq'), scatter_dimension=1, t...  179 us
    reduce_scatter x3, waiting for transfers between devices, backward(): lax.psum_scatter(grad_kpart.astype(jnp.bfloat16), 'seq', scatter_dimensio...  173 us
    all_gather x3, waiting for transfers between devices, body(): forward_values_all = lax.all_gather(values_low, 'seq', axis=0, tiled=True)  110 us
  transfers between devices with their start and end apart: 30, of which 26 were waited for; matrix products, arithmetic and copies ran while one was open for 9% of the time, Pallas kernels for 0%

commit v1 on v0

v1 whole, which is shorter than its diff:
```python
import functools
import math

import jax
import jax.numpy as jnp
from jax import lax
from jax.experimental import pallas as pl
from jax.experimental.pallas import tpu as pltpu
from jax.sharding import PartitionSpec as P

HEADS = 16
KV_HEADS = 8
HEAD = 96
LANES = 128
EPS = 1e-05
ROPE_BASE = 100000.0
NEG = -1e30
PREFIX_MAX = 1024
SCALE = 1.0 / math.sqrt(HEAD)
MESH = pl.DeviceIdType.MESH
ANY = pl.BlockSpec(memory_space=pl.ANY)
VMEM = pl.BlockSpec(memory_space=pltpu.VMEM)
SMEM = pl.BlockSpec(memory_space=pltpu.SMEM)
MIB = 1 << 20

PIECES = (
    (24, 2048, "y", 1),
    (24, 2048, "y", -1),
    (24, 1536, "z", 1),
    (24, 768, "z", 1),
    (24, 128, "z", 1),
    (64, 768, "z", -1),
)
OTHER = {"y": "z", "z": "y"}


def f32dot(a, b, dims):
    return lax.dot_general(a, b, (dims, ((), ())), preferred_element_type=jnp.float32)


class Place:
    def __init__(self):
        self.s = lax.axis_index("section")
        self.d = lax.axis_index("dp")
        self.q = lax.axis_index("seq")
        self.y = lax.div(self.q, 8)
        self.z = lax.rem(lax.div(self.q, 2), 4)
        self.c = lax.rem(self.q, 2)

    def coord(self, axis):
        return self.y if axis == "y" else self.z

    def step(self, axis, by):
        y, z = self.y, self.z
        if axis == "y":
            y = lax.rem(y + by + 4, 4)
        else:
            z = lax.rem(z + by + 4, 4)
        return (self.s, self.d, y * 8 + z * 2 + self.c)

    def sibling(self):
        return (self.s, self.d, self.q + 1 - 2 * self.c)

    def dp_peer(self):
        return (self.s, 1 - self.d, self.q)


def meet(devices):
    barrier = pltpu.get_barrier_semaphore()
    for device in devices:
        pl.semaphore_signal(barrier, inc=1, device_id=device, device_id_type=MESH)
    pl.semaphore_wait(barrier, len(devices))


def remote(src, dst, send, recv, device):
    return pltpu.make_async_remote_copy(
        src_ref=src, dst_ref=dst, send_sem=send, recv_sem=recv, device_id=device, device_id_type=MESH
    )


def gather_kernel(*refs):
    n = len(PIECES)
    ins, outs = refs[:n], refs[n : 2 * n]
    give, got, chip = refs[2 * n : 3 * n], refs[3 * n : 4 * n], refs[4 * n : 5 * n]
    first, local, over, ring_s, ring_r, sib_s, sib_r = refs[5 * n :]
    me = Place()
    meet(
        [me.step("y", 1), me.step("y", -1), me.step("z", 1), me.step("z", -1), me.dp_peer(), me.sibling()]
    )
    pending = []
    swaps = []
    for i, (rows, width, _, _) in enumerate(PIECES):
        start = pl.multiple_of((1 - me.c) * width, LANES)
        give[i][...] = ins[i][:, pl.ds(start, width)].astype(jnp.float32)
        cp = remote(give[i], got[i], first.at[0, i], first.at[1, i], me.sibling())
        cp.start()
        swaps.append(cp)

    def shard(i, dp, y, z):
        width = PIECES[i][1]
        return outs[i].at[dp, y, z, :, pl.ds(pl.multiple_of(me.c * width, LANES), width)]

    def column(i, dp, pos):
        width = PIECES[i][1]
        lanes = pl.ds(pl.multiple_of(me.c * width, LANES), width)
        if PIECES[i][2] == "y":
            return outs[i].at[dp, pl.ds(0, 4), pos, :, lanes]
        return outs[i].at[dp, pos, pl.ds(0, 4), :, lanes]

    def along(i, dp, by):
        a1 = PIECES[i][2]
        pos = lax.rem(me.coord(a1) + by + 4, 4)
        return shard(i, dp, pos, me.z) if a1 == "y" else shard(i, dp, me.y, pos)

    def across(i, dp, by):
        a2 = OTHER[PIECES[i][2]]
        return column(i, dp, lax.rem(me.coord(a2) + by + 4, 4))

    def send(i, block, k, src, dst, device):
        cp = remote(src, dst, ring_s.at[i, block, k], ring_r.at[i, block, k], device)
        cp.start()
        pending.append(cp)
        return cp

    def share(i, block, k, ref):
        cp = remote(ref, ref, sib_s.at[i, block, k], sib_r.at[i, block, k], me.sibling())
        cp.start()
        pending.append(cp)
        shares.append(cp)

    shares = []
    dps = (me.d, 1 - me.d)
    one, two, locals_, overs = {}, {}, [], []
    for i, (rows, width, a1, _) in enumerate(PIECES):
        swaps[i].wait()
        start = pl.multiple_of(me.c * width, LANES)
        mine = ins[i][:, pl.ds(start, width)].astype(jnp.float32)
        theirs = got[i][...]
        low = jnp.where(me.c == 0, mine, theirs)
        high = jnp.where(me.c == 0, theirs, mine)
        chip[i][...] = jnp.concatenate([low, high], axis=0).astype(jnp.bfloat16)
        here = along(i, me.d, 0)
        one[i, 0, 1] = send(i, 0, 0, chip[i], here, me.step(a1, 1))
        one[i, 0, -1] = send(i, 0, 1, chip[i], here, me.step(a1, -1))
        cp = remote(chip[i], here, over.at[0, i], over.at[1, i], me.dp_peer())
        cp.start()
        overs.append(cp)
        cp = pltpu.make_async_copy(chip[i], here, local.at[i])
        cp.start()
        locals_.append(cp)
        cp = remote(chip[i], here, sib_s.at[i, 0, 0], sib_r.at[i, 0, 0], me.sibling())
        cp.start()
        pending.append(cp)
        shares.append(cp)

    def ring_one_end(block):
        dp = dps[block]
        for i, (_, _, a1, sign) in enumerate(PIECES):
            one[i, block, sign].wait_recv()
            came = along(i, dp, -sign)
            one[i, block, 0] = send(i, block, 2, came, came, me.step(a1, sign))
            share(i, block, 1, came)
        for i, (_, _, a1, sign) in enumerate(PIECES):
            one[i, block, -sign].wait_recv()
            share(i, block, 2, along(i, dp, sign))

    def ring_two_start(block):
        dp = dps[block]
        for i, (_, _, a1, sign) in enumerate(PIECES):
            one[i, block, 0].wait_recv()
            share(i, block, 3, along(i, dp, 2))
            if block == 0:
                locals_[i].wait()
            here = across(i, dp, 0)
            a2 = OTHER[a1]
            two[i, block, sign] = send(i, block, 3, here, here, me.step(a2, sign))
            two[i, block, -sign] = send(i, block, 4, here, here, me.step(a2, -sign))

    def ring_two_end(block):
        dp = dps[block]
        for i, (_, _, a1, sign) in enumerate(PIECES):
            two[i, block, sign].wait_recv()
            came = across(i, dp, -sign)
            two[i, block, 0] = send(i, block, 5, came, came, me.step(OTHER[a1], sign))
            share(i, block, 4, came)
        for i, (_, _, a1, sign) in enumerate(PIECES):
            two[i, block, -sign].wait_recv()
            share(i, block, 5, across(i, dp, sign))

    def finish(block):
        for i in range(n):
            two[i, block, 0].wait_recv()
            share(i, block, 6, across(i, dps[block], 2))

    ring_one_end(0)
    ring_two_start(0)
    for i, (_, _, a1, _) in enumerate(PIECES):
        overs[i].wait_recv()
        here = along(i, dps[1], 0)
        one[i, 1, 1] = send(i, 1, 0, here, here, me.step(a1, 1))
        one[i, 1, -1] = send(i, 1, 1, here, here, me.step(a1, -1))
        share(i, 1, 0, here)
    ring_two_end(0)
    ring_one_end(1)
    ring_two_start(1)
    finish(0)
    ring_two_end(1)
    finish(1)
    for cp in shares:
        cp.wait_recv()
    for cp in pending:
        cp.wait_send()
    for cp in overs:
        cp.wait_send()


def gather_weights(shards):
    n = len(PIECES)
    outs = pl.pallas_call(
        gather_kernel,
        out_shape=[
            jax.ShapeDtypeStruct((2, 4, 4, 2 * rows, 2 * width), jnp.bfloat16) for rows, width, _, _ in PIECES
        ],
        in_specs=[VMEM] * n,
        out_specs=[ANY] * n,
        scratch_shapes=[pltpu.VMEM((rows, width), jnp.float32) for rows, width, _, _ in PIECES]
        + [pltpu.VMEM((rows, width), jnp.float32) for rows, width, _, _ in PIECES]
        + [pltpu.VMEM((2 * rows, width), jnp.bfloat16) for rows, width, _, _ in PIECES]
        + [
            pltpu.SemaphoreType.DMA((2, n)),
            pltpu.SemaphoreType.DMA((n,)),
            pltpu.SemaphoreType.DMA((2, n)),
            pltpu.SemaphoreType.DMA((n, 2, 6)),
            pltpu.SemaphoreType.DMA((n, 2, 6)),
            pltpu.SemaphoreType.DMA((n, 2, 7)),
            pltpu.SemaphoreType.DMA((n, 2, 7)),
        ],
        compiler_params=pltpu.CompilerParams(
            collective_id=1, has_side_effects=True, vmem_limit_bytes=24 * MIB
        ),
        name="gather_weights",
    )(*shards)
    return [
        out.reshape(64 * rows, 2 * width) for out, (rows, width, _, _) in zip(outs, PIECES, strict=True)
    ]


def add_into(total, term):
    chunks = total.shape[1] // 16

    def step(k, carry):
        j = lax.div(k, chunks)
        rows = pl.ds(pl.multiple_of(lax.rem(k, chunks) * 16, 16), 16)
        both = total[j, rows, :].astype(jnp.float32) + term[j, rows, :].astype(jnp.float32)
        total[j, rows, :] = both.astype(jnp.bfloat16)
        return carry

    lax.fori_loop(0, total.shape[0] * chunks, step, 0)


def add_two(total, left, right):
    chunks = total.shape[1] // 16

    def step(k, carry):
        j = lax.div(k, chunks)
        rows = pl.ds(pl.multiple_of(lax.rem(k, chunks) * 16, 16), 16)
        parts = [ref[j, rows, :].astype(jnp.float32) for ref in (total, left, right)]
        total[j, rows, :] = (parts[0] + (parts[1] + parts[2])).astype(jnp.bfloat16)
        return carry

    lax.fori_loop(0, total.shape[0] * chunks, step, 0)


def scatter_kernel(*refs):
    n = len(PIECES)
    take = iter(range(0, 100 * n, n))

    def group():
        k = next(take)
        return refs[k : k + n]

    ins, outs = group(), group()
    near, far, last, mid, own = group(), group(), group(), group(), group()
    near1, far1, last1 = group(), group(), group()
    sent, came, total = group(), group(), group()
    load, ring_s, ring_r, over, fin, keep = refs[13 * n :]
    me = Place()
    meet(
        [me.step("y", 1), me.step("y", -1), me.step("z", 1), me.step("z", -1), me.dp_peer(), me.sibling()]
    )
    dps = (1 - me.d, me.d)
    pending = []

    def column(i, block, by):
        a2 = OTHER[PIECES[i][2]]
        pos = lax.rem(me.coord(a2) + by + 4, 4)
        if a2 == "y":
            return ins[i].at[dps[block], pos, pl.ds(0, 4)]
        return ins[i].at[dps[block], pl.ds(0, 4), pos]

    def send(i, block, k, src, dst, device):
        cp = remote(src, dst, ring_s.at[i, block, k], ring_r.at[i, block, k], device)
        cp.start()
        pending.append(cp)
        return cp

    loads, one, two = {}, {}, {}
    for block in range(2):
        for i, (_, _, a1, sign) in enumerate(PIECES):
            a2 = OTHER[a1]
            one[i, block, 0] = send(i, block, 0, column(i, block, 2 * sign), near[i].at[block], me.step(a2, sign))
        for i, (_, _, a1, sign) in enumerate(PIECES):
            a2 = OTHER[a1]
            one[i, block, 1] = send(i, block, 1, column(i, block, -sign), far[i].at[block], me.step(a2, -sign))
        for i, (_, _, a1, sign) in enumerate(PIECES):
            cp = pltpu.make_async_copy(column(i, block, sign), mid[i].at[block], load.at[0, i, block])
            cp.start()
            loads[i, block, 0] = cp
            cp = pltpu.make_async_copy(column(i, block, 0), own[i].at[block], load.at[1, i, block])
            cp.start()
            loads[i, block, 1] = cp
    for block in range(2):
        for i, (_, _, a1, sign) in enumerate(PIECES):
            one[i, block, 0].wait_recv()
            loads[i, block, 0].wait()
            add_into(near[i].at[block], mid[i].at[block])
            one[i, block, 2] = send(
                i, block, 2, near[i].at[block], last[i].at[block], me.step(OTHER[a1], sign)
            )
    overs = []
    for block in range(2):
        for i, (_, _, a1, sign) in enumerate(PIECES):
            one[i, block, 1].wait_recv()
            loads[i, block, 1].wait()
            one[i, block, 2].wait_recv()
            add_two(own[i].at[block], far[i].at[block], last[i].at[block])
            pos = me.coord(a1)
            far_place = lax.rem(pos + 2, 4)
            two[i, block, 0] = send(
                i, block, 3, own[i].at[block, far_place], near1[i].at[block], me.step(a1, sign)
            )
            back_place = lax.rem(pos - sign + 4, 4)
            two[i, block, 1] = send(
                i, block, 4, own[i].at[block, back_place], far1[i].at[block], me.step(a1, -sign)
            )
        for i, (_, _, a1, sign) in enumerate(PIECES):
            two[i, block, 0].wait_recv()
            place = lax.rem(me.coord(a1) + sign + 4, 4)
            add_into(near1[i].at[pl.ds(block, 1)], own[i].at[block, pl.ds(place, 1)])
            two[i, block, 2] = send(
                i, block, 5, near1[i].at[block], last1[i].at[block], me.step(a1, sign)
            )
        for i, (rows, width, a1, sign) in enumerate(PIECES):
            two[i, block, 1].wait_recv()
            two[i, block, 2].wait_recv()
            pos = me.coord(a1)
            if block == 1:
                overs[i].wait_recv()

            def step(k, carry, i=i, block=block, pos=pos):
                part = pl.ds(pl.multiple_of(k * 16, 16), 16)
                both = far1[i][block, part, :].astype(jnp.float32) + last1[i][block, part, :].astype(
                    jnp.float32
                )
                both = both + own[i][block, pos, part, :].astype(jnp.float32)
                if block == 0:
                    sent[i][part, :] = both.astype(jnp.bfloat16)
                else:
                    total[i][part, :] = both + came[i][part, :].astype(jnp.float32)
                return carry

            lax.fori_loop(0, 2 * rows // 16, step, 0)
            if block == 0:
                cp = remote(sent[i], came[i], over.at[0, i], over.at[1, i], me.dp_peer())
                cp.start()
                overs.append(cp)
            else:
                mine = total[i].at[pl.ds(pl.multiple_of(me.c * rows, 8), rows)]
                theirs = total[i].at[pl.ds(pl.multiple_of((1 - me.c) * rows, 8), rows)]
                cp = pltpu.make_async_copy(mine, outs[i].at[me.c], keep.at[i])
                cp.start()
                loads[i, "keep"] = cp
                cp = remote(theirs, outs[i].at[me.c], fin.at[0, i], fin.at[1, i], me.sibling())
                cp.start()
                loads[i, "fin"] = cp
    for i in range(n):
        loads[i, "keep"].wait()
        loads[i, "fin"].wait()
    for cp in pending:
        cp.wait_send()
    for cp in overs:
        cp.wait_send()


def scatter_grads(parts):
    n = len(PIECES)
    shapes = [(2 * rows, width) for rows, width, _, _ in PIECES]
    bf16 = jnp.bfloat16
    return pl.pallas_call(
        scatter_kernel,
        out_shape=[jax.ShapeDtypeStruct((2, rows, width), jnp.float32) for rows, width, _, _ in PIECES],
        in_specs=[ANY] * n,
        out_specs=[ANY] * n,
        scratch_shapes=[pltpu.VMEM((2, 4, *shape), bf16) for _ in range(5) for shape in shapes]
        + [pltpu.VMEM((2, *shape), bf16) for _ in range(3) for shape in shapes]
        + [pltpu.VMEM(shape, bf16) for _ in range(2) for shape in shapes]
        + [pltpu.VMEM(shape, jnp.float32) for shape in shapes]
        + [
            pltpu.SemaphoreType.DMA((2, n, 2)),
            pltpu.SemaphoreType.DMA((n, 2, 6)),
            pltpu.SemaphoreType.DMA((n, 2, 6)),
            pltpu.SemaphoreType.DMA((2, n)),
            pltpu.SemaphoreType.DMA((2, n)),
            pltpu.SemaphoreType.DMA((n,)),
        ],
        compiler_params=pltpu.CompilerParams(
            collective_id=2, has_side_effects=True, vmem_limit_bytes=56 * MIB
        ),
        name="scatter_grads",
    )(*[part.reshape(2, 4, 4, *shape) for part, shape in zip(parts, shapes, strict=True)])


def meet_plane(me, count):
    barrier = pltpu.get_barrier_semaphore()

    def greet(k, carry):
        to = lax.rem(me.q + k, count)
        pl.semaphore_signal(barrier, inc=1, device_id=(me.s, me.d, to), device_id_type=MESH)
        return carry

    lax.fori_loop(1, count, greet, 0)
    pl.semaphore_wait(barrier, count - 1)


def all_to_all(me, src, dst_of, send_sem, recv_sem, own_sem):
    count = src.shape[0]
    own = pltpu.make_async_copy(src.at[me.q], dst_of(me.q, me.q), own_sem)
    own.start()

    def out(k, carry):
        to = lax.rem(me.q + k, count)
        remote(
            src.at[to], dst_of(me.q, to), send_sem.at[to], recv_sem.at[me.q], (me.s, me.d, to)
        ).start()
        return carry

    lax.fori_loop(1, count, out, 0)

    def arrive(k, carry):
        origin = lax.rem(me.q + k, count)
        remote(
            src.at[origin],
            dst_of(origin, me.q),
            send_sem.at[origin],
            recv_sem.at[origin],
            (me.s, me.d, origin),
        ).wait()
        return carry

    lax.fori_loop(1, count, arrive, 0)
    own.wait()


def spread_kernel(src, dst, send_sem, recv_sem, own_sem, sib):
    me = Place()
    meet_plane(me, src.shape[0])
    all_to_all(
        me, src, lambda origin, to: dst.at[origin, lax.rem(to, 2)], send_sem, recv_sem, own_sem.at[0]
    )
    mine = dst.at[pl.ds(0, src.shape[0]), me.c]
    cp = remote(mine, mine, sib.at[0], sib.at[1], me.sibling())
    cp.start()
    cp.wait()


def spread(src):
    count, rows, width = src.shape
    return pl.pallas_call(
        spread_kernel,
        out_shape=jax.ShapeDtypeStruct((count, 2, rows, width), src.dtype),
        in_specs=[VMEM],
        out_specs=VMEM,
        scratch_shapes=[
            pltpu.SemaphoreType.DMA((count,)),
            pltpu.SemaphoreType.DMA((count,)),
            pltpu.SemaphoreType.DMA((1,)),
            pltpu.SemaphoreType.DMA((2,)),
        ],
        compiler_params=pltpu.CompilerParams(
            collective_id=3, has_side_effects=True, vmem_limit_bytes=16 * MIB
        ),
        name="spread",
    )(src)


def swap_kernel(src, dst, send_sem, recv_sem, own_sem):
    me = Place()
    meet_plane(me, src.shape[0])
    all_to_all(me, src, lambda origin, to: dst.at[origin], send_sem, recv_sem, own_sem.at[0])


def swap(src):
    count = src.shape[0]
    return pl.pallas_call(
        swap_kernel,
        out_shape=jax.ShapeDtypeStruct(src.shape, src.dtype),
        in_specs=[VMEM],
        out_specs=VMEM,
        scratch_shapes=[
            pltpu.SemaphoreType.DMA((count,)),
            pltpu.SemaphoreType.DMA((count,)),
            pltpu.SemaphoreType.DMA((1,)),
        ],
        compiler_params=pltpu.CompilerParams(
            collective_id=4, has_side_effects=True, vmem_limit_bytes=16 * MIB
        ),
        name="swap",
    )(src)


def return_kernel(dkv, dq, dst, got, bundle, send_sem, recv_sem, own_sem, sib):
    me = Place()
    count = dq.shape[0]
    meet_plane(me, count)
    cp = remote(dkv.at[pl.ds(0, count), 1 - me.c], got, sib.at[0], sib.at[1], me.sibling())
    cp.start()
    cp.wait()

    def step(k, carry):
        bundle[k, :, 0:256] = (dkv[k, me.c] + got[k]).astype(jnp.bfloat16)
        bundle[k, :, 256:512] = dq[k]
        return carry

    lax.fori_loop(0, count, step, 0)
    all_to_all(me, bundle, lambda origin, to: dst.at[origin], send_sem, recv_sem, own_sem.at[0])


def send_back(dkv, dq):
    count, rows, _ = dq.shape
    return pl.pallas_call(
        return_kernel,
        out_shape=jax.ShapeDtypeStruct((count, rows, 512), jnp.bfloat16),
        in_specs=[VMEM] * 2,
        out_specs=VMEM,
        scratch_shapes=[
            pltpu.VMEM((count, rows, 256), jnp.float32),
            pltpu.VMEM((count, rows, 512), jnp.bfloat16),
            pltpu.SemaphoreType.DMA((count,)),
            pltpu.SemaphoreType.DMA((count,)),
            pltpu.SemaphoreType.DMA((1,)),
            pltpu.SemaphoreType.DMA((2,)),
        ],
        compiler_params=pltpu.CompilerParams(
            collective_id=5, has_side_effects=True, vmem_limit_bytes=24 * MIB
        ),
        name="send_back",
    )(dkv, dq)


def pair_kernel(whole_count, *refs):
    n = (len(refs) - 3) // 2
    ins, outs = refs[:n], refs[n : 2 * n]
    send_sem, recv_sem, own_sem = refs[2 * n :]
    me = Place()
    meet([me.sibling()])
    copies = []
    for i in range(n):
        here = ins[i] if i < whole_count else ins[i].at[me.c]
        there = ins[i] if i < whole_count else ins[i].at[1 - me.c]
        cp = remote(there, outs[i].at[me.c], send_sem.at[i], recv_sem.at[i], me.sibling())
        cp.start()
        copies.append(cp)
        cp = pltpu.make_async_copy(here, outs[i].at[me.c], own_sem.at[i])
        cp.start()
        copies.append(cp)
    for cp in copies:
        cp.wait()


def pair_up(whole, halved):
    n = len(whole) + len(halved)
    return pl.pallas_call(
        functools.partial(pair_kernel, len(whole)),
        out_shape=[jax.ShapeDtypeStruct((2, *a.shape), a.dtype) for a in whole]
        + [jax.ShapeDtypeStruct(a.shape, a.dtype) for a in halved],
        in_specs=[ANY] * n,
        out_specs=[ANY] * n,
        scratch_shapes=[pltpu.SemaphoreType.DMA((n,))] * 3,
        compiler_params=pltpu.CompilerParams(collective_id=6, has_side_effects=True),
        name="pair_up",
    )(*whole, *halved)


ORIGINS = 32
BLOCK = 8


def block_mask(block, keys, core, prefix_len):
    rows = BLOCK * 32
    row = lax.broadcasted_iota(jnp.int32, (rows, keys), 0)
    key = lax.broadcasted_iota(jnp.int32, (rows, keys), 1)
    pos = block * BLOCK * 64 + 64 * (row // 32) + 32 * core + row % 32
    return (key <= pos) | (key < prefix_len)


def keys_of(block):
    return max((block + 1) * BLOCK * 64, PREFIX_MAX)


def attend_kernel(meta, bundle, out):
    core, prefix_len = meta[0], meta[1]
    for block in range(ORIGINS // BLOCK):
        keys = keys_of(block)
        src = pl.ds(block * BLOCK, BLOCK)
        k = bundle[pl.ds(0, keys // 64), :, :, 0:128].reshape(keys, LANES)
        v = bundle[pl.ds(0, keys // 64), :, :, 128:256].reshape(keys, LANES)
        allowed = block_mask(block, keys, core, prefix_len)
        for h in range(2):
            lanes = slice(256 + 128 * h, 384 + 128 * h)
            q = bundle[src, core, :, lanes].reshape(BLOCK * 32, LANES)
            s = jnp.where(allowed, f32dot(q, k, ((1,), (1,))) * SCALE, NEG)
            top = jnp.max(s, axis=-1, keepdims=True)
            e = jnp.exp(s - top)
            p = (e * (1.0 / jnp.sum(e, axis=-1, keepdims=True))).astype(jnp.bfloat16)
            o = f32dot(p, v, ((1,), (0,)))
            out[src, :, 128 * h : 128 * h + 128] = o.astype(jnp.bfloat16).reshape(BLOCK, 32, LANES)


def attend(meta, bundle):
    return pl.pallas_call(
        attend_kernel,
        out_shape=jax.ShapeDtypeStruct((ORIGINS, 32, 256), jnp.bfloat16),
        in_specs=[SMEM, VMEM],
        out_specs=VMEM,
        compiler_params=pltpu.CompilerParams(vmem_limit_bytes=48 * MIB),
        name="attend",
    )(meta, bundle)


def attend_back_kernel(meta, bundle, datt, dkv, dq, dk_sum, dv_sum):
    core, prefix_len = meta[0], meta[1]
    dk_sum[...] = jnp.zeros_like(dk_sum)
    dv_sum[...] = jnp.zeros_like(dv_sum)
    for block in range(ORIGINS // BLOCK):
        keys = keys_of(block)
        src = pl.ds(block * BLOCK, BLOCK)
        k = bundle[pl.ds(0, keys // 64), :, :, 0:128].reshape(keys, LANES)
        v = bundle[pl.ds(0, keys // 64), :, :, 128:256].reshape(keys, LANES)
        allowed = block_mask(block, keys, core, prefix_len)
        for h in range(2):
            lanes = slice(256 + 128 * h, 384 + 128 * h)
            q = bundle[src, core, :, lanes].reshape(BLOCK * 32, LANES)
            g = datt[src, :, 128 * h : 128 * h + 128].reshape(BLOCK * 32, LANES)
            s = jnp.where(allowed, f32dot(q, k, ((1,), (1,))) * SCALE, NEG)
            top = jnp.max(s, axis=-1, keepdims=True)
            e = jnp.exp(s - top)
            p = e * (1.0 / jnp.sum(e, axis=-1, keepdims=True))
            dp = f32dot(g, v, ((1,), (1,)))
            delta = jnp.sum(p * dp, axis=-1, keepdims=True)
            ds = (p * (dp - delta)).astype(jnp.bfloat16)
            dq[src, :, 128 * h : 128 * h + 128] = (
                (f32dot(ds, k, ((1,), (0,))) * SCALE).astype(jnp.bfloat16).reshape(BLOCK, 32, LANES)
            )
            dk_sum[pl.ds(0, keys), :] += f32dot(ds, q, ((0,), (0,)))
            dv_sum[pl.ds(0, keys), :] += f32dot(p.astype(jnp.bfloat16), g, ((0,), (0,)))
    dkv[:, :, :, 0:128] = (dk_sum[...] * SCALE).reshape(ORIGINS, 2, 32, LANES)
    dkv[:, :, :, 128:256] = dv_sum[...].reshape(ORIGINS, 2, 32, LANES)


def attend_back(meta, bundle, datt):
    return pl.pallas_call(
        attend_back_kernel,
        out_shape=[
            jax.ShapeDtypeStruct((ORIGINS, 2, 32, 256), jnp.float32),
            jax.ShapeDtypeStruct((ORIGINS, 32, 256), jnp.bfloat16),
        ],
        in_specs=[SMEM, VMEM, VMEM],
        out_specs=[VMEM, VMEM],
        scratch_shapes=[pltpu.VMEM((ORIGINS * 64, LANES), jnp.float32)] * 2,
        compiler_params=pltpu.CompilerParams(vmem_limit_bytes=56 * MIB),
        name="attend_back",
    )(meta, bundle, datt)


def mm(a, b):
    return jnp.dot(a, b, preferred_element_type=jnp.float32)


def mm_t(a, b):
    return lax.dot_general(a, b, (((1,), (1,)), ((), ())), preferred_element_type=jnp.float32)


def rope_tables(positions):
    half = HEAD // 2
    frequency = ROPE_BASE ** (-jnp.arange(half, dtype=jnp.float32) * 2.0 / HEAD)
    angles = positions.astype(jnp.float32)[:, None] * frequency[None, :]
    cos = jnp.concatenate([jnp.cos(angles)] * 2, -1)[:, None, None, :]
    sin = jnp.concatenate([jnp.sin(angles)] * 2, -1)[:, None, None, :]
    turned = (jnp.arange(4) != 1)[None, None, :, None]
    return jnp.where(turned, cos, 1.0), jnp.where(turned, sin, 0.0)


def forward(x, weights, tables, meta):
    qkv_w, o_w, gate_w, up_w, down_w, gain_attn, gain_mlp = weights
    cos, sin = tables
    tokens, width = x.shape
    hidden = x.astype(jnp.float32)
    r1 = lax.rsqrt(jnp.mean(hidden * hidden, axis=-1, keepdims=True) + EPS)
    normed = (hidden * r1 * gain_attn).astype(jnp.bfloat16)
    qkv = mm(normed, qkv_w).reshape(2, 64, KV_HEADS, 4, HEAD)
    half = HEAD // 2
    turned = jnp.concatenate([-qkv[..., half:], qkv[..., :half]], -1)
    bundle = (qkv * cos + turned * sin).astype(jnp.bfloat16)
    bundle = jnp.pad(bundle, ((0, 0),) * 4 + ((0, LANES - HEAD),))
    bundle = bundle.transpose(0, 2, 1, 3, 4).reshape(32, 32, 512)
    whole = spread(bundle)
    out = swap(attend(meta, whole))
    attended = (
        out.reshape(2, KV_HEADS, 64, 2, LANES)[..., :HEAD].transpose(0, 2, 1, 3, 4).reshape(tokens, width)
    )
    middle = hidden + mm(attended, o_w)
    r2 = lax.rsqrt(jnp.mean(middle * middle, axis=-1, keepdims=True) + EPS)
    normed_two = (middle * r2 * gain_mlp).astype(jnp.bfloat16)
    gate = mm(normed_two, gate_w)
    up = mm(normed_two, up_w)
    mixed = (jax.nn.silu(gate) * up).astype(jnp.bfloat16)
    result = (middle + mm(mixed, down_w)).astype(jnp.bfloat16)
    return result, (hidden, r1, normed, whole, attended, middle, r2, normed_two, gate, up, mixed)


def norm_back(dn, gain, u, r):
    scaled = dn * gain
    return r * (scaled - u * jnp.mean(scaled * u, axis=-1, keepdims=True))


def backward(g_low, state, weights, tables, meta):
    qkv_w, o_w, gate_w, up_w, down_w, gain_attn, gain_mlp = weights
    hidden, r1, normed, whole, attended, middle, r2, normed_two, gate, up, mixed = state
    cos, sin = tables
    tokens, width = hidden.shape
    g = g_low.astype(jnp.float32)
    gm = mm_t(g_low, down_w)
    sig = jax.nn.sigmoid(gate)
    dgate = (gm * up * sig * (1.0 + gate * (1.0 - sig))).astype(jnp.bfloat16)
    dup = (gm * (gate * sig)).astype(jnp.bfloat16)
    dn2 = mm_t(dgate, gate_w) + mm_t(dup, up_w)
    u2 = middle * r2
    dgain_mlp = jnp.sum(dn2 * u2, axis=0)
    dmiddle = g + norm_back(dn2, gain_mlp, u2, r2)
    db = dmiddle.astype(jnp.bfloat16)
    datt = mm_t(db, o_w).astype(jnp.bfloat16).reshape(2, 64, KV_HEADS, 2, HEAD)
    datt = jnp.pad(datt, ((0, 0),) * 4 + ((0, LANES - HEAD),))
    datt = swap(datt.transpose(0, 2, 1, 3, 4).reshape(32, 32, 256))
    dkv, dq = attend_back(meta, whole, datt)
    back = send_back(dkv, dq).reshape(2, KV_HEADS, 64, 4, LANES)[..., :HEAD]
    back = back.transpose(0, 2, 1, 3, 4).astype(jnp.float32)
    half = HEAD // 2
    slanted = back * sin
    turned = jnp.concatenate([slanted[..., half:], -slanted[..., :half]], -1)
    dqkv = (back * cos + turned).astype(jnp.bfloat16).reshape(tokens, 2 * width)
    dn1 = mm_t(dqkv, qkv_w)
    u1 = hidden * r1
    dgain_attn = jnp.sum(dn1 * u1, axis=0)
    dx = (dmiddle + norm_back(dn1, gain_attn, u1, r1)).astype(jnp.bfloat16)
    return dx, (g_low, dgate, dup, db, dqkv, dgain_attn, dgain_mlp)


def halves(a):
    rows, width = a.shape
    return a.reshape(rows, 2, width // 2).transpose(1, 0, 2)


def body(
    inputs, prefix, cotangent, attn_gain, w_query, w_key, w_value, w_out, mlp_gain, w_gate, w_up, w_down
):
    seqs, rows, width = inputs.shape
    tokens = seqs * rows
    section = lax.axis_index("section")
    seq = lax.axis_index("seq")
    positions = seq * rows + jnp.arange(rows, dtype=jnp.int32)
    tables = rope_tables(positions)
    meta = jnp.stack([seq % 2, lax.dynamic_index_in_dim(prefix, seq // 16, 0, keepdims=False)])

    part = w_query.shape[1]
    qkv_shard = jnp.concatenate(
        [
            w_key[0].reshape(part, KV_HEADS, HEAD),
            w_value[0].reshape(part, KV_HEADS, HEAD),
            w_query[0].reshape(part, KV_HEADS, 2 * HEAD),
        ],
        -1,
    ).reshape(part, 2 * width)
    gains = jnp.concatenate(
        [
            jnp.broadcast_to(attn_gain[0][:, None], (part, LANES)),
            jnp.broadcast_to(mlp_gain[0][:, None], (part, LANES)),
        ],
        -1,
    )
    gate_w, up_w, qkv_w, o_w, gains_w, down_w = gather_weights(
        [w_gate[0], w_up[0], qkv_shard, w_out[0], gains, w_down[0]]
    )
    gain_attn = gains_w[:, 0].astype(jnp.float32)[None, :]
    gain_mlp = gains_w[:, LANES].astype(jnp.float32)[None, :]
    weights = (qkv_w, o_w, gate_w, up_w, down_w, gain_attn, gain_mlp)

    x0 = inputs.reshape(tokens, width)
    out0, _ = forward(x0, weights, tables, meta)
    received = lax.ppermute(out0, "section", [(0, 1)])
    x1 = jnp.where(section == 0, x0, received)
    out, state = forward(x1, weights, tables, meta)

    g0 = cotangent.reshape(tokens, width)
    dx0, _ = backward(g0, state, weights, tables, meta)
    received = lax.ppermute(dx0, "section", [(1, 0)])
    g1 = jnp.where(section == 1, g0, received)
    dx, (g_low, dgate, dup, db, dqkv, dgain_attn, dgain_mlp) = backward(g1, state, weights, tables, meta)

    normed, attended, normed_two, mixed = state[2], state[4], state[7], state[10]
    dgains = jnp.broadcast_to(jnp.stack([dgain_attn, dgain_mlp])[:, None, :], (2, 8, width))
    normed, attended, normed_two, mixed, g_half, dgate, dup, db, dqkv, dgains = pair_up(
        [normed, attended, normed_two, mixed],
        [halves(g_low), halves(dgate), halves(dup), halves(db), halves(dqkv), dgains],
    )

    def outer(a, b):
        a, b = a.reshape(2 * tokens, -1), b.reshape(2 * tokens, -1)
        return lax.dot_general(
            a, b, (((0,), (0,)), ((), ())), preferred_element_type=jnp.float32
        ).astype(jnp.bfloat16)

    gain_part = jnp.broadcast_to(
        (dgains[0, 0] + dgains[1, 0]).astype(jnp.bfloat16)[:, None], (width, LANES)
    )
    sums = scatter_grads(
        [
            outer(normed_two, dgate),
            outer(normed_two, dup),
            outer(normed, dqkv),
            outer(attended, db),
            gain_part,
            outer(mixed, g_half),
        ]
    )

    def joined(a):
        return a.transpose(1, 0, 2).reshape(1, a.shape[1], -1)

    gate_g, up_g, qkv_g, o_g, gain_g, down_g = sums
    qkv_g = joined(qkv_g).reshape(1, part, KV_HEADS, 4 * HEAD)
    key_g = qkv_g[..., :HEAD].reshape(1, part, -1)
    value_g = qkv_g[..., HEAD : 2 * HEAD].reshape(1, part, -1)
    query_g = qkv_g[..., 2 * HEAD :].reshape(1, part, -1)
    return (
        out.reshape(1, seqs, rows, width),
        dx.reshape(1, seqs, rows, width),
        gain_g[0, :, 0][None],
        query_g,
        key_g,
        value_g,
        joined(o_g),
        gain_g[1, :, 0][None],
        joined(gate_g),
        joined(up_g),
        joined(down_g),
    )


def solution(mesh):
    split = ("dp", "seq")
    matrix = P("section", split, None)
    vector = P("section", split)
    rows = P("dp", "seq", None)
    layer = P("section", "dp", "seq", None)
    return jax.shard_map(
        body,
        mesh=mesh,
        in_specs=(
            rows, P("dp"), rows, vector, matrix, matrix, matrix, matrix, vector, matrix, matrix, matrix
        ),
        out_specs=(
            layer, layer, vector, matrix, matrix, matrix, matrix, vector, matrix, matrix, matrix
        ),
        check_vma=False,
    )
```

time: 3060 us -> 934 us (0.31)
  waiting for transfers between devices: 1970 us -> 10.1 us
  Pallas kernels: 0 us -> 645 us
  blocking collectives: 488 us -> 0 us
  matrix products: 343 us -> 157 us
  local copies, waits for them, and re-layouts: 157 us -> 91.4 us
  other arithmetic: 63.3 us -> 16.1 us
    reduce_scatter x10 -> x0, waiting for transfers between devices: 1180 us -> none  [the longest x1 241 us: body(): lax.psum_scatter(full_set[6][None], ('dp', 'seq'), scatter_dimension=1, t...]
    pallas_call x0 -> x15, Pallas kernels: none -> 645 us  [the longest x1 159 us: gather_weights(): pl.pallas_call(gather_kernel, out_shape=[jax.ShapeDtypeStruct((2, 4, 4, 2...]
    all_gather x13 -> x0, waiting for transfers between devices: 571 us -> none  [the longest x3 110 us: body(): forward_values_all = lax.all_gather(values_low, 'seq', axis=0, tiled=True)]
    unnamed x2 -> x0, blocking collectives: 488 us -> none
    unnamed x29 -> x0, waiting for transfers between devices: 205 us -> none
    dot_general x70 -> x24, matrix products: 343 us -> 157 us  [the longest x10 78.9 us: mm_t(): lax.dot_general(a, b, (((1,), (1,)), ((), ())), preferred_element_type=jn...]
    dynamic_slice x12 -> x1, local copies, waits for them, and re-layouts: 37.6 us -> 0.59 us  [body(): lax.dynamic_index_in_dim(prefix, seq // 16, 0, keepdims=False)]
  transfers between devices with their start and end apart: 30 -> 2, of which waited for: 26 -> 1; matrix products, arithmetic and copies ran while one was open for 9% -> 1% of each run, Pallas kernels for 0% -> 0%
where the time goes in v1:
time: 934 us; the launch traced here: 926 us
  Pallas kernels  645 us (69%)
  matrix products  157 us (17%)
  local copies, waits for them, and re-layouts  91.4 us (10%)
  other arithmetic  16.1 us (2%)
  waiting for transfers between devices  10.1 us (1%)
    pallas_call x1, Pallas kernels, gather_weights(): pl.pallas_call(gather_kernel, out_shape=[jax.ShapeDtypeStruct((2, 4, 4, 2...  159 us
    pallas_call x1, Pallas kernels, scatter_grads(): pl.pallas_call(scatter_kernel, out_shape=[jax.ShapeDtypeStruct((2, rows,...  156 us
    pallas_call x1, Pallas kernels, pair_up(): pl.pallas_call(functools.partial(pair_kernel, len(whole)), out_shape=[jax...  127 us
    dot_general x10, matrix products, mm_t(): lax.dot_general(a, b, (((1,), (1,)), ((), ())), preferred_element_type=jn...  78.9 us
    pallas_call x4, Pallas kernels, swap(): pl.pallas_call(swap_kernel, out_shape=jax.ShapeDtypeStruct(src.shape, src...  64.8 us
    dot_general x9, matrix products, mm(): return jnp.dot(a, b, preferred_element_type=jnp.float32)  55.7 us
    pallas_call x2, Pallas kernels, send_back(): pl.pallas_call(return_kernel, out_shape=jax.ShapeDtypeStruct((count, rows...  47 us
    pallas_call x2, Pallas kernels, spread(): pl.pallas_call(spread_kernel, out_shape=jax.ShapeDtypeStruct((count, 2, r...  43.2 us
  transfers between devices with their start and end apart: 2, of which 1 were waited for; matrix products, arithmetic and copies ran while one was open for 1% of the time, Pallas kernels for 0%

profile of v1, /device:TPU:1, one launch (start us, length us, event | category | flops | bytes accessed | tf_op | source)
XLA Modules:
  0.0 926.2 jit_solution(9364069681292836148)
XLA Ops:
  8.8 159.2 %gather_weights.1 = (bf16[2,4,4,48,4096]{4,3,2,1,0:T(8,128)(2,1)S(1)}, bf16[2,4,4,48,4096]{4,3,2,1,0:T(8,128)(2,1)}, bf16[2,4,4,48,3072]{4,3,2,1,0:T(8,128)(2,1)...) custom-call(bf16[24,4096]{1,0:T(8,128)(2,1)S(1)} %bitcast.169, ...), custom_call_target="tpu_custom_call" | custom-call | tf_op jit(solution)/shard_map/gather_weights/pallas_call | solution.py:219
  178.8 12.7 %copy.38 = bf16[3072,1536]{1,0:T(8,128)(2,1)} copy(bf16[3072,1536]{0,1:T(8,128)(2,1)} %bitcast.156) | data formatting | bytes 18874368 | tf_op jit(solution)/shard_map/dot_general | solution.py:686
  202.1 20.4 %spread.2.bundle = bf16[32,2,32,512]{3,2,1,0:T(8,128)(2,1)S(1)} custom-call(bf16[32,32,512]{2,1,0:T(8,128)(2,1)S(1)} %reshape.288.src), custom_call_target="tpu_custom_call" | custom-call | tf_op jit(solution)/shard_map/spread/pallas_call | solution.py:478
  223.8 8.3 attend.2.src
  232.1 17.1 %swap.4 = bf16[32,32,256]{2,1,0:T(8,128)(2,1)S(1)} custom-call(bf16[32,32,256]{2,1,0:T(8,128)(2,1)S(1)} %attend.2.src), custom_call_target="tpu_custom_call" | custom-call | tf_op jit(solution)/shard_map/swap/pallas_call | solution.py:504
  260.0 13.0 %fusion.2 = bf16[128,1536]{1,0:T(8,128)(2,1)} fusion(f32[128,1536]{1,0:T(8,128)S(1)} %get-tuple-element.91, bf16[4096,1536]{1,0:T(8,128)(2,1)} %bitcast.175, bf16[1536,4096]{1,0:T(8,128)(2,1)} %bitcast.179, f32[128,4096]{1,0:T(8,128)S(1)} %fusion.41, f32[1536]{0:T(1024)S(1)} %copy-done.62, f32[128]{0:T(128)S(1)} %add_rsqrt_fusion.3), kind=kOutput, calls=%fused_computation.20 | convolution fusion | flops 3225354240 | bytes 28449280 | tf_op jit(solution)/shard_map/dot_general | solution.py:686
  275.4 10.2 %convolution_bitcast_fusion = f32[128,4096]{1,0:T(8,128)} fusion(bf16[4096,1536]{1,0:T(8,128)(2,1)} %bitcast.176, bf16[128,1536]{1,0:T(8,128)(2,1)S(1)} %bitcast.194), kind=kOutput, calls=%fused_computation.4 | convolution fusion | flops 1610612736 | bytes 15073280 | tf_op jit(solution)/shard_map/dot_general | solution.py:690
  298.2 22.8 %spread.3.bundle = bf16[32,2,32,512]{3,2,1,0:T(8,128)(2,1)S(1)} custom-call(bf16[32,32,512]{2,1,0:T(8,128)(2,1)S(1)} %reshape.295.src), custom_call_target="tpu_custom_call" | custom-call | tf_op jit(solution)/shard_map/spread/pallas_call | solution.py:478
  321.0 8.3 attend.3.src
  329.3 15.9 %swap.5 = bf16[32,32,256]{2,1,0:T(8,128)(2,1)S(1)} custom-call(bf16[32,32,256]{2,1,0:T(8,128)(2,1)S(1)} %attend.3.src), custom_call_target="tpu_custom_call" | custom-call | tf_op jit(solution)/shard_map/swap/pallas_call | solution.py:504
  360.2 9.8 %fusion.23 = f32[128,1536]{1,0:T(8,128)S(1)} fusion(bf16[1536,4096]{1,0:T(8,128)(2,1)} %bitcast.151, f32[128,4096]{1,0:T(8,128)S(1)} %copy-done.39, f32[128,4096]{1,0:T(8,128)S(1)} %fusion.64, f32[128,4096]{1,0:T(8,128)} %fusion.63), kind=kOutput, calls=%fused_computation.58 | convolution fusion | flops 1615855616 | bytes 19660800 | tf_op jit(solution)/shard_map/dot_general | solution.py:690
  370.0 9.7 %multiply_reduce_fusion.2 = (f32[128]{0:T(128)S(1)}, f32[128,1536]{1,0:T(8,128)S(1)}) fusion(f32[128,1536]{1,0:T(8,128)S(1)} %get-tuple-element.93, f32[128]{0:T(128)S(1)} %add_rsqrt_fusion.1, f32[1536]{0:T(1024)S(1)} %copy-done.63, f32[128,1536]{1,0:T(8,128)S(1)} %fusion.23, bf16[1536,4096]{1,0:T(8,128)(2,1)} %bitcast.181, f32[128,4096]{1,0:T(8,128)S(1)} %copy-done.39, ...), kind=kOutput, calls=%fused_computation.85 | convolution fusion | flops 1614741376 | bytes 19143680 | tf_op jit(solution)/shard_map/dot_general | solution.py:690
  383.3 14.1 %swap.6.datt = bf16[32,32,256]{2,1,0:T(8,128)(2,1)S(1)} custom-call(bf16[32,32,256]{2,1,0:T(8,128)(2,1)S(1)} %reshape.301.src), custom_call_target="tpu_custom_call" | custom-call | tf_op jit(solution)/shard_map/swap/pallas_call | solution.py:504
  398.2 15.9 %attend_back.2 = (f32[32,2,32,256]{3,2,1,0:T(8,128)}, bf16[32,32,256]{2,1,0:T(8,128)(2,1)}) custom-call(s32[2]{0:T(128)} %copy-done.14, bf16[32,2,32,512]{3,2,1,0:T(8,128)(2,1)} %copy-done.3, bf16[32,32,256]{2,1,0:T(8,128)(2,1)} %copy-done.7), custom_call_target="tpu_custom_call" | custom-call | tf_op jit(solution)/shard_map/attend_back/pallas_call | solution.py:671
  416.7 23.6 %send_back.2 = bf16[32,32,512]{2,1,0:T(8,128)(2,1)S(1)} custom-call(f32[32,2,32,256]{3,2,1,0:T(8,128)S(1)} %copy-done.5, bf16[32,32,256]{2,1,0:T(8,128)(2,1)S(1)} %copy-done.9), custom_call_target="tpu_custom_call" | custom-call | tf_op jit(solution)/shard_map/send_back/pallas_call | solution.py:540
  456.0 10.1 %collective-permute-done.1 = bf16[128,1536]{1,0:T(8,128)(2,1)S(1)} collective-permute-done((bf16[128,1536]{1,0:T(8,128)(2,1)S(1)}, bf16[128,1536]{1,0:T(8,128)(2,1)S(1)}, u32[]{:S(2)}, u32[]{:S(2)}) %collective-permute-start.1) | collective-permute-done | bytes 393248 | tf_op jit(solution)/shard_map/ppermute | solution.py:815
  466.2 11.2 %multiply_convert_fusion = (bf16[128,4096]{1,0:T(8,128)(2,1)S(1)}, bf16[128,4096]{1,0:T(8,128)(2,1)S(1)}, bf16[128,4096]{1,0:T(8,128)(2,1)}) fusion(f32[128,4096]{1,0:T(8,128)} %fusion.63, f32[128,4096]{1,0:T(8,128)} %copy-done.40, bf16[128,1536]{1,0:T(8,128)(2,1)S(1)} %broadcast_select_fusion, bf16[4096,1536]{1,0:T(8,128)(2,1)} %bitcast.177), kind=kOutput, calls=%fused_computation.42 | convolution fusion | flops 1618477056 | bytes 20316160 | tf_op jit(solution)/shard_map/dot_general | solution.py:690
  477.4 9.6 %fusion.65 = f32[128,1536]{1,0:T(8,128)S(1)} fusion(bf16[128,4096]{1,0:T(8,128)(2,1)S(1)} %get-tuple-element.72, bf16[1536,4096]{1,0:T(8,128)(2,1)} %bitcast.152), kind=kOutput, calls=%fused_computation.142 | convolution fusion | flops 1610612736 | bytes 14417920 | tf_op jit(solution)/shard_map/dot_general | solution.py:690
  487.1 9.7 %multiply_reduce_fusion = (f32[1536]{0:T(1024)}, f32[128]{0:T(128)S(1)}, f32[128,1536]{1,0:T(8,128)S(1)}) fusion(f32[128,1536]{1,0:T(8,128)S(1)} %get-tuple-element.93, f32[128]{0:T(128)S(1)} %add_rsqrt_fusion.1, f32[1536]{0:T(1024)S(1)} %copy-done.64, f32[128,1536]{1,0:T(8,128)S(1)} %fusion.65, bf16[128,4096]{1,0:T(8,128)(2,1)S(1)} %get-tuple-element.71, ...), kind=kOutput, calls=%fused_computation.81 | convolution fusion | flops 1611987328 | bytes 16004096 | tf_op jit(solution)/shard_map/dot_general | solution.py:690
  501.3 17.7 %swap.7.datt = bf16[32,32,256]{2,1,0:T(8,128)(2,1)S(1)} custom-call(bf16[32,32,256]{2,1,0:T(8,128)(2,1)S(1)} %reshape.305.src), custom_call_target="tpu_custom_call" | custom-call | tf_op jit(solution)/shard_map/swap/pallas_call | solution.py:504
  519.9 15.9 %attend_back.3 = (f32[32,2,32,256]{3,2,1,0:T(8,128)}, bf16[32,32,256]{2,1,0:T(8,128)(2,1)}) custom-call(s32[2]{0:T(128)} %copy-done.14, bf16[32,2,32,512]{3,2,1,0:T(8,128)(2,1)} %copy-done.3, bf16[32,32,256]{2,1,0:T(8,128)(2,1)} %copy-done.6), custom_call_target="tpu_custom_call" | custom-call | tf_op jit(solution)/shard_map/attend_back/pallas_call | solution.py:671
  538.4 23.4 %send_back.3 = bf16[32,32,512]{2,1,0:T(8,128)(2,1)S(1)} custom-call(f32[32,2,32,256]{3,2,1,0:T(8,128)S(1)} %copy-done.4, bf16[32,32,256]{2,1,0:T(8,128)(2,1)S(1)} %copy-done.8), custom_call_target="tpu_custom_call" | custom-call | tf_op jit(solution)/shard_map/send_back/pallas_call | solution.py:540
  591.6 126.7 %pair_up.1 = (bf16[2,128,1536]{2,1,0:T(8,128)(2,1)}, bf16[2,128,1536]{2,1,0:T(8,128)(2,1)}, bf16[2,128,1536]{2,1,0:T(8,128)(2,1)}, bf16[2,128,4096]{2,1,0:T(8,12...) custom-call(bf16[128,1536]{1,0:T(8,128)(2,1)} %copy-done.30, ...), custom_call_target="tpu_custom_call" | custom-call | tf_op jit(solution)/shard_map/pair_up/pallas_call | solution.py:582
  742.9 156.2 %scatter_grads.1 = (f32[2,24,2048]{2,1,0:T(8,128)}, f32[2,24,2048]{2,1,0:T(8,128)}, f32[2,24,1536]{2,1,0:T(8,128)}, f32[2,24,768]{2,1,0:T(8,128)}, f32[2,24,128]{2,1,0:T(8,128)}, /*index=5*/f32[2,64,768]{2,1,0:T(8,128)}) custom-call(bf16[2,4,4,48,2048]{4,3,2,1,0:T(8,128)(2,1)} %bitcast.185, bf16[2,4,4,48,2048]{4,3,2,1,0:T(8,128)(2,1)} %bitcast.184, ...), custom_call_target="tpu_custom_call" | custom-call | tf_op jit(solution)/shard_map/scatter_grads/pallas_call | solution.py:399
  (283 shorter events, 182.8 us)
Async XLA Ops:
  178.8 12.7 %copy-start.20 = (bf16[2,64,1536]{2,1,0:T(8,128)(2,1)S(1)}, bf16[2,64,1536]{2,1,0:T(8,128)(2,1)}, u32[]{:S(2)}) copy-start(bf16[2,64,1536]{2,1,0:T(8,128)(2,1)} %param.12) | copy-start | bytes 1179652
  202.1 20.4 %copy-start.70 = (s32[2]{0:T(128)S(1)}, s32[2]{0:T(128)}, u32[]{:S(2)}) copy-start(s32[2]{0:T(128)} %param.13) | copy-start | bytes 28
  223.8 97.2 %copy-start.14 = (s32[2]{0:T(128)}, s32[2]{0:T(128)S(1)}, u32[]{:S(2)}) copy-start(s32[2]{0:T(128)S(1)} %pad_add_fusion.meta) | copy-start | bytes 28
  260.0 15.4 %copy-start.32 = (bf16[2,64,1536]{2,1,0:T(8,128)(2,1)S(1)}, bf16[2,64,1536]{2,1,0:T(8,128)(2,1)}, u32[]{:S(2)}) copy-start(bf16[2,64,1536]{2,1,0:T(8,128)(2,1)} %param.14) | copy-start | bytes 1179652
  273.0 14.1 %collective-permute-start = (bf16[128,1536]{1,0:T(8,128)(2,1)}, bf16[128,1536]{1,0:T(8,128)(2,1)S(1)}, u32[]{:S(2)}, u32[]{:S(2)}) collective-permute-start(bf16[128,1536]{1,0:T(8,128)(2,1)} %fusion.2), channel_id=1, source_target_pairs={{0,64},{1,65},{2,66},{3,67},{4,68},{5,69},{6,70},{7,71},{8,72},{9,... | collective-permute-start | bytes 1179656 | tf_op jit(solution)/shard_map/ppermute | solution.py:809
  275.4 10.2 %copy-start.45 = (f32[64,4,96]{2,0,1:T(8,128)S(1)}, f32[64,4,96]{2,0,1:T(8,128)}, u32[]{:S(2)}) copy-start(f32[64,4,96]{2,0,1:T(8,128)} %copy-done.44) | copy-start | bytes 294916
  275.4 10.9 %copy-start.42 = (f32[64,4,96]{2,0,1:T(8,128)S(1)}, f32[64,4,96]{2,0,1:T(8,128)}, u32[]{:S(2)}) copy-start(f32[64,4,96]{2,0,1:T(8,128)} %copy-done.41) | copy-start | bytes 294916
  275.4 11.7 %copy-start.21 = (bf16[2,64,1536]{2,1,0:T(8,128)(2,1)S(1)}, bf16[2,64,1536]{2,1,0:T(8,128)(2,1)}, u32[]{:S(2)}) copy-start(bf16[2,64,1536]{2,1,0:T(8,128)(2,1)} %param.12) | copy-start | bytes 1179652
  321.0 24.3 %copy-start.3 = (bf16[32,2,32,512]{3,2,1,0:T(8,128)(2,1)}, bf16[32,2,32,512]{3,2,1,0:T(8,128)(2,1)S(1)}, u32[]{:S(2)}) copy-start(bf16[32,2,32,512]{3,2,1,0:T(8,128)(2,1)S(1)} %spread.3.bundle) | copy-start | bytes 6291460
  346.3 10.2 %slice-start = ((s8[12582912]{0:T(1024)(128)(4,1)}), s8[4194304]{0:T(1024)(128)(4,1)S(1)}, s32[]{:S(2)}) async-start(s8[12582912]{0:T(1024)(128)(4,1)} %bitcast.153), calls=%async_computation | async-start | bytes 8388608
  360.2 19.8 %slice-start.3 = ((s8[4718592]{0:T(1024)(128)(4,1)}), s8[4194304]{0:T(1024)(128)(4,1)S(1)}, s32[]{:S(2)}) async-start(s8[4718592]{0:T(1024)(128)(4,1)} %bitcast.161), calls=%async_computation.3 | async-start | bytes 8388608
  370.0 10.0 %slice-start.4 = ((s8[4718592]{0:T(1024)(128)(4,1)}), s8[524288]{0:T(1024)(128)(4,1)S(1)}, s32[]{:S(2)}) async-start(s8[4718592]{0:T(1024)(128)(4,1)} %bitcast.161), calls=%async_computation.4 | async-start | bytes 1048576
  416.7 23.9 %copy-start.51 = (f32[64,4,96]{2,1,0:T(4,128)S(1)}, f32[64,4,96]{2,1,0:T(4,128)}, u32[]{:S(2)}) copy-start(f32[64,4,96]{2,1,0:T(4,128)} %copy.48) | copy-start | bytes 294916
  453.9 12.2 %copy-start.34 = (bf16[2,64,1536]{2,1,0:T(8,128)(2,1)S(1)}, bf16[2,64,1536]{2,1,0:T(8,128)(2,1)}, u32[]{:S(2)}) copy-start(bf16[2,64,1536]{2,1,0:T(8,128)(2,1)} %param.14) | copy-start | bytes 1179652
  454.3 11.8 %collective-permute-start.1 = (bf16[128,1536]{1,0:T(8,128)(2,1)S(1)}, bf16[128,1536]{1,0:T(8,128)(2,1)S(1)}, u32[]{:S(2)}, u32[]{:S(2)}) collective-permute-start(bf16[128,1536]{1,0:T(8,128)(2,1)S(1)} %fusion.33), channel_id=1, source_target_pairs={{64,0},{65,1},{66,2},{67,3},{68,4},{69,5},{70,6},{71,7},{72,8},{73... | collective-permute-start | bytes 1179656 | tf_op jit(solution)/shard_map/ppermute | solution.py:815
  466.2 30.6 %copy-start.22 = (bf16[128,1536]{1,0:T(8,128)(2,1)}, bf16[128,1536]{1,0:T(8,128)(2,1)S(1)}, u32[]{:S(2)}) copy-start(bf16[128,1536]{1,0:T(8,128)(2,1)S(1)} %broadcast_select_fusion) | copy-start | bytes 1179652
  487.0 11.2 %slice-start.5 = ((s8[4718592]{0:T(1024)(128)(4,1)}), s8[4194304]{0:T(1024)(128)(4,1)S(1)}, s32[]{:S(2)}) async-start(s8[4718592]{0:T(1024)(128)(4,1)} %bitcast.164), calls=%async_computation.5 | async-start | bytes 8388608
  487.1 11.2 %slice-start.6 = ((s8[4718592]{0:T(1024)(128)(4,1)}), s8[524288]{0:T(1024)(128)(4,1)S(1)}, s32[]{:S(2)}) async-start(s8[4718592]{0:T(1024)(128)(4,1)} %bitcast.164), calls=%async_computation.6 | async-start | bytes 1048576
  538.4 23.7 %copy-start.52 = (f32[64,4,96]{2,1,0:T(4,128)S(1)}, f32[64,4,96]{2,1,0:T(4,128)}, u32[]{:S(2)}) copy-start(f32[64,4,96]{2,1,0:T(4,128)} %copy.48) | copy-start | bytes 294916
  911.9 12.2 %copy-start.67 = (f32[2,24,128]{2,1,0:T(8,128)S(1)}, f32[2,24,128]{2,1,0:T(8,128)}, u32[]{:S(2)}) copy-start(f32[2,24,128]{2,1,0:T(8,128)} %get-tuple-element.57) | copy-start | bytes 73732
  911.9 12.8 %copy-start.17 = (f32[128,1536]{1,0:T(8,128)S(1)}, f32[128,1536]{1,0:T(8,128)}, u32[]{:S(2)}) copy-start(f32[128,1536]{1,0:T(8,128)} %copy-done.16) | copy-start | bytes 2359300
  911.9 12.8 %copy-start.38 = (f32[128,1536]{1,0:T(8,128)S(1)}, f32[128,1536]{1,0:T(8,128)}, u32[]{:S(2)}) copy-start(f32[128,1536]{1,0:T(8,128)} %get-tuple-element.99) | copy-start | bytes 2359300
  912.0 12.8 %copy-start.65 = (f32[1536]{0:T(1024)S(1)}, f32[1536]{0:T(1024)}, u32[]{:S(2)}) copy-start(f32[1536]{0:T(1024)} %get-tuple-element.102) | copy-start | bytes 18436
  912.0 12.8 %copy-start.69 = (f32[128]{0:T(128)S(1)}, f32[128]{0:T(128)}, u32[]{:S(2)}) copy-start(f32[128]{0:T(128)} %copy-done.68) | copy-start | bytes 1540
  (56 other events, 220.3 us)

commit v2 on v1

--- a/solution.py
+++ b/solution.py
@@ -236,7 +236,7 @@
             pltpu.SemaphoreType.DMA((n, 2, 7)),
         ],
         compiler_params=pltpu.CompilerParams(
-            collective_id=1, has_side_effects=True, vmem_limit_bytes=24 * MIB
+            collective_id=1, has_side_effects=True, vmem_limit_bytes=60 * MIB
         ),
         name="gather_weights",
     )(*shards)
@@ -377,10 +377,11 @@
             else:
                 mine = total[i].at[pl.ds(pl.multiple_of(me.c * rows, 8), rows)]
                 theirs = total[i].at[pl.ds(pl.multiple_of((1 - me.c) * rows, 8), rows)]
-                cp = pltpu.make_async_copy(mine, outs[i].at[me.c], keep.at[i])
+                place = outs[i].at[:, pl.ds(pl.multiple_of(me.c * width, LANES), width)]
+                cp = pltpu.make_async_copy(mine, place, keep.at[i])
                 cp.start()
                 loads[i, "keep"] = cp
-                cp = remote(theirs, outs[i].at[me.c], fin.at[0, i], fin.at[1, i], me.sibling())
+                cp = remote(theirs, place, fin.at[0, i], fin.at[1, i], me.sibling())
                 cp.start()
                 loads[i, "fin"] = cp
     for i in range(n):
@@ -398,7 +399,7 @@
     bf16 = jnp.bfloat16
     return pl.pallas_call(
         scatter_kernel,
-        out_shape=[jax.ShapeDtypeStruct((2, rows, width), jnp.float32) for rows, width, _, _ in PIECES],
+        out_shape=[jax.ShapeDtypeStruct((rows, 2 * width), jnp.float32) for rows, width, _, _ in PIECES],
         in_specs=[ANY] * n,
         out_specs=[ANY] * n,
         scratch_shapes=[pltpu.VMEM((2, 4, *shape), bf16) for _ in range(5) for shape in shapes]
@@ -420,141 +421,300 @@
     )(*[part.reshape(2, 4, 4, *shape) for part, shape in zip(parts, shapes, strict=True)])
 
 
-def meet_plane(me, count):
+ORIGINS = 32
+BLOCK = 8
+BLOCKS = ORIGINS // BLOCK
+
+
+def meet_plane(me):
     barrier = pltpu.get_barrier_semaphore()
 
     def greet(k, carry):
-        to = lax.rem(me.q + k, count)
+        to = lax.rem(me.q + k, ORIGINS)
         pl.semaphore_signal(barrier, inc=1, device_id=(me.s, me.d, to), device_id_type=MESH)
         return carry
 
-    lax.fori_loop(1, count, greet, 0)
-    pl.semaphore_wait(barrier, count - 1)
-
-
-def all_to_all(me, src, dst_of, send_sem, recv_sem, own_sem):
-    count = src.shape[0]
-    own = pltpu.make_async_copy(src.at[me.q], dst_of(me.q, me.q), own_sem)
-    own.start()
-
-    def out(k, carry):
-        to = lax.rem(me.q + k, count)
-        remote(
-            src.at[to], dst_of(me.q, to), send_sem.at[to], recv_sem.at[me.q], (me.s, me.d, to)
-        ).start()
-        return carry
-
-    lax.fori_loop(1, count, out, 0)
-
-    def arrive(k, carry):
-        origin = lax.rem(me.q + k, count)
-        remote(
-            src.at[origin],
-            dst_of(origin, me.q),
-            send_sem.at[origin],
-            recv_sem.at[origin],
-            (me.s, me.d, origin),
-        ).wait()
-        return carry
-
-    lax.fori_loop(1, count, arrive, 0)
-    own.wait()
-
-
-def spread_kernel(src, dst, send_sem, recv_sem, own_sem, sib):
+    lax.fori_loop(1, ORIGINS, greet, 0)
+    pl.semaphore_wait(barrier, ORIGINS - 1)
+
+
+class Exchange:
+    def __init__(self, me, src, dst_of, sems):
+        self.me, self.src, self.dst_of, self.sems = me, src, dst_of, sems
+
+    def copy(self, origin, to):
+        me, (send, recv, _) = self.me, self.sems
+        peer = to + origin - me.q
+        return remote(
+            self.src.at[to], self.dst_of(origin, to), send.at[to], recv.at[origin], (me.s, me.d, peer)
+        )
+
+    def own(self):
+        q = self.me.q
+        return pltpu.make_async_copy(self.src.at[q], self.dst_of(q, q), self.sems[2].at[0])
+
+    def start_all(self):
+        self.own().start()
+
+        def step(k, carry):
+            self.copy(self.me.q, lax.rem(self.me.q + k, ORIGINS)).start()
+            return carry
+
+        lax.fori_loop(1, ORIGINS, step, 0)
+
+    def start(self, block):
+        def step(k, carry):
+            to = block * BLOCK + lax.rem(self.me.q + k, BLOCK)
+
+            @pl.when(to == self.me.q)
+            def _():
+                self.own().start()
+
+            @pl.when(to != self.me.q)
+            def _():
+                self.copy(self.me.q, to).start()
+
+            return carry
+
+        lax.fori_loop(0, BLOCK, step, 0)
+
+    def arrived(self, first, count):
+        def step(k, carry):
+            origin = first + k
+
+            @pl.when(origin == self.me.q)
+            def _():
+                self.own().wait()
+
+            @pl.when(origin != self.me.q)
+            def _():
+                self.copy(origin, self.me.q).wait_recv()
+
+            return carry
+
+        lax.fori_loop(0, count, step, 0)
+
+    def sent(self):
+        def step(k, carry):
+            self.copy(self.me.q, lax.rem(self.me.q + k, ORIGINS)).wait_send()
+            return carry
+
+        lax.fori_loop(1, ORIGINS, step, 0)
+
+
+EXCHANGE_SEMS = [
+    pltpu.SemaphoreType.DMA((ORIGINS,)),
+    pltpu.SemaphoreType.DMA((ORIGINS,)),
+    pltpu.SemaphoreType.DMA((1,)),
+]
+
+
+def block_mask(block, keys, core, prefix_len):
+    rows = BLOCK * 32
+    row = lax.broadcasted_iota(jnp.int32, (rows, keys), 0)
+    key = lax.broadcasted_iota(jnp.int32, (rows, keys), 1)
+    pos = block * BLOCK * 64 + 64 * (row // 32) + 32 * core + row % 32
+    return (key <= pos) | (key < prefix_len)
+
+
+def keys_of(block):
+    return max((block + 1) * BLOCK * 64, PREFIX_MAX)
+
+
+def group(block):
+    return pl.ds(block * BLOCK, BLOCK)
+
+
+def attend_steps(me, prefix, src, whole, dst, out, there, back, sib):
+    prefix_len = prefix[0]
+    coming = Exchange(me, src, lambda origin, to: whole.at[origin, lax.rem(to, 2)], there)
+    going = Exchange(me, out, lambda origin, to: dst.at[origin], back)
+    coming.start_all()
+    yield
+    shares = []
+    for block in range(BLOCKS):
+        coming.arrived(block * BLOCK, BLOCK)
+        mine = whole.at[group(block), me.c]
+        cp = remote(mine, mine, sib.at[0, block], sib.at[1, block], me.sibling())
+        cp.start()
+        shares.append(cp)
+    ready = 0
+    for block in range(BLOCKS):
+        keys = keys_of(block)
+        while ready * BLOCK * 64 < keys:
+            shares[ready].wait_recv()
+            ready += 1
+        src_rows = group(block)
+        k = whole[pl.ds(0, keys // 64), :, :, 0:128].reshape(keys, LANES)
+        v = whole[pl.ds(0, keys // 64), :, :, 128:256].reshape(keys, LANES)
+        allowed = block_mask(block, keys, me.c, prefix_len)
+        for h in range(2):
+            lanes = slice(256 + 128 * h, 384 + 128 * h)
+            q = whole[src_rows, me.c, :, lanes].reshape(BLOCK * 32, LANES)
+            s = jnp.where(allowed, f32dot(q, k, ((1,), (1,))) * SCALE, NEG)
+            top = jnp.max(s, axis=-1, keepdims=True)
+            e = jnp.exp(s - top)
+            p = (e * (1.0 / jnp.sum(e, axis=-1, keepdims=True))).astype(jnp.bfloat16)
+            o = f32dot(p, v, ((1,), (0,)))
+            out[src_rows, :, 128 * h : 128 * h + 128] = o.astype(jnp.bfloat16).reshape(BLOCK, 32, LANES)
+        going.start(block)
+        yield
+    going.arrived(0, ORIGINS)
+    coming.sent()
+    going.sent()
+    for cp in shares:
+        cp.wait_send()
+
+
+ATTEND_SCRATCH = [
+    pltpu.VMEM((ORIGINS, 32, 256), jnp.bfloat16),
+    *EXCHANGE_SEMS,
+    *EXCHANGE_SEMS,
+    pltpu.SemaphoreType.DMA((2, BLOCKS)),
+]
+
+
+def attend_kernel(prefix, src, whole, dst, out, *sems):
     me = Place()
-    meet_plane(me, src.shape[0])
-    all_to_all(
-        me, src, lambda origin, to: dst.at[origin, lax.rem(to, 2)], send_sem, recv_sem, own_sem.at[0]
-    )
-    mine = dst.at[pl.ds(0, src.shape[0]), me.c]
-    cp = remote(mine, mine, sib.at[0], sib.at[1], me.sibling())
-    cp.start()
-    cp.wait()
-
-
-def spread(src):
-    count, rows, width = src.shape
+    meet_plane(me)
+    for _ in attend_steps(me, prefix, src, whole, dst, out, sems[:3], sems[3:6], sems[6]):
+        pass
+
+
+def attend(prefix, src):
+    _, rows, width = src.shape
     return pl.pallas_call(
-        spread_kernel,
-        out_shape=jax.ShapeDtypeStruct((count, 2, rows, width), src.dtype),
-        in_specs=[VMEM],
+        attend_kernel,
+        out_shape=[
+            jax.ShapeDtypeStruct((ORIGINS, 2, rows, width), jnp.bfloat16),
+            jax.ShapeDtypeStruct((ORIGINS, rows, width // 2), jnp.bfloat16),
+        ],
+        in_specs=[SMEM, VMEM],
+        out_specs=[VMEM, VMEM],
+        scratch_shapes=ATTEND_SCRATCH,
+        compiler_params=pltpu.CompilerParams(
+            collective_id=3, has_side_effects=True, vmem_limit_bytes=56 * MIB
+        ),
+        name="attend",
+    )(prefix, src)
+
+
+def attend_back_steps(me, prefix, whole, src, dst, datt, acc, theirs, dq, bundle, there, back, sib):
+    prefix_len = prefix[0]
+    coming = Exchange(me, src, lambda origin, to: datt.at[origin], there)
+    going = Exchange(me, bundle, lambda origin, to: dst.at[origin], back)
+    coming.start_all()
+    yield
+    coming.arrived(0, ORIGINS)
+    shares = {}
+
+    def share(block):
+        cp = remote(
+            acc.at[group(block), 1 - me.c],
+            theirs.at[group(block)],
+            sib.at[0, block],
+            sib.at[1, block],
+            me.sibling(),
+        )
+        cp.start()
+        shares[block] = cp
+
+    def finish(block):
+        shares[block].wait_recv()
+
+        def step(i, carry):
+            both = acc[block * BLOCK + i, me.c] + theirs[block * BLOCK + i]
+            bundle[block * BLOCK + i, :, 0:128] = (both[:, 0:128] * SCALE).astype(jnp.bfloat16)
+            bundle[block * BLOCK + i, :, 128:256] = both[:, 128:256].astype(jnp.bfloat16)
+            bundle[block * BLOCK + i, :, 256:512] = dq[block * BLOCK + i]
+            return carry
+
+        lax.fori_loop(0, BLOCK, step, 0)
+        going.start(block)
+
+    for block in reversed(range(BLOCKS)):
+        keys = keys_of(block)
+        spread = pl.ds(0, keys // 64)
+        src_rows = group(block)
+        k = whole[spread, :, :, 0:128].reshape(keys, LANES)
+        v = whole[spread, :, :, 128:256].reshape(keys, LANES)
+        allowed = block_mask(block, keys, me.c, prefix_len)
+        for h in range(2):
+            lanes = slice(256 + 128 * h, 384 + 128 * h)
+            q = whole[src_rows, me.c, :, lanes].reshape(BLOCK * 32, LANES)
+            g = datt[src_rows, :, 128 * h : 128 * h + 128].reshape(BLOCK * 32, LANES)
+            s = jnp.where(allowed, f32dot(q, k, ((1,), (1,))) * SCALE, NEG)
+            top = jnp.max(s, axis=-1, keepdims=True)
+            e = jnp.exp(s - top)
+            p = e * (1.0 / jnp.sum(e, axis=-1, keepdims=True))
+            dp = f32dot(g, v, ((1,), (1,)))
+            delta = jnp.sum(p * dp, axis=-1, keepdims=True)
+            ds = (p * (dp - delta)).astype(jnp.bfloat16)
+            dq[src_rows, :, 128 * h : 128 * h + 128] = (
+                (f32dot(ds, k, ((1,), (0,))) * SCALE).astype(jnp.bfloat16).reshape(BLOCK, 32, LANES)
+            )
+            dk = f32dot(ds, q, ((0,), (0,))).reshape(keys // 64, 2, 32, LANES)
+            dv = f32dot(p.astype(jnp.bfloat16), g, ((0,), (0,))).reshape(keys // 64, 2, 32, LANES)
+            if block == BLOCKS - 1 and h == 0:
+                acc[spread, :, :, 0:128] = dk
+                acc[spread, :, :, 128:256] = dv
+            else:
+                acc[spread, :, :, 0:128] += dk
+                acc[spread, :, :, 128:256] += dv
+        if block >= 2:
+            share(block)
+        if block == 2:
+            finish(3)
+        if block == 1:
+            finish(2)
+        if block == 0:
+            share(1)
+            share(0)
+            finish(1)
+            finish(0)
+        yield
+    going.arrived(0, ORIGINS)
+    coming.sent()
+    going.sent()
+    for cp in shares.values():
+        cp.wait_send()
+
+
+ATTEND_BACK_SCRATCH = [
+    pltpu.VMEM((ORIGINS, 32, 256), jnp.bfloat16),
+    pltpu.VMEM((ORIGINS, 2, 32, 256), jnp.float32),
+    pltpu.VMEM((ORIGINS, 32, 256), jnp.float32),
+    pltpu.VMEM((ORIGINS, 32, 256), jnp.bfloat16),
+    pltpu.VMEM((ORIGINS, 32, 512), jnp.bfloat16),
+    *EXCHANGE_SEMS,
+    *EXCHANGE_SEMS,
+    pltpu.SemaphoreType.DMA((2, BLOCKS)),
+]
+
+
+def attend_back_kernel(prefix, whole, src, dst, *scratch):
+    me = Place()
+    meet_plane(me)
+    sems = scratch[5:]
+    for _ in attend_back_steps(
+        me, prefix, whole, src, dst, *scratch[:5], sems[:3], sems[3:6], sems[6]
+    ):
+        pass
+
+
+def attend_back(prefix, whole, src):
+    _, rows, width = src.shape
+    return pl.pallas_call(
+        attend_back_kernel,
+        out_shape=jax.ShapeDtypeStruct((ORIGINS, rows, 2 * width), jnp.bfloat16),
+        in_specs=[SMEM, VMEM, VMEM],
         out_specs=VMEM,
-        scratch_shapes=[
-            pltpu.SemaphoreType.DMA((count,)),
-            pltpu.SemaphoreType.DMA((count,)),
-            pltpu.SemaphoreType.DMA((1,)),
-            pltpu.SemaphoreType.DMA((2,)),
-        ],
+        scratch_shapes=ATTEND_BACK_SCRATCH,
         compiler_params=pltpu.CompilerParams(
-            collective_id=3, has_side_effects=True, vmem_limit_bytes=16 * MIB
+            collective_id=4, has_side_effects=True, vmem_limit_bytes=56 * MIB
         ),
-        name="spread",
-    )(src)
-
-
-def swap_kernel(src, dst, send_sem, recv_sem, own_sem):
-    me = Place()
-    meet_plane(me, src.shape[0])
-    all_to_all(me, src, lambda origin, to: dst.at[origin], send_sem, recv_sem, own_sem.at[0])
-
-
-def swap(src):
-    count = src.shape[0]
-    return pl.pallas_call(
-        swap_kernel,
-        out_shape=jax.ShapeDtypeStruct(src.shape, src.dtype),
-        in_specs=[VMEM],
-        out_specs=VMEM,
-        scratch_shapes=[
-            pltpu.SemaphoreType.DMA((count,)),
-            pltpu.SemaphoreType.DMA((count,)),
-            pltpu.SemaphoreType.DMA((1,)),
-        ],
-        compiler_params=pltpu.CompilerParams(
-            collective_id=4, has_side_effects=True, vmem_limit_bytes=16 * MIB
-        ),
-        name="swap",
-    )(src)
-
-
-def return_kernel(dkv, dq, dst, got, bundle, send_sem, recv_sem, own_sem, sib):
-    me = Place()
-    count = dq.shape[0]
-    meet_plane(me, count)
-    cp = remote(dkv.at[pl.ds(0, count), 1 - me.c], got, sib.at[0], sib.at[1], me.sibling())
-    cp.start()
-    cp.wait()
-
-    def step(k, carry):
-        bundle[k, :, 0:256] = (dkv[k, me.c] + got[k]).astype(jnp.bfloat16)
-        bundle[k, :, 256:512] = dq[k]
-        return carry
-
-    lax.fori_loop(0, count, step, 0)
-    all_to_all(me, bundle, lambda origin, to: dst.at[origin], send_sem, recv_sem, own_sem.at[0])
-
-
-def send_back(dkv, dq):
-    count, rows, _ = dq.shape
-    return pl.pallas_call(
-        return_kernel,
-        out_shape=jax.ShapeDtypeStruct((count, rows, 512), jnp.bfloat16),
-        in_specs=[VMEM] * 2,
-        out_specs=VMEM,
-        scratch_shapes=[
-            pltpu.VMEM((count, rows, 256), jnp.float32),
-            pltpu.VMEM((count, rows, 512), jnp.bfloat16),
-            pltpu.SemaphoreType.DMA((count,)),
-            pltpu.SemaphoreType.DMA((count,)),
-            pltpu.SemaphoreType.DMA((1,)),
-            pltpu.SemaphoreType.DMA((2,)),
-        ],
-        compiler_params=pltpu.CompilerParams(
-            collective_id=5, has_side_effects=True, vmem_limit_bytes=24 * MIB
-        ),
-        name="send_back",
-    )(dkv, dq)
+        name="attend_back",
+    )(prefix, whole, src)
 
 
 def pair_kernel(whole_count, *refs):
@@ -565,8 +725,11 @@
     meet([me.sibling()])
     copies = []
     for i in range(n):
-        here = ins[i] if i < whole_count else ins[i].at[me.c]
-        there = ins[i] if i < whole_count else ins[i].at[1 - me.c]
+        here = there = ins[i]
+        if i >= whole_count:
+            width = ins[i].shape[1] // 2
+            here = ins[i].at[:, pl.ds(pl.multiple_of(me.c * width, LANES), width)]
+            there = ins[i].at[:, pl.ds(pl.multiple_of((1 - me.c) * width, LANES), width)]
         cp = remote(there, outs[i].at[me.c], send_sem.at[i], recv_sem.at[i], me.sibling())
         cp.start()
         copies.append(cp)
@@ -582,150 +745,164 @@
     return pl.pallas_call(
         functools.partial(pair_kernel, len(whole)),
         out_shape=[jax.ShapeDtypeStruct((2, *a.shape), a.dtype) for a in whole]
-        + [jax.ShapeDtypeStruct(a.shape, a.dtype) for a in halved],
-        in_specs=[ANY] * n,
-        out_specs=[ANY] * n,
+        + [jax.ShapeDtypeStruct((2, a.shape[0], a.shape[1] // 2), a.dtype) for a in halved],
+        in_specs=[VMEM] * n,
+        out_specs=[VMEM] * n,
         scratch_shapes=[pltpu.SemaphoreType.DMA((n,))] * 3,
-        compiler_params=pltpu.CompilerParams(collective_id=6, has_side_effects=True),
+        compiler_params=pltpu.CompilerParams(
+            collective_id=6, has_side_effects=True, vmem_limit_bytes=40 * MIB
+        ),
         name="pair_up",
     )(*whole, *halved)
 
 
-ORIGINS = 32
-BLOCK = 8
-
-
-def block_mask(block, keys, core, prefix_len):
-    rows = BLOCK * 32
-    row = lax.broadcasted_iota(jnp.int32, (rows, keys), 0)
-    key = lax.broadcasted_iota(jnp.int32, (rows, keys), 1)
-    pos = block * BLOCK * 64 + 64 * (row // 32) + 32 * core + row % 32
-    return (key <= pos) | (key < prefix_len)
-
-
-def keys_of(block):
-    return max((block + 1) * BLOCK * 64, PREFIX_MAX)
-
-
-def attend_kernel(meta, bundle, out):
-    core, prefix_len = meta[0], meta[1]
-    for block in range(ORIGINS // BLOCK):
-        keys = keys_of(block)
-        src = pl.ds(block * BLOCK, BLOCK)
-        k = bundle[pl.ds(0, keys // 64), :, :, 0:128].reshape(keys, LANES)
-        v = bundle[pl.ds(0, keys // 64), :, :, 128:256].reshape(keys, LANES)
-        allowed = block_mask(block, keys, core, prefix_len)
-        for h in range(2):
-            lanes = slice(256 + 128 * h, 384 + 128 * h)
-            q = bundle[src, core, :, lanes].reshape(BLOCK * 32, LANES)
-            s = jnp.where(allowed, f32dot(q, k, ((1,), (1,))) * SCALE, NEG)
-            top = jnp.max(s, axis=-1, keepdims=True)
-            e = jnp.exp(s - top)
-            p = (e * (1.0 / jnp.sum(e, axis=-1, keepdims=True))).astype(jnp.bfloat16)
-            o = f32dot(p, v, ((1,), (0,)))
-            out[src, :, 128 * h : 128 * h + 128] = o.astype(jnp.bfloat16).reshape(BLOCK, 32, LANES)
-
-
-def attend(meta, bundle):
+STEPS = 8
+FF_BLOCK = 512
+HALF = HEAD // 2
+
+
+def rope_tables(positions):
+    lane = jnp.arange(LANES)
+    frequency = ROPE_BASE ** (-(lane % HALF).astype(jnp.float32) * 2.0 / HEAD)
+    angles = positions.astype(jnp.float32)[:, None] * frequency[None, :]
+    cos, sin = jnp.cos(angles), jnp.sin(angles)
+    low, high = (lane < HALF)[None, :], ((lane >= HALF) & (lane < HEAD))[None, :]
+    return (
+        jnp.where(low | high, cos, 0.0),
+        jnp.where(low, -sin, 0.0),
+        jnp.where(high, sin, 0.0),
+    )
+
+
+def split_four(y):
+    return [y[:, :LANES]] + [pltpu.roll(y, 4 * HEAD - HEAD * h, axis=1)[:, :LANES] for h in (1, 2, 3)]
+
+
+def pack_four(heads):
+    zero = jnp.zeros((heads[0].shape[0], 2 * LANES), jnp.float32)
+    wide = [jnp.concatenate([z, zero], axis=1) for z in heads]
+    total = wide[0]
+    for h in (1, 2, 3):
+        total = total + pltpu.roll(wide[h], HEAD * h, axis=1)
+    return total
+
+
+def turn(z, cos, ahead, back):
+    return z * cos + pltpu.roll(z, LANES - HALF, axis=1) * ahead + pltpu.roll(z, HALF, axis=1) * back
+
+
+def qkv_kernel(x, gain, w, cos, ahead, back, bundle, normed):
+    @pl.when(pl.program_id(0) == 0)
+    def _():
+        hidden = x[...].astype(jnp.float32)
+        r1 = lax.rsqrt(jnp.mean(hidden * hidden, axis=-1, keepdims=True) + EPS)
+        normed[...] = (hidden * r1 * gain[...]).astype(jnp.bfloat16)
+
+    y = f32dot(normed[...], w[...], ((1,), (0,)))
+    tokens = y.shape[0] // 2
+    inside = lax.broadcasted_iota(jnp.int32, (2 * tokens, LANES), 1) < HEAD
+    for h, z in enumerate(split_four(y)):
+        z = jnp.where(inside, z, 0.0) if h == 1 else turn(z, cos[...], ahead[...], back[...])
+        z = z.astype(jnp.bfloat16)
+        for s in range(2):
+            bundle[s, 0, :, LANES * h : LANES * (h + 1)] = z[s * tokens : (s + 1) * tokens]
+
+
+def whole_spec(a):
+    return pl.BlockSpec(a.shape, lambda k: (0,) * a.ndim, pipeline_mode=pl.Buffered(1))
+
+
+def project(x, gain, w, tables):
+    tokens, width = x.shape
     return pl.pallas_call(
-        attend_kernel,
-        out_shape=jax.ShapeDtypeStruct((ORIGINS, 32, 256), jnp.bfloat16),
-        in_specs=[SMEM, VMEM],
-        out_specs=VMEM,
+        qkv_kernel,
+        grid=(KV_HEADS,),
+        out_shape=[
+            jax.ShapeDtypeStruct((2, KV_HEADS, tokens // 2, 4 * LANES), jnp.bfloat16),
+            jax.ShapeDtypeStruct((tokens, width), jnp.bfloat16),
+        ],
+        in_specs=[
+            whole_spec(x),
+            whole_spec(gain),
+            pl.BlockSpec((width, 4 * HEAD), lambda k: (0, k)),
+            *[whole_spec(t) for t in tables],
+        ],
+        out_specs=[
+            pl.BlockSpec((2, 1, tokens // 2, 4 * LANES), lambda k: (0, k, 0, 0)),
+            pl.BlockSpec((tokens, width), lambda k: (0, 0)),
+        ],
+        compiler_params=pltpu.CompilerParams(vmem_limit_bytes=56 * MIB),
+        name="project",
+    )(x, gain, w, *tables)
+
+
+def mlp_kernel(
+    att, x, gain, o_w, gate_w, up_w, down_w, result, attended, middle, normed_two, gate, up, mixed, total
+):
+    k = pl.program_id(0)
+
+    @pl.when(k == 0)
+    def _():
+        for pair in range(KV_HEADS // 2):
+            heads = []
+            for g in (2 * pair, 2 * pair + 1):
+                for h in range(2):
+                    lanes = slice(LANES * h, LANES * (h + 1))
+                    heads.append(
+                        jnp.concatenate([att[0, g, :, lanes], att[1, g, :, lanes]], axis=0).astype(jnp.float32)
+                    )
+            attended[:, 384 * pair : 384 * (pair + 1)] = pack_four(heads).astype(jnp.bfloat16)
+        mid = x[...].astype(jnp.float32) + f32dot(attended[...], o_w[...], ((1,), (0,)))
+        middle[...] = mid
+        r2 = lax.rsqrt(jnp.mean(mid * mid, axis=-1, keepdims=True) + EPS)
+        normed_two[...] = (mid * r2 * gain[...]).astype(jnp.bfloat16)
+        total[...] = mid
+
+    g = f32dot(normed_two[...], gate_w[...], ((1,), (0,)))
+    u = f32dot(normed_two[...], up_w[...], ((1,), (0,)))
+    gate[...] = g
+    up[...] = u
+    m = (g * jax.nn.sigmoid(g) * u).astype(jnp.bfloat16)
+    mixed[...] = m
+    total[...] += f32dot(m, down_w[...], ((1,), (0,)))
+
+    @pl.when(k == STEPS - 1)
+    def _():
+        result[...] = total[...].astype(jnp.bfloat16)
+
+
+def mlp(att, x, gain, o_w, gate_w, up_w, down_w):
+    tokens, width = x.shape
+    ff = gate_w.shape[1]
+    in_block = pl.BlockSpec((width, FF_BLOCK), lambda k: (0, k))
+    ff_block = pl.BlockSpec((tokens, FF_BLOCK), lambda k: (0, k))
+    fixed = pl.BlockSpec((tokens, width), lambda k: (0, 0))
+    return pl.pallas_call(
+        mlp_kernel,
+        grid=(STEPS,),
+        out_shape=[
+            jax.ShapeDtypeStruct((tokens, width), jnp.bfloat16),
+            jax.ShapeDtypeStruct((tokens, width), jnp.bfloat16),
+            jax.ShapeDtypeStruct((tokens, width), jnp.float32),
+            jax.ShapeDtypeStruct((tokens, width), jnp.bfloat16),
+            jax.ShapeDtypeStruct((tokens, ff), jnp.float32),
+            jax.ShapeDtypeStruct((tokens, ff), jnp.float32),
+            jax.ShapeDtypeStruct((tokens, ff), jnp.bfloat16),
+        ],
+        in_specs=[
+            whole_spec(att),
+            whole_spec(x),
+            whole_spec(gain),
+            whole_spec(o_w),
+            in_block,
+            in_block,
+            pl.BlockSpec((FF_BLOCK, width), lambda k: (k, 0)),
+        ],
+        out_specs=[fixed, fixed, fixed, fixed, ff_block, ff_block, ff_block],
+        scratch_shapes=[pltpu.VMEM((tokens, width), jnp.float32)],
         compiler_params=pltpu.CompilerParams(vmem_limit_bytes=48 * MIB),
-        name="attend",
-    )(meta, bundle)
-
-
-def attend_back_kernel(meta, bundle, datt, dkv, dq, dk_sum, dv_sum):
-    core, prefix_len = meta[0], meta[1]
-    dk_sum[...] = jnp.zeros_like(dk_sum)
-    dv_sum[...] = jnp.zeros_like(dv_sum)
-    for block in range(ORIGINS // BLOCK):
-        keys = keys_of(block)
-        src = pl.ds(block * BLOCK, BLOCK)
-        k = bundle[pl.ds(0, keys // 64), :, :, 0:128].reshape(keys, LANES)
-        v = bundle[pl.ds(0, keys // 64), :, :, 128:256].reshape(keys, LANES)
-        allowed = block_mask(block, keys, core, prefix_len)
-        for h in range(2):
-            lanes = slice(256 + 128 * h, 384 + 128 * h)
-            q = bundle[src, core, :, lanes].reshape(BLOCK * 32, LANES)
-            g = datt[src, :, 128 * h : 128 * h + 128].reshape(BLOCK * 32, LANES)
-            s = jnp.where(allowed, f32dot(q, k, ((1,), (1,))) * SCALE, NEG)
-            top = jnp.max(s, axis=-1, keepdims=True)
-            e = jnp.exp(s - top)
-            p = e * (1.0 / jnp.sum(e, axis=-1, keepdims=True))
-            dp = f32dot(g, v, ((1,), (1,)))
-            delta = jnp.sum(p * dp, axis=-1, keepdims=True)
-            ds = (p * (dp - delta)).astype(jnp.bfloat16)
-            dq[src, :, 128 * h : 128 * h + 128] = (
-                (f32dot(ds, k, ((1,), (0,))) * SCALE).astype(jnp.bfloat16).reshape(BLOCK, 32, LANES)
-            )
-            dk_sum[pl.ds(0, keys), :] += f32dot(ds, q, ((0,), (0,)))
-            dv_sum[pl.ds(0, keys), :] += f32dot(p.astype(jnp.bfloat16), g, ((0,), (0,)))
-    dkv[:, :, :, 0:128] = (dk_sum[...] * SCALE).reshape(ORIGINS, 2, 32, LANES)
-    dkv[:, :, :, 128:256] = dv_sum[...].reshape(ORIGINS, 2, 32, LANES)
-
-
-def attend_back(meta, bundle, datt):
-    return pl.pallas_call(
-        attend_back_kernel,
-        out_shape=[
-            jax.ShapeDtypeStruct((ORIGINS, 2, 32, 256), jnp.float32),
-            jax.ShapeDtypeStruct((ORIGINS, 32, 256), jnp.bfloat16),
-        ],
-        in_specs=[SMEM, VMEM, VMEM],
-        out_specs=[VMEM, VMEM],
-        scratch_shapes=[pltpu.VMEM((ORIGINS * 64, LANES), jnp.float32)] * 2,
-        compiler_params=pltpu.CompilerParams(vmem_limit_bytes=56 * MIB),
-        name="attend_back",
-    )(meta, bundle, datt)
-
-
-def mm(a, b):
-    return jnp.dot(a, b, preferred_element_type=jnp.float32)
-
-
-def mm_t(a, b):
-    return lax.dot_general(a, b, (((1,), (1,)), ((), ())), preferred_element_type=jnp.float32)
-
-
-def rope_tables(positions):
-    half = HEAD // 2
-    frequency = ROPE_BASE ** (-jnp.arange(half, dtype=jnp.float32) * 2.0 / HEAD)
-    angles = positions.astype(jnp.float32)[:, None] * frequency[None, :]
-    cos = jnp.concatenate([jnp.cos(angles)] * 2, -1)[:, None, None, :]
-    sin = jnp.concatenate([jnp.sin(angles)] * 2, -1)[:, None, None, :]
-    turned = (jnp.arange(4) != 1)[None, None, :, None]
-    return jnp.where(turned, cos, 1.0), jnp.where(turned, sin, 0.0)
-
-
-def forward(x, weights, tables, meta):
-    qkv_w, o_w, gate_w, up_w, down_w, gain_attn, gain_mlp = weights
-    cos, sin = tables
-    tokens, width = x.shape
-    hidden = x.astype(jnp.float32)
-    r1 = lax.rsqrt(jnp.mean(hidden * hidden, axis=-1, keepdims=True) + EPS)
-    normed = (hidden * r1 * gain_attn).astype(jnp.bfloat16)
-    qkv = mm(normed, qkv_w).reshape(2, 64, KV_HEADS, 4, HEAD)
-    half = HEAD // 2
-    turned = jnp.concatenate([-qkv[..., half:], qkv[..., :half]], -1)
-    bundle = (qkv * cos + turned * sin).astype(jnp.bfloat16)
-    bundle = jnp.pad(bundle, ((0, 0),) * 4 + ((0, LANES - HEAD),))
-    bundle = bundle.transpose(0, 2, 1, 3, 4).reshape(32, 32, 512)
-    whole = spread(bundle)
-    out = swap(attend(meta, whole))
-    attended = (
-        out.reshape(2, KV_HEADS, 64, 2, LANES)[..., :HEAD].transpose(0, 2, 1, 3, 4).reshape(tokens, width)
-    )
-    middle = hidden + mm(attended, o_w)
-    r2 = lax.rsqrt(jnp.mean(middle * middle, axis=-1, keepdims=True) + EPS)
-    normed_two = (middle * r2 * gain_mlp).astype(jnp.bfloat16)
-    gate = mm(normed_two, gate_w)
-    up = mm(normed_two, up_w)
-    mixed = (jax.nn.silu(gate) * up).astype(jnp.bfloat16)
-    result = (middle + mm(mixed, down_w)).astype(jnp.bfloat16)
-    return result, (hidden, r1, normed, whole, attended, middle, r2, normed_two, gate, up, mixed)
+        name="mlp",
+    )(att, x, gain, o_w, gate_w, up_w, down_w)
 
 
 def norm_back(dn, gain, u, r):
@@ -733,41 +910,164 @@
     return r * (scaled - u * jnp.mean(scaled * u, axis=-1, keepdims=True))
 
 
-def backward(g_low, state, weights, tables, meta):
+def mlp_back_kernel(
+    g_low, gate, up, middle, gain, o_w, gate_w, up_w, down_w, dgate, dup, dmiddle, db, dgain, datt, total
+):
+    k = pl.program_id(0)
+
+    @pl.when(k == 0)
+    def _():
+        total[...] = jnp.zeros_like(total)
+
+    gm = f32dot(g_low[...], down_w[...], ((1,), (1,)))
+    sig = jax.nn.sigmoid(gate[...])
+    dg = (gm * up[...] * sig * (1.0 + gate[...] * (1.0 - sig))).astype(jnp.bfloat16)
+    du = (gm * (gate[...] * sig)).astype(jnp.bfloat16)
+    dgate[...] = dg
+    dup[...] = du
+    total[...] += f32dot(dg, gate_w[...], ((1,), (1,))) + f32dot(du, up_w[...], ((1,), (1,)))
+
+    @pl.when(k == STEPS - 1)
+    def _():
+        mid, dn2 = middle[...], total[...]
+        r2 = lax.rsqrt(jnp.mean(mid * mid, axis=-1, keepdims=True) + EPS)
+        u2 = mid * r2
+        dgain[...] = jnp.broadcast_to(jnp.sum(dn2 * u2, axis=0, keepdims=True), dgain.shape)
+        dm = g_low[...].astype(jnp.float32) + norm_back(dn2, gain[...], u2, r2)
+        dmiddle[...] = dm
+        low = dm.astype(jnp.bfloat16)
+        db[...] = low
+        tokens = low.shape[0] // 2
+        inside = lax.broadcasted_iota(jnp.int32, (2 * tokens, LANES), 1) < HEAD
+        for pair in range(KV_HEADS // 2):
+            y = f32dot(low, o_w[384 * pair : 384 * (pair + 1), :], ((1,), (1,)))
+            for i, z in enumerate(split_four(y)):
+                z = jnp.where(inside, z, 0.0).astype(jnp.bfloat16)
+                lanes = slice(LANES * (i % 2), LANES * (i % 2 + 1))
+                for s in range(2):
+                    datt[s, 2 * pair + i // 2, :, lanes] = z[s * tokens : (s + 1) * tokens]
+
+
+def mlp_back(g_low, gate, up, middle, gain, o_w, gate_w, up_w, down_w):
+    tokens, width = g_low.shape
+    ff = gate_w.shape[1]
+    in_block = pl.BlockSpec((width, FF_BLOCK), lambda k: (0, k))
+    ff_block = pl.BlockSpec((tokens, FF_BLOCK), lambda k: (0, k))
+    fixed = pl.BlockSpec((tokens, width), lambda k: (0, 0))
+    datt_shape = (2, KV_HEADS, tokens // 2, 2 * LANES)
+    return pl.pallas_call(
+        mlp_back_kernel,
+        grid=(STEPS,),
+        out_shape=[
+            jax.ShapeDtypeStruct((tokens, ff), jnp.bfloat16),
+            jax.ShapeDtypeStruct((tokens, ff), jnp.bfloat16),
+            jax.ShapeDtypeStruct((tokens, width), jnp.float32),
+            jax.ShapeDtypeStruct((tokens, width), jnp.bfloat16),
+            jax.ShapeDtypeStruct((8, width), jnp.float32),
+            jax.ShapeDtypeStruct(datt_shape, jnp.bfloat16),
+        ],
+        in_specs=[
+            whole_spec(g_low),
+            ff_block,
+            ff_block,
+            whole_spec(middle),
+            whole_spec(gain),
+            whole_spec(o_w),
+            in_block,
+            in_block,
+            pl.BlockSpec((FF_BLOCK, width), lambda k: (k, 0)),
+        ],
+        out_specs=[
+            ff_block,
+            ff_block,
+            fixed,
+            fixed,
+            pl.BlockSpec((8, width), lambda k: (0, 0)),
+            pl.BlockSpec(datt_shape, lambda k: (0, 0, 0, 0)),
+        ],
+        scratch_shapes=[pltpu.VMEM((tokens, width), jnp.float32)],
+        compiler_params=pltpu.CompilerParams(vmem_limit_bytes=48 * MIB),
+        name="mlp_back",
+    )(g_low, gate, up, middle, gain, o_w, gate_w, up_w, down_w)
+
+
+def qkv_back_kernel(back_in, cos, ahead, back, w, x, dmiddle, gain, dqkv, dx, dgain, total):
+    k = pl.program_id(0)
+
+    @pl.when(k == 0)
+    def _():
+        total[...] = jnp.zeros_like(total)
+
+    heads = []
+    for h in range(4):
+        lanes = slice(LANES * h, LANES * (h + 1))
+        z = jnp.concatenate([back_in[0, 0, :, lanes], back_in[1, 0, :, lanes]], axis=0).astype(jnp.float32)
+        heads.append(z if h == 1 else turn(z, cos[...], -ahead[...], -back[...]))
+    packed = pack_four(heads).astype(jnp.bfloat16)
+    dqkv[...] = packed
+    total[...] += f32dot(packed, w[...], ((1,), (1,)))
+
+    @pl.when(k == KV_HEADS - 1)
+    def _():
+        hidden, dn1 = x[...].astype(jnp.float32), total[...]
+        r1 = lax.rsqrt(jnp.mean(hidden * hidden, axis=-1, keepdims=True) + EPS)
+        u1 = hidden * r1
+        dgain[...] = jnp.broadcast_to(jnp.sum(dn1 * u1, axis=0, keepdims=True), dgain.shape)
+        dx[...] = (dmiddle[...] + norm_back(dn1, gain[...], u1, r1)).astype(jnp.bfloat16)
+
+
+def project_back(back_in, tables, w, x, dmiddle, gain):
+    tokens, width = x.shape
+    return pl.pallas_call(
+        qkv_back_kernel,
+        grid=(KV_HEADS,),
+        out_shape=[
+            jax.ShapeDtypeStruct((tokens, 2 * width), jnp.bfloat16),
+            jax.ShapeDtypeStruct((tokens, width), jnp.bfloat16),
+            jax.ShapeDtypeStruct((8, width), jnp.float32),
+        ],
+        in_specs=[
+            pl.BlockSpec((2, 1, tokens // 2, 4 * LANES), lambda k: (0, k, 0, 0)),
+            *[whole_spec(t) for t in tables],
+            pl.BlockSpec((width, 4 * HEAD), lambda k: (0, k)),
+            whole_spec(x),
+            whole_spec(dmiddle),
+            whole_spec(gain),
+        ],
+        out_specs=[
+            pl.BlockSpec((tokens, 4 * HEAD), lambda k: (0, k)),
+            pl.BlockSpec((tokens, width), lambda k: (0, 0)),
+            pl.BlockSpec((8, width), lambda k: (0, 0)),
+        ],
+        scratch_shapes=[pltpu.VMEM((tokens, width), jnp.float32)],
+        compiler_params=pltpu.CompilerParams(vmem_limit_bytes=56 * MIB),
+        name="project_back",
+    )(back_in, *tables, w, x, dmiddle, gain)
+
+
+def forward(x, weights, tables, prefix):
     qkv_w, o_w, gate_w, up_w, down_w, gain_attn, gain_mlp = weights
-    hidden, r1, normed, whole, attended, middle, r2, normed_two, gate, up, mixed = state
-    cos, sin = tables
-    tokens, width = hidden.shape
-    g = g_low.astype(jnp.float32)
-    gm = mm_t(g_low, down_w)
-    sig = jax.nn.sigmoid(gate)
-    dgate = (gm * up * sig * (1.0 + gate * (1.0 - sig))).astype(jnp.bfloat16)
-    dup = (gm * (gate * sig)).astype(jnp.bfloat16)
-    dn2 = mm_t(dgate, gate_w) + mm_t(dup, up_w)
-    u2 = middle * r2
-    dgain_mlp = jnp.sum(dn2 * u2, axis=0)
-    dmiddle = g + norm_back(dn2, gain_mlp, u2, r2)
-    db = dmiddle.astype(jnp.bfloat16)
-    datt = mm_t(db, o_w).astype(jnp.bfloat16).reshape(2, 64, KV_HEADS, 2, HEAD)
-    datt = jnp.pad(datt, ((0, 0),) * 4 + ((0, LANES - HEAD),))
-    datt = swap(datt.transpose(0, 2, 1, 3, 4).reshape(32, 32, 256))
-    dkv, dq = attend_back(meta, whole, datt)
-    back = send_back(dkv, dq).reshape(2, KV_HEADS, 64, 4, LANES)[..., :HEAD]
-    back = back.transpose(0, 2, 1, 3, 4).astype(jnp.float32)
-    half = HEAD // 2
-    slanted = back * sin
-    turned = jnp.concatenate([slanted[..., half:], -slanted[..., :half]], -1)
-    dqkv = (back * cos + turned).astype(jnp.bfloat16).reshape(tokens, 2 * width)
-    dn1 = mm_t(dqkv, qkv_w)
-    u1 = hidden * r1
-    dgain_attn = jnp.sum(dn1 * u1, axis=0)
-    dx = (dmiddle + norm_back(dn1, gain_attn, u1, r1)).astype(jnp.bfloat16)
+    bundle, normed = project(x, gain_attn, qkv_w, tables)
+    seqs, heads, rows, wide = bundle.shape
+    whole, out = attend(prefix, bundle.reshape(2 * seqs * heads, rows // 2, wide))
+    out = out.reshape(seqs, heads, rows, 2 * LANES)
+    result, attended, middle, normed_two, gate, up, mixed = mlp(
+        out, x, gain_mlp, o_w, gate_w, up_w, down_w
+    )
+    return result, (x, normed, whole, attended, middle, normed_two, gate, up, mixed)
+
+
+def backward(g_low, state, weights, tables, prefix):
+    qkv_w, o_w, gate_w, up_w, down_w, gain_attn, gain_mlp = weights
+    x, normed, whole, attended, middle, normed_two, gate, up, mixed = state
+    dgate, dup, dmiddle, db, dgain_mlp, datt = mlp_back(
+        g_low, gate, up, middle, gain_mlp, o_w, gate_w, up_w, down_w
+    )
+    seqs, heads, rows, wide = datt.shape
+    back = attend_back(prefix, whole, datt.reshape(2 * seqs * heads, rows // 2, wide))
+    back = back.reshape(seqs, heads, rows, 4 * LANES)
+    dqkv, dx, dgain_attn = project_back(back, tables, qkv_w, x, dmiddle, gain_attn)
     return dx, (g_low, dgate, dup, db, dqkv, dgain_attn, dgain_mlp)
-
-
-def halves(a):
-    rows, width = a.shape
-    return a.reshape(rows, 2, width // 2).transpose(1, 0, 2)
 
 
 def body(
@@ -778,8 +1078,8 @@
     section = lax.axis_index("section")
     seq = lax.axis_index("seq")
     positions = seq * rows + jnp.arange(rows, dtype=jnp.int32)
-    tables = rope_tables(positions)
-    meta = jnp.stack([seq % 2, lax.dynamic_index_in_dim(prefix, seq // 16, 0, keepdims=False)])
+    tables = rope_tables(jnp.concatenate([positions, positions]))
+    own_prefix = lax.dynamic_slice_in_dim(prefix, seq // 16, 1)
 
     part = w_query.shape[1]
     qkv_shard = jnp.concatenate(
@@ -805,22 +1105,21 @@
     weights = (qkv_w, o_w, gate_w, up_w, down_w, gain_attn, gain_mlp)
 
     x0 = inputs.reshape(tokens, width)
-    out0, _ = forward(x0, weights, tables, meta)
+    out0, _ = forward(x0, weights, tables, own_prefix)
     received = lax.ppermute(out0, "section", [(0, 1)])
     x1 = jnp.where(section == 0, x0, received)
-    out, state = forward(x1, weights, tables, meta)
+    out, state = forward(x1, weights, tables, own_prefix)
 
     g0 = cotangent.reshape(tokens, width)
-    dx0, _ = backward(g0, state, weights, tables, meta)
+    dx0, _ = backward(g0, state, weights, tables, own_prefix)
     received = lax.ppermute(dx0, "section", [(1, 0)])
     g1 = jnp.where(section == 1, g0, received)
-    dx, (g_low, dgate, dup, db, dqkv, dgain_attn, dgain_mlp) = backward(g1, state, weights, tables, meta)
-
-    normed, attended, normed_two, mixed = state[2], state[4], state[7], state[10]
-    dgains = jnp.broadcast_to(jnp.stack([dgain_attn, dgain_mlp])[:, None, :], (2, 8, width))
+    dx, (g_low, dgate, dup, db, dqkv, dgain_attn, dgain_mlp) = backward(g1, state, weights, tables, own_prefix)
+
+    _, normed, _, attended, _, normed_two, _, _, mixed = state
+    dgains = jnp.concatenate([dgain_attn, dgain_mlp], axis=1)
     normed, attended, normed_two, mixed, g_half, dgate, dup, db, dqkv, dgains = pair_up(
-        [normed, attended, normed_two, mixed],
-        [halves(g_low), halves(dgate), halves(dup), halves(db), halves(dqkv), dgains],
+        [normed, attended, normed_two, mixed], [g_low, dgate, dup, db, dqkv, dgains]
     )
 
     def outer(a, b):
@@ -832,7 +1131,7 @@
     gain_part = jnp.broadcast_to(
         (dgains[0, 0] + dgains[1, 0]).astype(jnp.bfloat16)[:, None], (width, LANES)
     )
-    sums = scatter_grads(
+    gate_g, up_g, qkv_g, o_g, gain_g, down_g = scatter_grads(
         [
             outer(normed_two, dgate),
             outer(normed_two, dup),
@@ -842,27 +1141,22 @@
             outer(mixed, g_half),
         ]
     )
-
-    def joined(a):
-        return a.transpose(1, 0, 2).reshape(1, a.shape[1], -1)
-
-    gate_g, up_g, qkv_g, o_g, gain_g, down_g = sums
-    qkv_g = joined(qkv_g).reshape(1, part, KV_HEADS, 4 * HEAD)
+    qkv_g = qkv_g.reshape(1, part, KV_HEADS, 4 * HEAD)
     key_g = qkv_g[..., :HEAD].reshape(1, part, -1)
     value_g = qkv_g[..., HEAD : 2 * HEAD].reshape(1, part, -1)
     query_g = qkv_g[..., 2 * HEAD :].reshape(1, part, -1)
     return (
         out.reshape(1, seqs, rows, width),
         dx.reshape(1, seqs, rows, width),
-        gain_g[0, :, 0][None],
+        gain_g[:, 0][None],
         query_g,
         key_g,
         value_g,
-        joined(o_g),
-        gain_g[1, :, 0][None],
-        joined(gate_g),
-        joined(up_g),
-        joined(down_g),
+        o_g[None],
+        gain_g[:, LANES][None],
+        gate_g[None],
+        up_g[None],
+        down_g[None],
     )
 
 

time: 934 us -> 728 us (0.78)
  matrix products: 157 us -> 20.7 us
  local copies, waits for them, and re-layouts: 91.4 us -> 37.6 us
  other arithmetic: 16.1 us -> 4.19 us
  waiting for transfers between devices: 10.1 us -> 20.1 us
  Pallas kernels: 645 us -> 635 us
    dot_general x19 -> x0, matrix products: 135 us -> none  [the longest x10 78.9 us: mm_t(): lax.dot_general(a, b, (((1,), (1,)), ((), ())), preferred_element_type=jn...]
    pallas_call x1, Pallas kernels: 127 us -> 7.31 us  [pair_up(): pl.pallas_call(functools.partial(pair_kernel, len(whole)), out_shape=[jax...]
    pallas_call x13, Pallas kernels: 359 us -> 466 us  [the longest x1 155 us: scatter_grads(): pl.pallas_call(scatter_kernel, out_shape=[jax.ShapeDtypeStruct((rows, 2 *...]
    reshape x22 -> x0, local copies, waits for them, and re-layouts: 22 us -> none  [the longest x4 7.11 us: joined(): return a.transpose(1, 0, 2).reshape(1, a.shape[1], -1)]
    dot_general x1 -> x0, local copies, waits for them, and re-layouts: 12.7 us -> none  [mm(): return jnp.dot(a, b, preferred_element_type=jnp.float32)]
    transpose x13 -> x0, local copies, waits for them, and re-layouts: 11.7 us -> none  [the longest x5 7.4 us: joined(): return a.transpose(1, 0, 2).reshape(1, a.shape[1], -1)]
    unnamed x159 -> x78, local copies, waits for them, and re-layouts: 24.2 us -> 26.1 us
  transfers between devices with their start and end apart: 2 -> 2, of which waited for: 1 -> 2; matrix products, arithmetic and copies ran while one was open for 1% -> 0% of each run, Pallas kernels for 0% -> 0%
where the time goes in v2:
time: 728 us; the launch traced here: 722 us
  Pallas kernels  635 us (87%)
  local copies, waits for them, and re-layouts  37.6 us (5%)
  matrix products  20.7 us (3%)
  waiting for transfers between devices  20.1 us (3%)
    pallas_call x1, Pallas kernels, gather_weights(): pl.pallas_call(gather_kernel, out_shape=[jax.ShapeDtypeStruct((2, 4, 4, 2...  161 us
    pallas_call x1, Pallas kernels, scatter_grads(): pl.pallas_call(scatter_kernel, out_shape=[jax.ShapeDtypeStruct((rows, 2 *...  155 us
    pallas_call x2, Pallas kernels, attend_back(): pl.pallas_call(attend_back_kernel, out_shape=jax.ShapeDtypeStruct((ORIGIN...  103 us
    pallas_call x2, Pallas kernels, attend(): pl.pallas_call(attend_kernel, out_shape=[jax.ShapeDtypeStruct((ORIGINS, 2...  78.5 us
    pallas_call x2, Pallas kernels, mlp_back(): pl.pallas_call(mlp_back_kernel, grid=(STEPS,), out_shape=[jax.ShapeDtypeS...  48.4 us
    pallas_call x2, Pallas kernels, mlp(): pl.pallas_call(mlp_kernel, grid=(STEPS,), out_shape=[jax.ShapeDtypeStruct...  40.5 us
    unnamed x78, local copies, waits for them, and re-layouts  26.1 us
    pallas_call x2, Pallas kernels, project_back(): pl.pallas_call(qkv_back_kernel, grid=(KV_HEADS,), out_shape=[jax.ShapeDty...  21.2 us
  transfers between devices with their start and end apart: 2, of which 2 were waited for; matrix products, arithmetic and copies ran while one was open for 0% of the time, Pallas kernels for 0%

profile of v2, /device:TPU:1, one launch (start us, length us, event | category | flops | bytes accessed | tf_op | source)
XLA Modules:
  0.0 722.3 jit_solution(9334434710927478481)
XLA Ops:
  6.5 161.0 %gather_weights.1 = (bf16[2,4,4,48,4096]{4,3,2,1,0:T(8,128)(2,1)}, bf16[2,4,4,48,4096]{4,3,2,1,0:T(8,128)(2,1)}, bf16[2,4,4,48,3072]{4,3,2,1,0:T(8,128)(2,1)}, b...) custom-call(bf16[24,4096]{1,0:T(8,128)(2,1)} %bitcast.119, ...), custom_call_target="tpu_custom_call" | custom-call | tf_op jit(solution)/shard_map/gather_weights/pallas_call | solution.py:219
  171.9 10.0 %project.2 = (bf16[2,8,64,512]{3,2,1,0:T(8,128)(2,1)}, bf16[128,1536]{1,0:T(8,128)(2,1)}) custom-call(bf16[128,1536]{1,0:T(8,128)(2,1)} %bitcast.74, f32[1,1536]{1,0:T(1,128)} %bitcast_convert_fusion.5.gain, bf16[1536,3072]{1,0:T(8,128)(2,1)} %bitcast.93, f32[128,128]{1,0:T(8,128)} %get-tuple-element.115.cos, f32[128,128]{1,0:T(8,128)} %get-tuple-element.114.ahead, ...), custom_call_target="tpu_custom_call" | custom-call | tf_op jit(solution)/shard_map/project/pallas_call | solution.py:817
  181.9 36.0 %attend.2 = (bf16[32,2,32,512]{3,2,1,0:T(8,128)(2,1)}, bf16[32,32,256]{2,1,0:T(8,128)(2,1)}) custom-call(s32[1]{0:T(128)} %dynamic_slice.3.prefix, bf16[32,32,512]{2,1,0:T(8,128)(2,1)} %bitcast.110), custom_call_target="tpu_custom_call" | custom-call | tf_op jit(solution)/shard_map/attend/pallas_call | solution.py:586
  219.0 21.1 %mlp.2 = (bf16[128,1536]{1,0:T(8,128)(2,1)S(1)}, bf16[128,1536]{1,0:T(8,128)(2,1)}, f32[128,1536]{1,0:T(8,128)}, bf16[128,1536]{1,0:T(8,128)(2,1)}, f32[128,4096...) custom-call(bf16[2,8,64,256]{3,2,1,0:T(8,128)(2,1)S(1)} %bitcast.77, bf16[128,1536]{1,0:T(8,128)(2,1)S(1)} %bitcast.75, ...), custom_call_target="tpu_custom_call" | custom-call | tf_op jit(solution)/shard_map/mlp/pallas_call | solution.py:880
  240.1 2.2 collective-permute-start
  242.3 8.1 %collective-permute-done = bf16[128,1536]{1,0:T(8,128)(2,1)S(1)} collective-permute-done((bf16[128,1536]{1,0:T(8,128)(2,1)S(1)}, bf16[128,1536]{1,0:T(8,128)(2,1)S(1)}, u32[]{:S(2)}, u32[]{:S(2)}) %collective-permute-start) | collective-permute-done | bytes 393248 | tf_op jit(solution)/shard_map/ppermute | solution.py:1109
  251.2 10.0 %project.3 = (bf16[2,8,64,512]{3,2,1,0:T(8,128)(2,1)}, bf16[128,1536]{1,0:T(8,128)(2,1)}) custom-call(bf16[128,1536]{1,0:T(8,128)(2,1)} %broadcast_select_fusion.1.x, f32[1,1536]{1,0:T(1,128)} %bitcast_convert_fusion.5.gain, bf16[1536,3072]{1,0:T(8,128)(2,1)} %bitcast.94, f32[128,128]{1,0:T(8,128)} %get-tuple-element.115.cos, ...), custom_call_target="tpu_custom_call" | custom-call | tf_op jit(solution)/shard_map/project/pallas_call | solution.py:817
  261.3 42.4 %attend.3 = (bf16[32,2,32,512]{3,2,1,0:T(8,128)(2,1)}, bf16[32,32,256]{2,1,0:T(8,128)(2,1)}) custom-call(s32[1]{0:T(128)} %dynamic_slice.3.prefix, bf16[32,32,512]{2,1,0:T(8,128)(2,1)} %bitcast.111), custom_call_target="tpu_custom_call" | custom-call | tf_op jit(solution)/shard_map/attend/pallas_call | solution.py:586
  304.8 19.5 %mlp.3 = (bf16[128,1536]{1,0:T(8,128)(2,1)}, bf16[128,1536]{1,0:T(8,128)(2,1)S(1)}, f32[128,1536]{1,0:T(8,128)S(1)}, bf16[128,1536]{1,0:T(8,128)(2,1)S(1)}, f32[...) custom-call(bf16[2,8,64,256]{3,2,1,0:T(8,128)(2,1)S(1)} %bitcast.78, ...), custom_call_target="tpu_custom_call" | custom-call | tf_op jit(solution)/shard_map/mlp/pallas_call | solution.py:880
  326.3 24.9 %mlp_back.2 = (bf16[128,4096]{1,0:T(8,128)(2,1)}, bf16[128,4096]{1,0:T(8,128)(2,1)}, f32[128,1536]{1,0:T(8,128)S(1)}, bf16[128,1536]{1,0:T(8,128)(2,1)}, f32[8,1...) custom-call(bf16[128,1536]{1,0:T(8,128)(2,1)S(1)} %bitcast.76, f32[128,4096]{1,0:T(8,128)} %copy-done.1, ...), custom_call_target="tpu_custom_call" | custom-call | tf_op jit(solution)/shard_map/mlp_back/pallas_call | solution.py:958
  352.9 54.5 %attend_back.2 = bf16[32,32,512]{2,1,0:T(8,128)(2,1)} custom-call(s32[1]{0:T(128)} %dynamic_slice.3.prefix, bf16[32,2,32,512]{3,2,1,0:T(8,128)(2,1)} %get-tuple-element.71.whole, bf16[32,32,256]{2,1,0:T(8,128)(2,1)} %bitcast.80), custom_call_target="tpu_custom_call" | custom-call | tf_op jit(solution)/shard_map/attend_back/pallas_call | solution.py:707
  407.4 10.5 %project_back.2 = (bf16[128,3072]{1,0:T(8,128)(2,1)}, bf16[128,1536]{1,0:T(8,128)(2,1)}, f32[8,1536]{1,0:T(8,128)}) custom-call(bf16[2,8,64,512]{3,2,1,0:T(8,128)(2,1)} %bitcast.107, f32[128,128]{1,0:T(8,128)} %get-tuple-element.115.cos, f32[128,128]{1,0:T(8,128)} %get-tuple-element.114.ahead, f32[128,128]{1,0:T(8,128)} %get-tuple-element.113.back, ...), custom_call_target="tpu_custom_call" | custom-call | tf_op jit(solution)/shard_map/project_back/pallas_call | solution.py:1021
  419.2 12.0 %collective-permute-done.1 = bf16[128,1536]{1,0:T(8,128)(2,1)S(1)} collective-permute-done((bf16[128,1536]{1,0:T(8,128)(2,1)}, bf16[128,1536]{1,0:T(8,128)(2,1)S(1)}, u32[]{:S(2)}, u32[]{:S(2)}) %collective-permute-start.1) | collective-permute-done | bytes 393248 | tf_op jit(solution)/shard_map/ppermute | solution.py:1115
  431.3 23.5 %mlp_back.3 = (bf16[128,4096]{1,0:T(8,128)(2,1)S(1)}, bf16[128,4096]{1,0:T(8,128)(2,1)S(1)}, f32[128,1536]{1,0:T(8,128)S(1)}, bf16[128,1536]{1,0:T(8,128)(2,1)S(...) custom-call(bf16[128,1536]{1,0:T(8,128)(2,1)S(1)} %broadcast_select_fusion.g_low.refs_4_, ...), custom_call_target="tpu_custom_call" | custom-call | tf_op jit(solution)/shard_map/mlp_back/pallas_call | solution.py:958
  455.6 48.2 %attend_back.3 = bf16[32,32,512]{2,1,0:T(8,128)(2,1)} custom-call(s32[1]{0:T(128)} %dynamic_slice.3.prefix, bf16[32,2,32,512]{3,2,1,0:T(8,128)(2,1)} %get-tuple-element.71.whole, bf16[32,32,256]{2,1,0:T(8,128)(2,1)} %bitcast.79), custom_call_target="tpu_custom_call" | custom-call | tf_op jit(solution)/shard_map/attend_back/pallas_call | solution.py:707
  503.9 10.6 %project_back.3 = (bf16[128,3072]{1,0:T(8,128)(2,1)}, bf16[128,1536]{1,0:T(8,128)(2,1)}, f32[8,1536]{1,0:T(8,128)}) custom-call(bf16[2,8,64,512]{3,2,1,0:T(8,128)(2,1)} %bitcast.106, f32[128,128]{1,0:T(8,128)} %get-tuple-element.115.cos, f32[128,128]{1,0:T(8,128)} %get-tuple-element.114.ahead, f32[128,128]{1,0:T(8,128)} %get-tuple-element.113.back, ...), custom_call_target="tpu_custom_call" | custom-call | tf_op jit(solution)/shard_map/project_back/pallas_call | solution.py:1021
  520.5 7.3 %pair_up.1 = (bf16[2,128,1536]{2,1,0:T(8,128)(2,1)S(1)}, bf16[2,128,1536]{2,1,0:T(8,128)(2,1)S(1)}, bf16[2,128,1536]{2,1,0:T(8,128)(2,1)S(1)}, bf16[2,128,4096]{...) custom-call(bf16[128,1536]{1,0:T(8,128)(2,1)S(1)} %copy-done.26, ...), custom_call_target="tpu_custom_call" | custom-call | tf_op jit(solution)/shard_map/pair_up/pallas_call | solution.py:745
  533.4 5.8 bitcast_convert_fusion.2
  539.2 4.5 bitcast_convert_fusion.1
  543.8 2.3 bitcast_convert_fusion.4
  546.1 3.6 bitcast_convert_fusion.3
  549.7 4.5 bitcast_convert_fusion
  555.1 155.0 %scatter_grads.1 = (f32[24,4096]{1,0:T(8,128)}, f32[24,4096]{1,0:T(8,128)}, f32[24,3072]{1,0:T(8,128)}, f32[24,1536]{1,0:T(8,128)}, f32[24,256]{1,0:T(8,128)}, /*index=5*/f32[64,1536]{1,0:T(8,128)}) custom-call(bf16[2,4,4,48,2048]{4,3,2,1,0:T(8,128)(2,1)} %bitcast.102, bf16[2,4,4,48,2048]{4,3,2,1,0:T(8,128)(2,1)} %bitcast.103, ...), custom_call_target="tpu_custom_call" | custom-call | tf_op jit(solution)/shard_map/scatter_grads/pallas_call | solution.py:400
  720.1 1.8 copy.51
  (107 shorter events, 41.3 us)
Async XLA Ops:
  171.9 46.1 %copy-start.2 = (bf16[2,64,1536]{2,1,0:T(8,128)(2,1)S(1)}, bf16[2,64,1536]{2,1,0:T(8,128)(2,1)}, u32[]{:S(2)}) copy-start(bf16[2,64,1536]{2,1,0:T(8,128)(2,1)} %param.12) | copy-start | bytes 1179652
  218.0 1.0 copy-start.22
  240.1 10.3 %collective-permute-start = (bf16[128,1536]{1,0:T(8,128)(2,1)S(1)}, bf16[128,1536]{1,0:T(8,128)(2,1)S(1)}, u32[]{:S(2)}, u32[]{:S(2)}) collective-permute-start(bf16[128,1536]{1,0:T(8,128)(2,1)S(1)} %get-tuple-element.67), channel_id=1, source_target_pairs={{0,64},{1,65},{2,66},{3,67},{4,68},{5,69},{6,70},{7,71},{8,72},{9,... | collective-permute-start | bytes 1179656 | tf_op jit(solution)/shard_map/ppermute | solution.py:1109
  251.2 52.5 %copy-start = (bf16[128,1536]{1,0:T(8,128)(2,1)S(1)}, bf16[128,1536]{1,0:T(8,128)(2,1)}, u32[]{:S(2)}) copy-start(bf16[128,1536]{1,0:T(8,128)(2,1)} %broadcast_select_fusion.1.x) | copy-start | bytes 1179652
  303.7 1.0 copy-start.23
  304.7 21.6 %copy-start.5 = (bf16[2,64,1536]{2,1,0:T(8,128)(2,1)S(1)}, bf16[2,64,1536]{2,1,0:T(8,128)(2,1)}, u32[]{:S(2)}) copy-start(bf16[2,64,1536]{2,1,0:T(8,128)(2,1)} %param.14) | copy-start | bytes 1179652
  324.2 1.3 copy-start.1
  326.3 24.9 %copy-start.9 = (bf16[128,4096]{1,0:T(8,128)(2,1)}, bf16[128,4096]{1,0:T(8,128)(2,1)S(1)}, u32[]{:S(2)}) copy-start(bf16[128,4096]{1,0:T(8,128)(2,1)S(1)} %get-tuple-element.84.refs_3_) | copy-start | bytes 3145732
  326.3 24.9 %copy-start.27 = (bf16[128,1536]{1,0:T(8,128)(2,1)}, bf16[128,1536]{1,0:T(8,128)(2,1)S(1)}, u32[]{:S(2)}) copy-start(bf16[128,1536]{1,0:T(8,128)(2,1)S(1)} %get-tuple-element.82.refs_1_) | copy-start | bytes 1179652
  417.9 13.3 %collective-permute-start.1 = (bf16[128,1536]{1,0:T(8,128)(2,1)}, bf16[128,1536]{1,0:T(8,128)(2,1)S(1)}, u32[]{:S(2)}, u32[]{:S(2)}) collective-permute-start(bf16[128,1536]{1,0:T(8,128)(2,1)} %get-tuple-element.77), channel_id=1, source_target_pairs={{64,0},{65,1},{66,2},{67,3},{68,4},{69,5},{70,6},{71,7},{72,8},{73... | collective-permute-start | bytes 1179656 | tf_op jit(solution)/shard_map/ppermute | solution.py:1115
  455.6 48.2 %copy-start.11 = (bf16[128,4096]{1,0:T(8,128)(2,1)}, bf16[128,4096]{1,0:T(8,128)(2,1)S(1)}, u32[]{:S(2)}) copy-start(bf16[128,4096]{1,0:T(8,128)(2,1)S(1)} %get-tuple-element.85.refs_5_) | copy-start | bytes 3145732
  455.6 48.2 %copy-start.13 = (bf16[128,4096]{1,0:T(8,128)(2,1)}, bf16[128,4096]{1,0:T(8,128)(2,1)S(1)}, u32[]{:S(2)}) copy-start(bf16[128,4096]{1,0:T(8,128)(2,1)S(1)} %get-tuple-element.86.refs_6_) | copy-start | bytes 3145732
  455.6 48.2 %copy-start.15 = (f32[128,1536]{1,0:T(8,128)}, f32[128,1536]{1,0:T(8,128)S(1)}, u32[]{:S(2)}) copy-start(f32[128,1536]{1,0:T(8,128)S(1)} %get-tuple-element.79.dmiddle) | copy-start | bytes 2359300
  455.6 58.9 %copy-start.31 = (bf16[128,1536]{1,0:T(8,128)(2,1)}, bf16[128,1536]{1,0:T(8,128)(2,1)S(1)}, u32[]{:S(2)}) copy-start(bf16[128,1536]{1,0:T(8,128)(2,1)S(1)} %get-tuple-element.87.refs_7_) | copy-start | bytes 1179652
  503.9 11.5 %copy-start.10 = (bf16[128,4096]{1,0:T(8,128)(2,1)S(1)}, bf16[128,4096]{1,0:T(8,128)(2,1)}, u32[]{:S(2)}) copy-start(bf16[128,4096]{1,0:T(8,128)(2,1)} %copy-done.9) | copy-start | bytes 3145732
  503.9 11.5 %copy-start.12 = (bf16[128,4096]{1,0:T(8,128)(2,1)S(1)}, bf16[128,4096]{1,0:T(8,128)(2,1)}, u32[]{:S(2)}) copy-start(bf16[128,4096]{1,0:T(8,128)(2,1)} %copy-done.11) | copy-start | bytes 3145732
  503.9 11.5 %copy-start.14 = (bf16[128,4096]{1,0:T(8,128)(2,1)S(1)}, bf16[128,4096]{1,0:T(8,128)(2,1)}, u32[]{:S(2)}) copy-start(bf16[128,4096]{1,0:T(8,128)(2,1)} %copy-done.13) | copy-start | bytes 3145732
  515.4 1.1 copy-start.21
  529.7 1.0 copy-start.8
  533.4 5.8 copy-start.7
  539.2 4.6 copy-start.19
  539.2 4.6 copy-start.34
  539.2 6.9 copy-start.4
  539.2 6.9 copy-start.17
  (13 other events, 11.6 us)

commit v3 on v2

v3 whole, which is shorter than its diff:
```python
import functools
import math

import jax
import jax.numpy as jnp
from jax import lax
from jax.experimental import pallas as pl
from jax.experimental.pallas import tpu as pltpu
from jax.sharding import PartitionSpec as P

HEADS = 16
KV_HEADS = 8
HEAD = 96
LANES = 128
HALF = HEAD // 2
PACKED = 4 * HEAD
EPS = 1e-05
ROPE_BASE = 100000.0
NEG = -1e30
PREFIX_MAX = 1024
SCALE = 1.0 / math.sqrt(HEAD)
MESH = pl.DeviceIdType.MESH
ANY = pl.BlockSpec(memory_space=pl.ANY)
VMEM = pl.BlockSpec(memory_space=pltpu.VMEM)
SMEM = pl.BlockSpec(memory_space=pltpu.SMEM)
MIB = 1 << 20

ARRAYS = ((24, 2048), (24, 2048), (24, 1536), (24, 768), (24, 128), (64, 768))
GATE, UP, QKV, OUT, GAIN, DOWN = range(6)
QKV_PIECES = (
    (QKV, 0, 512, "y", 1, -1),
    (QKV, 512, 256, "y", -1, -1),
    (QKV, 768, 512, "z", 1, -1),
    (QKV, 1280, 256, "z", -1, -1),
    (GAIN, 0, 128, "y", 1, -1),
)
GATHER_PIECES = QKV_PIECES + (
    (OUT, 0, 384, "y", -1, 1),
    (OUT, 384, 384, "z", -1, 1),
    (GATE, 0, 512, "y", 1, -1),
    (GATE, 512, 1536, "y", -1, None),
    (UP, 0, 512, "z", 1, -1),
    (UP, 512, 1536, "z", -1, None),
    (DOWN, 0, 384, "y", 1, 1),
    (DOWN, 384, 384, "z", 1, 1),
)
ATTN_PIECES = (
    (QKV, 0, 512, "y", 1, 1),
    (QKV, 512, 256, "y", -1, -1),
    (QKV, 768, 512, "z", 1, 1),
    (QKV, 1280, 256, "z", -1, -1),
    (GAIN, 0, 128, "y", -1, -1),
    (OUT, 0, 384, "y", -1, None),
    (OUT, 384, 384, "z", -1, None),
)
MLP_PIECES = (
    (GATE, 0, 1024, "y", 1, 1),
    (UP, 0, 1024, "z", 1, 1),
    (DOWN, 0, 384, "y", -1, -1),
    (DOWN, 384, 384, "z", -1, -1),
    (GATE, 1024, 512, "y", 1, None),
    (GATE, 1536, 512, "y", -1, None),
    (UP, 1024, 512, "z", 1, None),
    (UP, 1536, 512, "z", -1, None),
)
OTHER = {"y": "z", "z": "y"}


def f32dot(a, b, dims):
    return lax.dot_general(a, b, (dims, ((), ())), preferred_element_type=jnp.float32)


class Place:
    def __init__(self):
        self.s = lax.axis_index("section")
        self.d = lax.axis_index("dp")
        self.q = lax.axis_index("seq")
        self.y = lax.div(self.q, 8)
        self.z = lax.rem(lax.div(self.q, 2), 4)
        self.c = lax.rem(self.q, 2)

    def coord(self, axis):
        return self.y if axis == "y" else self.z

    def step(self, axis, by):
        y, z = self.y, self.z
        if axis == "y":
            y = lax.rem(y + by + 4, 4)
        else:
            z = lax.rem(z + by + 4, 4)
        return (self.s, self.d, y * 8 + z * 2 + self.c)

    def sibling(self):
        return (self.s, self.d, self.q + 1 - 2 * self.c)

    def dp_peer(self):
        return (self.s, 1 - self.d, self.q)


def meet(devices):
    barrier = pltpu.get_barrier_semaphore()
    for device in devices:
        pl.semaphore_signal(barrier, inc=1, device_id=device, device_id_type=MESH)
    pl.semaphore_wait(barrier, len(devices))


def remote(src, dst, send, recv, device):
    return pltpu.make_async_remote_copy(
        src_ref=src, dst_ref=dst, send_sem=send, recv_sem=recv, device_id=device, device_id_type=MESH
    )


EARLY = len(QKV_PIECES)


class Gather:
    def __init__(self, me, ins, outs, scratch):
        n = len(ARRAYS)
        self.me, self.ins, self.outs = me, ins, outs
        self.give, self.got, self.chip = scratch[:n], scratch[n : 2 * n], scratch[2 * n : 3 * n]
        self.first, self.local, self.over, self.ring_s, self.ring_r, self.sib_s, self.sib_r = scratch[3 * n :]
        self.dps = (me.d, 1 - me.d)
        self.one, self.two, self.held, self.overs, self.swaps = {}, {}, {}, {}, {}
        self.shares, self.pending = {}, []

    def neighbours(self):
        me = self.me
        near = [me.step(axis, by) for axis in "yz" for by in (1, -1)]
        return near + [me.dp_peer(), me.sibling()]

    def lanes(self, i):
        array, start, width = GATHER_PIECES[i][:3]
        return pl.ds(pl.multiple_of(self.me.c * ARRAYS[array][1] + start, LANES), width)

    def along(self, i, dp, by):
        array, _, _, a1 = GATHER_PIECES[i][:4]
        pos = lax.rem(self.me.coord(a1) + by + 4, 4)
        y, z = (pos, self.me.z) if a1 == "y" else (self.me.y, pos)
        return self.outs[array].at[dp, y, z, :, self.lanes(i)]

    def across(self, i, dp, by):
        array, _, _, a1 = GATHER_PIECES[i][:4]
        pos = lax.rem(self.me.coord(OTHER[a1]) + by + 4, 4)
        if a1 == "y":
            return self.outs[array].at[dp, pl.ds(0, 4), pos, :, self.lanes(i)]
        return self.outs[array].at[dp, pos, pl.ds(0, 4), :, self.lanes(i)]

    def send(self, i, block, k, src, dst, device):
        cp = remote(src, dst, self.ring_s.at[i, block, k], self.ring_r.at[i, block, k], device)
        cp.start()
        self.pending.append(cp)
        return cp

    def share(self, i, block, k, ref, src=None):
        src = ref if src is None else src
        cp = remote(src, ref, self.sib_s.at[i, block, k], self.sib_r.at[i, block, k], self.me.sibling())
        cp.start()
        self.pending.append(cp)
        self.shares.setdefault(i, []).append(cp)
        if block == 0 and (k == 0 or self.crosses(i)):
            cp = remote(src, ref, self.over.at[0, i, k], self.over.at[1, i, k], self.me.dp_peer())
            cp.start()
            self.pending.append(cp)
            self.overs[i, k] = cp

    def crosses(self, i):
        return GATHER_PIECES[i][5] is None

    def way(self, i, block):
        return GATHER_PIECES[i][4 + block]

    def both(self, pieces):
        return [i for i in pieces if not self.crosses(i)]

    def cross(self, pieces, spots):
        for k in spots:
            for i in pieces:
                if self.crosses(i):
                    way = self.way(i, 0)
                    by = (0, -way, way, 2, -way, way, 2)[k]
                    place = self.along if k < 4 else self.across
                    self.overs[i, k].wait_recv()
                    self.share(i, 1, k, place(i, self.dps[1], by))

    def swap(self):
        me = self.me
        for a, (_, width) in enumerate(ARRAYS):
            start = pl.multiple_of((1 - me.c) * width, LANES)
            self.give[a][...] = self.ins[a][:, pl.ds(start, width)].astype(jnp.float32)
            cp = remote(self.give[a], self.got[a], self.first.at[0, a], self.first.at[1, a], me.sibling())
            cp.start()
            self.swaps[a] = cp

    def join(self, a):
        me, width = self.me, ARRAYS[a][1]
        self.swaps[a].wait()
        start = pl.multiple_of(me.c * width, LANES)
        mine = self.ins[a][:, pl.ds(start, width)].astype(jnp.float32)
        theirs = self.got[a][...]
        low = jnp.where(me.c == 0, mine, theirs)
        high = jnp.where(me.c == 0, theirs, mine)
        self.chip[a][...] = jnp.concatenate([low, high], axis=0).astype(jnp.bfloat16)

    def start(self, pieces):
        me = self.me
        for i in pieces:
            array, start, width, a1 = GATHER_PIECES[i][:4]
            src = self.chip[array].at[:, pl.ds(start, width)]
            here = self.along(i, me.d, 0)
            self.one[i, 0, 1] = self.send(i, 0, 0, src, here, me.step(a1, 1))
            self.one[i, 0, -1] = self.send(i, 0, 1, src, here, me.step(a1, -1))
            cp = pltpu.make_async_copy(src, here, self.local.at[i])
            cp.start()
            self.held[i] = cp
            self.share(i, 0, 0, here, src)

    def start_other(self, pieces):
        me = self.me
        for i in self.both(pieces):
            a1 = GATHER_PIECES[i][3]
            self.overs[i, 0].wait_recv()
            here = self.along(i, self.dps[1], 0)
            self.one[i, 1, 1] = self.send(i, 1, 0, here, here, me.step(a1, 1))
            self.one[i, 1, -1] = self.send(i, 1, 1, here, here, me.step(a1, -1))
            self.share(i, 1, 0, here)

    def hop(self, pieces, block, second):
        kept, place, base = (self.two, self.across, 3) if second else (self.one, self.along, 0)
        dp = self.dps[block]
        pieces = self.both(pieces) if block else pieces
        for i in pieces:
            axis, way = GATHER_PIECES[i][3], self.way(i, block)
            axis = OTHER[axis] if second else axis
            kept[i, block, way].wait_recv()
            came = place(i, dp, -way)
            kept[i, block, 0] = self.send(i, block, base + 2, came, came, self.me.step(axis, way))
            self.share(i, block, base + 1, came)
        for i in pieces:
            way = self.way(i, block)
            kept[i, block, -way].wait_recv()
            self.share(i, block, base + 2, place(i, dp, way))

    def turn(self, pieces, block):
        dp = self.dps[block]
        for i in self.both(pieces) if block else pieces:
            a2 = OTHER[GATHER_PIECES[i][3]]
            self.one[i, block, 0].wait_recv()
            self.share(i, block, 3, self.along(i, dp, 2))
            if block == 0:
                self.held[i].wait()
            here = self.across(i, dp, 0)
            self.two[i, block, 1] = self.send(i, block, 3, here, here, self.me.step(a2, 1))
            self.two[i, block, -1] = self.send(i, block, 4, here, here, self.me.step(a2, -1))

    def finish(self, pieces, block):
        for i in self.both(pieces) if block else pieces:
            self.two[i, block, 0].wait_recv()
            self.share(i, block, 6, self.across(i, self.dps[block], 2))

    def shown(self, pieces):
        for i in pieces:
            for cp in self.shares[i]:
                cp.wait_recv()

    def drain(self):
        for cp in self.pending:
            cp.wait_send()


GATHER_SCRATCH = (
    [pltpu.VMEM(shape, jnp.float32) for shape in ARRAYS]
    + [pltpu.VMEM(shape, jnp.float32) for shape in ARRAYS]
    + [pltpu.VMEM((2 * rows, width), jnp.bfloat16) for rows, width in ARRAYS]
    + [
        pltpu.SemaphoreType.DMA((2, len(ARRAYS))),
        pltpu.SemaphoreType.DMA((len(GATHER_PIECES),)),
        pltpu.SemaphoreType.DMA((2, len(GATHER_PIECES), 7)),
        pltpu.SemaphoreType.DMA((len(GATHER_PIECES), 2, 6)),
        pltpu.SemaphoreType.DMA((len(GATHER_PIECES), 2, 6)),
        pltpu.SemaphoreType.DMA((len(GATHER_PIECES), 2, 7)),
        pltpu.SemaphoreType.DMA((len(GATHER_PIECES), 2, 7)),
    ]
)


def gather_steps(gather):
    early = range(EARLY)
    late = range(EARLY, len(GATHER_PIECES))
    gather.swap()
    for a in (QKV, GAIN):
        gather.join(a)
    gather.start(early)
    for a in (OUT, GATE, UP, DOWN):
        gather.join(a)
    gather.start(late)
    gather.hop(early, 0, False)
    gather.turn(early, 0)
    gather.start_other(early)
    gather.hop(late, 0, False)
    gather.hop(early, 1, False)
    gather.turn(early, 1)
    gather.turn(late, 0)
    gather.start_other(late)
    gather.hop(early, 0, True)
    gather.hop(late, 1, False)
    gather.hop(early, 1, True)
    gather.finish(early, 0)
    gather.hop(late, 0, True)
    gather.turn(late, 1)
    gather.finish(early, 1)
    gather.shown(early)
    yield
    gather.finish(late, 0)
    gather.cross(late, range(4))
    gather.hop(late, 1, True)
    yield
    gather.finish(late, 1)
    gather.cross(late, range(4, 7))
    gather.shown(late)
    gather.drain()


def add_into(total, term):
    chunks = total.shape[1] // 16

    def step(k, carry):
        j = lax.div(k, chunks)
        rows = pl.ds(pl.multiple_of(lax.rem(k, chunks) * 16, 16), 16)
        both = total[j, rows, :].astype(jnp.float32) + term[j, rows, :].astype(jnp.float32)
        total[j, rows, :] = both.astype(jnp.bfloat16)
        return carry

    lax.fori_loop(0, total.shape[0] * chunks, step, 0)


def add_two(total, left, right):
    chunks = total.shape[1] // 16

    def step(k, carry):
        j = lax.div(k, chunks)
        rows = pl.ds(pl.multiple_of(lax.rem(k, chunks) * 16, 16), 16)
        parts = [ref[j, rows, :].astype(jnp.float32) for ref in (total, left, right)]
        total[j, rows, :] = (parts[0] + (parts[1] + parts[2])).astype(jnp.bfloat16)
        return carry

    lax.fori_loop(0, total.shape[0] * chunks, step, 0)


class Scatter:
    def __init__(self, me, pieces, arrays, ins, outs, scratch):
        n, m = len(pieces), len(arrays)
        self.me, self.pieces, self.ins, self.outs = me, pieces, ins, outs
        self.at = {a: k for k, a in enumerate(arrays)}
        names = ("near", "far", "last", "mid", "own", "near1", "far1", "last1", "sent", "came")
        for k, name in enumerate(names):
            setattr(self, name, scratch[k * n : (k + 1) * n])
        rest = scratch[len(names) * n :]
        whole = [i for i in range(n) if self.crosses(i)]
        self.ours, rest = dict(zip(whole, rest)), rest[len(whole) :]
        self.theirs, rest = dict(zip(whole, rest)), rest[len(whole) :]
        self.total, rest = rest[:m], rest[m:]
        self.load, self.ring_s, self.ring_r, self.over, self.fin, self.keep = rest
        self.dps = (1 - me.d, me.d)
        self.loads, self.one, self.two, self.overs, self.pending = {}, {}, {}, {}, []

    def neighbours(self):
        me = self.me
        near = [me.step(axis, by) for axis in "yz" for by in (1, -1)]
        return near + [me.dp_peer(), me.sibling()]

    def crosses(self, i):
        return self.pieces[i][5] is None

    def way(self, i, block):
        return self.pieces[i][5 - block]

    def of(self, block, crossing=None):
        picked = [i for i in range(len(self.pieces)) if block or not self.crosses(i)]
        return [i for i in picked if crossing is None or self.crosses(i) == crossing]

    def slot(self, i, block):
        return 0 if self.crosses(i) else block

    def column(self, i, block, by):
        array, start, width, a1 = self.pieces[i][:4]
        pos = lax.rem(self.me.coord(OTHER[a1]) + by + 4, 4)
        ref, dp, lanes = self.ins[self.at[array]], self.dps[block], pl.ds(start, width)
        if a1 == "z":
            return ref.at[dp, pos, pl.ds(0, 4), :, lanes]
        return ref.at[dp, pl.ds(0, 4), pos, :, lanes]

    def send(self, i, block, k, src, dst, device):
        cp = remote(src, dst, self.ring_s.at[i, block, k], self.ring_r.at[i, block, k], device)
        cp.start()
        self.pending.append(cp)
        return cp

    def start_crossing(self):
        for k in range(4):
            for i in self.of(1, True):
                way = self.way(i, 1)
                by = (2 * way, -way, way, 0)[k]
                there = self.theirs[i].at[k]
                cp = remote(
                    self.column(i, 0, by), there, self.over.at[0, i, k], self.over.at[1, i, k], self.me.dp_peer()
                )
                cp.start()
                self.pending.append(cp)
                self.overs[i, k] = cp
                cp = pltpu.make_async_copy(self.column(i, 1, by), self.ours[i].at[k], self.load.at[k, i, 0])
                cp.start()
                self.loads[i, k] = cp

    def add_crossed(self, i, k):
        self.overs[i, k].wait_recv()
        self.loads[i, k].wait()
        add_into(self.ours[i].at[k], self.theirs[i].at[k])

    def start(self, block):
        for i in self.of(block, False):
            way = self.way(i, block)
            there = self.me.step(OTHER[self.pieces[i][3]], way)
            self.one[i, block, 0] = self.send(
                i, block, 0, self.column(i, block, 2 * way), self.near[i].at[block], there
            )
        for i in self.of(block, False):
            way = self.way(i, block)
            there = self.me.step(OTHER[self.pieces[i][3]], -way)
            self.one[i, block, 1] = self.send(
                i, block, 1, self.column(i, block, -way), self.far[i].at[block], there
            )
        for i in self.of(block, False):
            way = self.way(i, block)
            for k, (by, ref) in enumerate(((way, self.mid[i]), (0, self.own[i]))):
                cp = pltpu.make_async_copy(self.column(i, block, by), ref.at[block], self.load.at[k, i, block])
                cp.start()
                self.loads[i, block, k] = cp

    def start_crossed(self):
        for k in range(2):
            for i in self.of(1, True):
                way = self.way(i, 1)
                self.add_crossed(i, k)
                there = self.me.step(OTHER[self.pieces[i][3]], -way if k else way)
                dst = (self.far if k else self.near)[i].at[0]
                self.one[i, 1, k] = self.send(i, 1, k, self.ours[i].at[k], dst, there)

    def hop(self, block, crossing):
        for i in self.of(block, crossing):
            slot = self.slot(i, block)
            self.one[i, block, 0].wait_recv()
            if crossing:
                self.add_crossed(i, 2)
                mid = self.ours[i].at[2]
            else:
                self.loads[i, block, 0].wait()
                mid = self.mid[i].at[block]
            near = self.near[i].at[slot]
            add_into(near, mid)
            there = self.me.step(OTHER[self.pieces[i][3]], self.way(i, block))
            self.one[i, block, 2] = self.send(i, block, 2, near, self.last[i].at[slot], there)

    def own_of(self, i, block):
        return self.ours[i].at[3] if self.crosses(i) else self.own[i].at[block]

    def turn(self, block, crossing):
        me = self.me
        for i in self.of(block, crossing):
            slot, a1, way = self.slot(i, block), self.pieces[i][3], self.way(i, block)
            if crossing:
                self.add_crossed(i, 3)
            else:
                self.loads[i, block, 1].wait()
            self.one[i, block, 1].wait_recv()
            self.one[i, block, 2].wait_recv()
            own = self.own_of(i, block)
            add_two(own, self.far[i].at[slot], self.last[i].at[slot])
            pos = me.coord(a1)
            self.two[i, block, 0] = self.send(
                i, block, 3, own.at[lax.rem(pos + 2, 4)], self.near1[i].at[slot], me.step(a1, way)
            )
            self.two[i, block, 1] = self.send(
                i, block, 4, own.at[lax.rem(pos - way + 4, 4)], self.far1[i].at[slot], me.step(a1, -way)
            )

    def hop_two(self, block, crossing):
        me = self.me
        for i in self.of(block, crossing):
            slot, a1, way = self.slot(i, block), self.pieces[i][3], self.way(i, block)
            self.two[i, block, 0].wait_recv()
            place = lax.rem(me.coord(a1) + way + 4, 4)
            add_into(self.near1[i].at[pl.ds(slot, 1)], self.own_of(i, block).at[pl.ds(place, 1)])
            self.two[i, block, 2] = self.send(
                i, block, 5, self.near1[i].at[slot], self.last1[i].at[slot], me.step(a1, way)
            )

    def finish(self, block, crossing):
        me = self.me
        for i in self.of(block, crossing):
            array, start, width, a1 = self.pieces[i][:4]
            slot, pos = self.slot(i, block), me.coord(a1)
            self.two[i, block, 1].wait_recv()
            self.two[i, block, 2].wait_recv()
            if block == 1 and not crossing:
                self.overs[i, 0].wait_recv()
            far1, last1, sent, came = (ref[i] for ref in (self.far1, self.last1, self.sent, self.came))
            own = self.own_of(i, block)
            total = self.total[self.at[array]]

            def step(k, carry):
                part = pl.ds(pl.multiple_of(k * 16, 16), 16)
                both = far1[slot, part, :].astype(jnp.float32) + last1[slot, part, :].astype(jnp.float32)
                both = both + own[pos, part, :].astype(jnp.float32)
                if block == 0:
                    sent[part, :] = both.astype(jnp.bfloat16)
                elif crossing:
                    total[part, start : start + width] = both
                else:
                    total[part, start : start + width] = both + came[part, :].astype(jnp.float32)
                return carry

            lax.fori_loop(0, 2 * ARRAYS[array][0] // 16, step, 0)
            if block == 0:
                cp = remote(sent, came, self.over.at[0, i, 0], self.over.at[1, i, 0], me.dp_peer())
                cp.start()
                self.pending.append(cp)
                self.overs[i, 0] = cp

    def hand_out(self):
        me = self.me
        copies = []
        for array, k in self.at.items():
            rows, width = ARRAYS[array]
            mine = self.total[k].at[pl.ds(pl.multiple_of(me.c * rows, 8), rows)]
            theirs = self.total[k].at[pl.ds(pl.multiple_of((1 - me.c) * rows, 8), rows)]
            place = self.outs[k].at[:, pl.ds(pl.multiple_of(me.c * width, LANES), width)]
            copies.append(pltpu.make_async_copy(mine, place, self.keep.at[k]))
            copies.append(remote(theirs, place, self.fin.at[0, k], self.fin.at[1, k], me.sibling()))
        for cp in copies:
            cp.start()
        for cp in copies:
            cp.wait()
        for cp in self.pending:
            cp.wait_send()


def scatter_steps(scatter):
    scatter.start_crossing()
    scatter.start(0)
    scatter.start(1)
    yield
    scatter.hop(0, False)
    scatter.start_crossed()
    scatter.hop(1, False)
    scatter.turn(0, False)
    scatter.hop_two(0, False)
    scatter.hop(1, True)
    scatter.finish(0, False)
    scatter.turn(1, False)
    scatter.hop_two(1, False)
    scatter.turn(1, True)
    scatter.finish(1, False)
    scatter.hop_two(1, True)
    scatter.finish(1, True)
    scatter.hand_out()


def scatter_scratch(pieces, arrays):
    n, m = len(pieces), len(arrays)
    bf16 = jnp.bfloat16
    shapes = [(2 * ARRAYS[piece[0]][0], piece[2]) for piece in pieces]
    crossing = [piece[5] is None for piece in pieces]

    def buffers(count, *lead):
        return [pltpu.VMEM((1 if one else 2, *lead, *shape), bf16) for _ in range(count) for shape, one in zip(shapes, crossing)]

    held = [
        pltpu.VMEM((1, 16, LANES) if one else (2, 4, *shape), bf16)
        for _ in range(2)
        for shape, one in zip(shapes, crossing)
    ]
    whole = [pltpu.VMEM((4, 4, *shape), bf16) for _ in range(2) for shape, one in zip(shapes, crossing) if one]
    return (
        buffers(3, 4)
        + held
        + buffers(3)
        + [pltpu.VMEM((16, LANES) if one else shape, bf16) for _ in range(2) for shape, one in zip(shapes, crossing)]
        + whole
        + [pltpu.VMEM((2 * ARRAYS[a][0], ARRAYS[a][1]), jnp.float32) for a in arrays]
        + [
            pltpu.SemaphoreType.DMA((4, n, 2)),
            pltpu.SemaphoreType.DMA((n, 2, 6)),
            pltpu.SemaphoreType.DMA((n, 2, 6)),
            pltpu.SemaphoreType.DMA((2, n, 4)),
            pltpu.SemaphoreType.DMA((2, m)),
            pltpu.SemaphoreType.DMA((m,)),
        ]
    )


def scatter_shapes(arrays):
    return [jax.ShapeDtypeStruct((ARRAYS[a][0], 2 * ARRAYS[a][1]), jnp.float32) for a in arrays]


def in_shards(parts, arrays):
    return [part.reshape(2, 4, 4, 2 * ARRAYS[a][0], ARRAYS[a][1]) for part, a in zip(parts, arrays, strict=True)]


ATTN_ARRAYS = (QKV, OUT, GAIN)
MLP_ARRAYS = (GATE, UP, DOWN)


def scatter_kernel(pieces, arrays, *refs):
    m = len(arrays)
    me = Place()
    scatter = Scatter(me, pieces, arrays, refs[:m], refs[m : 2 * m], refs[2 * m :])
    meet(scatter.neighbours())
    for _ in scatter_steps(scatter):
        pass


def scatter_attn(parts):
    pieces, arrays = ATTN_PIECES, ATTN_ARRAYS
    return pl.pallas_call(
        functools.partial(scatter_kernel, pieces, arrays),
        out_shape=scatter_shapes(arrays),
        in_specs=[ANY] * len(arrays),
        out_specs=[ANY] * len(arrays),
        scratch_shapes=scatter_scratch(pieces, arrays),
        compiler_params=pltpu.CompilerParams(
            collective_id=2, has_side_effects=True, vmem_limit_bytes=56 * MIB
        ),
        name="scatter_attn",
    )(*in_shards(parts, arrays))


ORIGINS = 32
BLOCK = 8
BLOCKS = ORIGINS // BLOCK


def meet_plane(me, others=()):
    barrier = pltpu.get_barrier_semaphore()
    for device in others:
        pl.semaphore_signal(barrier, inc=1, device_id=device, device_id_type=MESH)

    def greet(k, carry):
        to = lax.rem(me.q + k, ORIGINS)
        pl.semaphore_signal(barrier, inc=1, device_id=(me.s, me.d, to), device_id_type=MESH)
        return carry

    lax.fori_loop(1, ORIGINS, greet, 0)
    pl.semaphore_wait(barrier, ORIGINS - 1 + len(others))


class Exchange:
    def __init__(self, me, src, dst_of, sems):
        self.me, self.src, self.dst_of, self.sems = me, src, dst_of, sems

    def copy(self, origin, to):
        me, (send, recv, _) = self.me, self.sems
        peer = to + origin - me.q
        return remote(
            self.src.at[to], self.dst_of(origin, to), send.at[to], recv.at[origin], (me.s, me.d, peer)
        )

    def own(self):
        q = self.me.q
        return pltpu.make_async_copy(self.src.at[q], self.dst_of(q, q), self.sems[2].at[0])

    def start_all(self):
        self.own().start()

        def step(k, carry):
            by = (k + 1) // 2
            by = jnp.where(lax.rem(k, 2) == 1, by, ORIGINS - by)
            self.copy(self.me.q, lax.rem(self.me.q + by, ORIGINS)).start()
            return carry

        lax.fori_loop(1, ORIGINS, step, 0)

    def start_one(self, to):
        @pl.when(to == self.me.q)
        def _():
            self.own().start()

        @pl.when(to != self.me.q)
        def _():
            self.copy(self.me.q, to).start()

    def start(self, block):
        def step(k, carry):
            self.start_one(block * BLOCK + lax.rem(self.me.q + k, BLOCK))
            return carry

        lax.fori_loop(0, BLOCK, step, 0)

    def arrived(self, first, count):
        def step(k, carry):
            origin = first + k

            @pl.when(origin == self.me.q)
            def _():
                self.own().wait()

            @pl.when(origin != self.me.q)
            def _():
                self.copy(origin, self.me.q).wait_recv()

            return carry

        lax.fori_loop(0, count, step, 0)

    def sent(self):
        def step(k, carry):
            self.copy(self.me.q, lax.rem(self.me.q + k, ORIGINS)).wait_send()
            return carry

        lax.fori_loop(1, ORIGINS, step, 0)


EXCHANGE_SEMS = [
    pltpu.SemaphoreType.DMA((ORIGINS,)),
    pltpu.SemaphoreType.DMA((ORIGINS,)),
    pltpu.SemaphoreType.DMA((1,)),
]


def block_mask(block, keys, core, prefix_len):
    rows = BLOCK * 32
    row = lax.broadcasted_iota(jnp.int32, (rows, keys), 0)
    key = lax.broadcasted_iota(jnp.int32, (rows, keys), 1)
    pos = block * BLOCK * 64 + 64 * (row // 32) + 32 * core + row % 32
    return (key <= pos) | (key < prefix_len)


def keys_of(block):
    return max((block + 1) * BLOCK * 64, PREFIX_MAX)


def group(block):
    return pl.ds(block * BLOCK, BLOCK)


def split_four(y):
    inside = lax.broadcasted_iota(jnp.int32, (y.shape[0], LANES), 1) < HEAD
    heads = [y[:, :LANES]] + [pltpu.roll(y, PACKED - HEAD * h, axis=1)[:, :LANES] for h in (1, 2, 3)]
    return [jnp.where(inside, z, 0.0) for z in heads]


def pack_four(heads):
    zero = jnp.zeros((heads[0].shape[0], 2 * LANES), jnp.float32)
    wide = [jnp.concatenate([z, zero], axis=1) for z in heads]
    total = wide[0]
    for h in (1, 2, 3):
        total = total + pltpu.roll(wide[h], HEAD * h, axis=1)
    return total


def turn_heads(z, cos, ahead, back):
    return z * cos + pltpu.roll(z, PACKED - HALF, axis=1) * ahead + pltpu.roll(z, HALF, axis=1) * back


def project_and_send(x, gain, w, tables, normed, bundle, held, held_sem, coming):
    cos, ahead, back = tables
    tokens = x.shape[0]

    def fetch(g, slot):
        lanes = pl.ds(pl.multiple_of(g * PACKED, LANES), PACKED)
        return pltpu.make_async_copy(w.at[:, :, :, :, lanes], held.at[slot], held_sem.at[slot])

    begin = lax.rem(coming.me.q // 2, KV_HEADS)
    fetch(begin, 0).start()
    hidden = x[...].astype(jnp.float32)
    r1 = lax.rsqrt(jnp.mean(hidden * hidden, axis=-1, keepdims=True) + EPS)
    normed[...] = (hidden * r1 * gain).astype(jnp.bfloat16)

    def step(k, carry):
        slot = lax.rem(k, 2)
        g = lax.rem(begin + k, KV_HEADS)
        fetch(g, slot).wait()

        @pl.when(k + 1 < KV_HEADS)
        def _():
            fetch(lax.rem(g + 1, KV_HEADS), 1 - slot).start()

        y = f32dot(normed[...], held[slot].reshape(x.shape[1], PACKED), ((1,), (0,)))
        z = turn_heads(y, cos[...], ahead[...], back[...]).astype(jnp.bfloat16)
        for part in range(4):
            to = (part // 2) * 16 + g * 2 + part % 2
            bundle[to] = z[part * 32 : (part + 1) * 32]
            coming.start_one(to)
        return carry

    lax.fori_loop(0, KV_HEADS, step, 0)


PROJECT_SCRATCH = [
    pltpu.VMEM((ORIGINS, 32, PACKED), jnp.bfloat16),
    pltpu.VMEM((2, 2, 4, 4, 48, PACKED), jnp.bfloat16),
    pltpu.SemaphoreType.DMA((2,)),
]


class Attend:
    def __init__(self, me, prefix, bundle, dst, keys, values, queries, scratch):
        self.me, self.prefix, self.keys, self.values, self.queries = me, prefix, keys, values, queries
        self.whole, self.out = scratch[:2]
        self.sib = scratch[8]
        self.coming = Exchange(
            me, bundle, lambda origin, to: self.whole.at[origin, lax.rem(to, 2)], scratch[2:5]
        )
        self.going = Exchange(me, self.out, lambda origin, to: dst.at[origin], scratch[5:8])
        self.shares = []

    def receive(self):
        for block in range(BLOCKS):
            self.coming.arrived(block * BLOCK, BLOCK)
            mine = self.whole.at[group(block), self.me.c, :, pl.ds(0, 2 * LANES)]
            cp = remote(mine, mine, self.sib.at[0, block], self.sib.at[1, block], self.me.sibling())
            cp.start()
            self.shares.append(cp)
            y = self.whole[group(block), self.me.c].reshape(BLOCK * 32, PACKED).astype(jnp.float32)
            heads = split_four(y)
            for h in range(2):
                self.queries[h, pl.ds(block * BLOCK * 32, BLOCK * 32), :] = heads[2 + h].astype(jnp.bfloat16)

    def unpack(self, block):
        self.shares[block].wait_recv()
        rows = BLOCK * 64
        both = self.whole[group(block), :, :, 0 : 2 * LANES].reshape(rows, 2 * LANES)
        at = pl.ds(block * rows, rows)
        self.keys[at, :] = both[:, :LANES]
        turned = pltpu.roll(both.astype(jnp.float32), 2 * LANES - HEAD, axis=1)
        self.values[at, :] = turned[:, :LANES].astype(jnp.bfloat16)

    def compute(self):
        ready = 0
        for block in range(BLOCKS):
            count = keys_of(block)
            while ready * BLOCK * 64 < count:
                self.unpack(ready)
                ready += 1
            k = self.keys[pl.ds(0, count), :]
            v = self.values[pl.ds(0, count), :]
            allowed = block_mask(block, count, self.me.c, self.prefix[0])
            quarters = []
            for h in range(2):
                q = self.queries[h, pl.ds(block * BLOCK * 32, BLOCK * 32), :]
                s = jnp.where(allowed, f32dot(q, k, ((1,), (1,))) * SCALE, NEG)
                top = jnp.max(s, axis=-1, keepdims=True)
                e = jnp.exp(s - top)
                p = (e * (1.0 / jnp.sum(e, axis=-1, keepdims=True))).astype(jnp.bfloat16)
                quarters.append(f32dot(p, v, ((1,), (0,))).reshape(BLOCK, 32, LANES))
            inside = lax.broadcasted_iota(jnp.int32, (BLOCK * 16, LANES), 1) < HEAD
            heads = [
                jnp.where(inside, o[:, r * 16 : r * 16 + 16].reshape(BLOCK * 16, LANES), 0.0)
                for r in range(2)
                for o in quarters
            ]
            packed = pack_four(heads).astype(jnp.bfloat16)
            self.out[group(block)] = packed.reshape(BLOCK, 16, PACKED)
        self.going.start_all()

    def drain(self):
        self.going.arrived(0, ORIGINS)
        self.coming.sent()
        self.going.sent()
        for cp in self.shares:
            cp.wait_send()


ATTEND_SCRATCH = [
    pltpu.VMEM((ORIGINS, 2, 32, PACKED), jnp.bfloat16),
    pltpu.VMEM((ORIGINS, 16, PACKED), jnp.bfloat16),
    *EXCHANGE_SEMS,
    *EXCHANGE_SEMS,
    pltpu.SemaphoreType.DMA((2, BLOCKS)),
]
KEPT = [
    ((ORIGINS * 64, LANES), jnp.bfloat16),
    ((ORIGINS * 64, LANES), jnp.bfloat16),
    ((2, ORIGINS * 32, LANES), jnp.bfloat16),
]
ATTENDED = ((ORIGINS, 16, PACKED), jnp.bfloat16)


def attend_kernel(prefix, x, gain, cos, ahead, back, w, normed, keys, values, queries, dst, *scratch):
    me = Place()
    meet_plane(me)
    bundle, held, held_sem = scratch[:3]
    attention = Attend(me, prefix, bundle, dst, keys, values, queries, scratch[3:])
    project_and_send(
        x, gain[0:1, :], w, (cos, ahead, back), normed, bundle, held, held_sem, attention.coming
    )
    attention.receive()
    attention.compute()
    attention.drain()


def attend(prefix, x, gain, tables, w):
    return pl.pallas_call(
        attend_kernel,
        out_shape=[jax.ShapeDtypeStruct(x.shape, jnp.bfloat16)]
        + [jax.ShapeDtypeStruct(*kept) for kept in KEPT]
        + [jax.ShapeDtypeStruct(*ATTENDED)],
        in_specs=[SMEM] + [VMEM] * 5 + [ANY],
        out_specs=[VMEM] * 5,
        scratch_shapes=PROJECT_SCRATCH + ATTEND_SCRATCH,
        compiler_params=pltpu.CompilerParams(
            collective_id=3, has_side_effects=True, vmem_limit_bytes=60 * MIB
        ),
        name="attend",
    )(prefix, x, gain, *tables, w)


def enter_kernel(prefix, x, cos, ahead, back, *refs):
    n = len(ARRAYS)
    ins, outs = refs[:n], refs[n : 2 * n]
    gains, dst = refs[2 * n : 2 * n + 2]
    normed, keys, values, queries, column, column_sem = refs[2 * n + 2 : 2 * n + 8]
    rest = refs[2 * n + 8 :]
    bundle, held, held_sem = rest[:3]
    k = 3 + len(ATTEND_SCRATCH)
    me = Place()
    attention = Attend(me, prefix, bundle, dst, keys, values, queries, rest[3:k])
    gather = Gather(me, ins, outs, rest[k:])
    meet_plane(me, [me.dp_peer()])
    steps = gather_steps(gather)
    next(steps)
    cp = pltpu.make_async_copy(outs[GAIN], column, column_sem.at[0])
    cp.start()
    cp.wait()
    first = (lax.broadcasted_iota(jnp.int32, (8, LANES), 1) == 0).astype(jnp.bfloat16)
    for half in range(2):
        one = column[:, :, :, :, half * LANES : (half + 1) * LANES].reshape(x.shape[1], LANES)
        gains[half] = f32dot(first, one, ((1,), (1,)))
    project_and_send(
        x, gains[0, 0:1, :], outs[QKV], (cos, ahead, back), normed, bundle, held, held_sem, attention.coming
    )
    attention.receive()
    next(steps)
    attention.compute()
    for _ in steps:
        pass
    attention.drain()


def enter(prefix, x, tables, shards):
    n = len(ARRAYS)
    width = x.shape[1]
    return pl.pallas_call(
        enter_kernel,
        out_shape=[jax.ShapeDtypeStruct((2, 4, 4, 2 * r, 2 * w), jnp.bfloat16) for r, w in ARRAYS]
        + [jax.ShapeDtypeStruct((2, 8, width), jnp.float32), jax.ShapeDtypeStruct(*ATTENDED)],
        in_specs=[SMEM] + [VMEM] * (4 + n),
        out_specs=[ANY] * n + [VMEM] * 2,
        scratch_shapes=[pltpu.VMEM(x.shape, jnp.bfloat16)]
        + [pltpu.VMEM(*kept) for kept in KEPT]
        + [pltpu.VMEM((2, 4, 4, 48, 2 * LANES), jnp.bfloat16), pltpu.SemaphoreType.DMA((1,))]
        + PROJECT_SCRATCH
        + ATTEND_SCRATCH
        + GATHER_SCRATCH,
        compiler_params=pltpu.CompilerParams(
            collective_id=1, has_side_effects=True, vmem_limit_bytes=60 * MIB
        ),
        name="enter",
    )(prefix, x, *tables, *shards)


class AttendBack:
    def __init__(self, me, prefix, keys, values, queries, src, dst, scratch):
        self.me, self.prefix, self.keys, self.values, self.queries = me, prefix, keys, values, queries
        self.datt, self.acc, self.theirs, self.dq, self.bundle = scratch[:5]
        self.sib = scratch[11]
        self.coming = Exchange(me, src, lambda origin, to: self.datt.at[origin], scratch[5:8])
        self.going = Exchange(me, self.bundle, lambda origin, to: dst.at[origin], scratch[8:11])
        self.shares = {}

    def share(self, block):
        cp = remote(
            self.acc.at[group(block), 1 - self.me.c],
            self.theirs.at[group(block)],
            self.sib.at[0, block],
            self.sib.at[1, block],
            self.me.sibling(),
        )
        cp.start()
        self.shares[block] = cp

    def finish(self, block):
        self.shares[block].wait_recv()
        rows = BLOCK * 32
        both = self.acc[group(block), self.me.c] + self.theirs[group(block)]
        both = both.reshape(rows, 2 * LANES)
        dq = self.dq[group(block)].reshape(rows, 2 * LANES)
        heads = [both[:, :LANES] * SCALE, both[:, LANES:], dq[:, :LANES], dq[:, LANES:]]
        self.bundle[group(block)] = pack_four(heads).astype(jnp.bfloat16).reshape(BLOCK, 32, PACKED)
        self.going.start(block)

    def block(self, block):
        count = keys_of(block)
        spread = pl.ds(0, count // 64)
        k = self.keys[pl.ds(0, count), :]
        v = self.values[pl.ds(0, count), :]
        allowed = block_mask(block, count, self.me.c, self.prefix[0])
        quarters = split_four(self.datt[group(block)].reshape(BLOCK * 16, PACKED).astype(jnp.float32))
        inside = lax.broadcasted_iota(jnp.int32, (BLOCK * 32, LANES), 1) < HEAD
        for h in range(2):
            q = self.queries[h, pl.ds(block * BLOCK * 32, BLOCK * 32), :]
            g = jnp.concatenate([quarters[2 * r + h].reshape(BLOCK, 16, LANES) for r in range(2)], axis=1)
            g = g.reshape(BLOCK * 32, LANES).astype(jnp.bfloat16)
            s = jnp.where(allowed, f32dot(q, k, ((1,), (1,))) * SCALE, NEG)
            top = jnp.max(s, axis=-1, keepdims=True)
            e = jnp.exp(s - top)
            p = e * (1.0 / jnp.sum(e, axis=-1, keepdims=True))
            dp = f32dot(g, v, ((1,), (1,)))
            delta = jnp.sum(p * dp, axis=-1, keepdims=True)
            ds = (p * (dp - delta)).astype(jnp.bfloat16)
            dq = jnp.where(inside, f32dot(ds, k, ((1,), (0,))) * SCALE, 0.0)
            self.dq[group(block), :, LANES * h : LANES * (h + 1)] = dq.reshape(BLOCK, 32, LANES)
            dk = f32dot(ds, q, ((0,), (0,))).reshape(count // 64, 2, 32, LANES)
            dv = f32dot(p.astype(jnp.bfloat16), g, ((0,), (0,))).reshape(count // 64, 2, 32, LANES)
            if block == BLOCKS - 1 and h == 0:
                self.acc[spread, :, :, 0:LANES] = dk
                self.acc[spread, :, :, LANES : 2 * LANES] = dv
            else:
                self.acc[spread, :, :, 0:LANES] += dk
                self.acc[spread, :, :, LANES : 2 * LANES] += dv

    def steps(self):
        self.coming.start_all()
        yield
        self.coming.arrived(0, ORIGINS)
        self.block(3)
        self.share(3)
        self.block(2)
        self.share(2)
        self.finish(3)
        self.block(1)
        self.finish(2)
        self.block(0)
        self.share(1)
        self.share(0)
        self.finish(1)
        self.finish(0)
        yield
        self.going.arrived(0, ORIGINS)
        self.coming.sent()
        self.going.sent()
        for cp in self.shares.values():
            cp.wait_send()


ATTEND_BACK_SCRATCH = [
    pltpu.VMEM((ORIGINS, 16, PACKED), jnp.bfloat16),
    pltpu.VMEM((ORIGINS, 2, 32, 2 * LANES), jnp.float32),
    pltpu.VMEM((ORIGINS, 32, 2 * LANES), jnp.float32),
    pltpu.VMEM((ORIGINS, 32, 2 * LANES), jnp.float32),
    pltpu.VMEM((ORIGINS, 32, PACKED), jnp.bfloat16),
    *EXCHANGE_SEMS,
    *EXCHANGE_SEMS,
    pltpu.SemaphoreType.DMA((2, BLOCKS)),
]
RETURNED = ((ORIGINS, 32, PACKED), jnp.bfloat16)


def attend_back_kernel(prefix, keys, values, queries, src, dst, *scratch):
    me = Place()
    meet_plane(me)
    for _ in AttendBack(me, prefix, keys, values, queries, src, dst, scratch).steps():
        pass


def attend_back(prefix, kept, src):
    return pl.pallas_call(
        attend_back_kernel,
        out_shape=jax.ShapeDtypeStruct(*RETURNED),
        in_specs=[SMEM] + [VMEM] * 4,
        out_specs=VMEM,
        scratch_shapes=ATTEND_BACK_SCRATCH,
        compiler_params=pltpu.CompilerParams(
            collective_id=4, has_side_effects=True, vmem_limit_bytes=60 * MIB
        ),
        name="attend_back",
    )(prefix, *kept, src)


def leave_kernel(prefix, keys, values, queries, src, *refs):
    m, n = len(MLP_ARRAYS), len(ATTEND_BACK_SCRATCH)
    ins, outs, dst = refs[:m], refs[m : 2 * m], refs[2 * m]
    scratch = refs[2 * m + 1 :]
    me = Place()
    scatter = Scatter(me, MLP_PIECES, MLP_ARRAYS, ins, outs, scratch[n:])
    attention = AttendBack(me, prefix, keys, values, queries, src, dst, scratch[:n]).steps()
    meet_plane(me, [me.dp_peer()])
    sums = scatter_steps(scatter)
    next(attention)
    next(sums)
    next(attention)
    for _ in sums:
        pass
    for _ in attention:
        pass


def leave(prefix, kept, src, parts):
    m = len(MLP_ARRAYS)
    return pl.pallas_call(
        leave_kernel,
        out_shape=scatter_shapes(MLP_ARRAYS) + [jax.ShapeDtypeStruct(*RETURNED)],
        in_specs=[SMEM] + [VMEM] * 4 + [ANY] * m,
        out_specs=[ANY] * m + [VMEM],
        scratch_shapes=ATTEND_BACK_SCRATCH + scatter_scratch(MLP_PIECES, MLP_ARRAYS),
        compiler_params=pltpu.CompilerParams(
            collective_id=5, has_side_effects=True, vmem_limit_bytes=62 * MIB
        ),
        name="leave",
    )(prefix, *kept, src, *in_shards(parts, MLP_ARRAYS))


def pair_kernel(whole_count, *refs):
    n = (len(refs) - 3) // 2
    ins, outs = refs[:n], refs[n : 2 * n]
    send_sem, recv_sem, own_sem = refs[2 * n :]
    me = Place()
    meet([me.sibling()])
    copies = []
    for i in range(n):
        here = there = ins[i]
        if i >= whole_count:
            width = ins[i].shape[1] // 2
            here = ins[i].at[:, pl.ds(pl.multiple_of(me.c * width, LANES), width)]
            there = ins[i].at[:, pl.ds(pl.multiple_of((1 - me.c) * width, LANES), width)]
        cp = remote(there, outs[i].at[me.c], send_sem.at[i], recv_sem.at[i], me.sibling())
        cp.start()
        copies.append(cp)
        cp = pltpu.make_async_copy(here, outs[i].at[me.c], own_sem.at[i])
        cp.start()
        copies.append(cp)
    for cp in copies:
        cp.wait()


def pair_up(collective_id, whole, halved):
    n = len(whole) + len(halved)
    return pl.pallas_call(
        functools.partial(pair_kernel, len(whole)),
        out_shape=[jax.ShapeDtypeStruct((2, *a.shape), a.dtype) for a in whole]
        + [jax.ShapeDtypeStruct((2, a.shape[0], a.shape[1] // 2), a.dtype) for a in halved],
        in_specs=[VMEM] * n,
        out_specs=[VMEM] * n,
        scratch_shapes=[pltpu.SemaphoreType.DMA((n,))] * 3,
        compiler_params=pltpu.CompilerParams(
            collective_id=collective_id, has_side_effects=True, vmem_limit_bytes=40 * MIB
        ),
        name="pair_up",
    )(*whole, *halved)


STEPS = 8
FF_BLOCK = 512


def rope_tables(positions):
    lane = jnp.arange(PACKED)
    head, spot = lane // HEAD, lane % HEAD
    frequency = ROPE_BASE ** (-(lane % HALF).astype(jnp.float32) * 2.0 / HEAD)
    angles = positions.astype(jnp.float32)[:, None] * frequency[None, :]
    cos, sin = jnp.cos(angles), jnp.sin(angles)
    still, low = (head == 1)[None, :], (spot < HALF)[None, :]
    return (
        jnp.where(still, 1.0, cos),
        jnp.where(still | ~low, 0.0, -sin),
        jnp.where(still | low, 0.0, sin),
    )


def whole_spec(a):
    return pl.BlockSpec(a.shape, lambda k: (0,) * a.ndim, pipeline_mode=pl.Buffered(1))


def mlp_kernel(
    att, x, gain, o_w, gate_w, up_w, down_w, result, attended, middle, normed_two, gate, up, mixed, total
):
    k = pl.program_id(0)

    @pl.when(k == 0)
    def _():
        low_half = lax.broadcasted_iota(jnp.int32, (64, PACKED), 1) < 2 * HEAD
        for pair in range(KV_HEADS // 2):
            even, odd = (
                att[:, 2 * pair + j].reshape(64, PACKED).astype(jnp.float32) for j in range(2)
            )
            upper = jnp.where(low_half, even, pltpu.roll(odd, 2 * HEAD, axis=1))
            lower = jnp.where(low_half, pltpu.roll(even, 2 * HEAD, axis=1), odd)
            rows = jnp.concatenate([upper.reshape(4, 16, PACKED), lower.reshape(4, 16, PACKED)], axis=1)
            attended[:, PACKED * pair : PACKED * (pair + 1)] = rows.reshape(128, PACKED).astype(jnp.bfloat16)
        mid = x[...].astype(jnp.float32) + f32dot(attended[...], o_w[...], ((1,), (0,)))
        middle[...] = mid
        r2 = lax.rsqrt(jnp.mean(mid * mid, axis=-1, keepdims=True) + EPS)
        normed_two[...] = (mid * r2 * gain[0:1, :]).astype(jnp.bfloat16)
        total[...] = mid

    g = f32dot(normed_two[...], gate_w[...], ((1,), (0,)))
    u = f32dot(normed_two[...], up_w[...], ((1,), (0,)))
    gate[...] = g
    up[...] = u
    m = (g * jax.nn.sigmoid(g) * u).astype(jnp.bfloat16)
    mixed[...] = m
    total[...] += f32dot(m, down_w[...], ((1,), (0,)))

    @pl.when(k == STEPS - 1)
    def _():
        result[...] = total[...].astype(jnp.bfloat16)


def mlp(att, x, gain, o_w, gate_w, up_w, down_w):
    tokens, width = x.shape
    ff = gate_w.shape[1]
    in_block = pl.BlockSpec((width, FF_BLOCK), lambda k: (0, k))
    ff_block = pl.BlockSpec((tokens, FF_BLOCK), lambda k: (0, k))
    fixed = pl.BlockSpec((tokens, width), lambda k: (0, 0))
    return pl.pallas_call(
        mlp_kernel,
        grid=(STEPS,),
        out_shape=[
            jax.ShapeDtypeStruct((tokens, width), jnp.bfloat16),
            jax.ShapeDtypeStruct((tokens, width), jnp.bfloat16),
            jax.ShapeDtypeStruct((tokens, width), jnp.float32),
            jax.ShapeDtypeStruct((tokens, width), jnp.bfloat16),
            jax.ShapeDtypeStruct((tokens, ff), jnp.float32),
            jax.ShapeDtypeStruct((tokens, ff), jnp.float32),
            jax.ShapeDtypeStruct((tokens, ff), jnp.bfloat16),
        ],
        in_specs=[
            whole_spec(att),
            whole_spec(x),
            whole_spec(gain),
            whole_spec(o_w),
            in_block,
            in_block,
            pl.BlockSpec((FF_BLOCK, width), lambda k: (k, 0)),
        ],
        out_specs=[fixed, fixed, fixed, fixed, ff_block, ff_block, ff_block],
        scratch_shapes=[pltpu.VMEM((tokens, width), jnp.float32)],
        compiler_params=pltpu.CompilerParams(vmem_limit_bytes=48 * MIB),
        name="mlp",
    )(att, x, gain, o_w, gate_w, up_w, down_w)


def norm_back(dn, gain, u, r):
    scaled = dn * gain
    return r * (scaled - u * jnp.mean(scaled * u, axis=-1, keepdims=True))


def mlp_back_kernel(
    g_low, gate, up, middle, gain, o_w, gate_w, up_w, down_w, dgate, dup, dmiddle, db, dgain, datt, total
):
    k = pl.program_id(0)

    @pl.when(k == 0)
    def _():
        total[...] = jnp.zeros_like(total)

    gm = f32dot(g_low[...], down_w[...], ((1,), (1,)))
    sig = jax.nn.sigmoid(gate[...])
    dg = (gm * up[...] * sig * (1.0 + gate[...] * (1.0 - sig))).astype(jnp.bfloat16)
    du = (gm * (gate[...] * sig)).astype(jnp.bfloat16)
    dgate[...] = dg
    dup[...] = du
    total[...] += f32dot(dg, gate_w[...], ((1,), (1,))) + f32dot(du, up_w[...], ((1,), (1,)))

    @pl.when(k == STEPS - 1)
    def _():
        mid, dn2 = middle[...], total[...]
        r2 = lax.rsqrt(jnp.mean(mid * mid, axis=-1, keepdims=True) + EPS)
        u2 = mid * r2
        dgain[...] = jnp.broadcast_to(jnp.sum(dn2 * u2, axis=0, keepdims=True), dgain.shape)
        dm = g_low[...].astype(jnp.float32) + norm_back(dn2, gain[0:1, :], u2, r2)
        dmiddle[...] = dm
        low = dm.astype(jnp.bfloat16)
        db[...] = low
        low_half = lax.broadcasted_iota(jnp.int32, (4, 16, PACKED), 2) < 2 * HEAD
        for pair in range(KV_HEADS // 2):
            y = f32dot(low, o_w[PACKED * pair : PACKED * (pair + 1), :], ((1,), (1,)))
            turned = pltpu.roll(y, 2 * HEAD, axis=1).reshape(4, 32, PACKED)
            y = y.reshape(4, 32, PACKED)
            even = jnp.where(low_half, y[:, :16], turned[:, 16:])
            odd = jnp.where(low_half, turned[:, :16], y[:, 16:])
            for j, z in enumerate((even, odd)):
                datt[:, 2 * pair + j] = z.astype(jnp.bfloat16).reshape(2, 2, 16, PACKED)


def mlp_back(g_low, gate, up, middle, gain, o_w, gate_w, up_w, down_w):
    tokens, width = g_low.shape
    ff = gate_w.shape[1]
    in_block = pl.BlockSpec((width, FF_BLOCK), lambda k: (0, k))
    ff_block = pl.BlockSpec((tokens, FF_BLOCK), lambda k: (0, k))
    fixed = pl.BlockSpec((tokens, width), lambda k: (0, 0))
    datt_shape = (2, KV_HEADS, 2, 16, PACKED)
    return pl.pallas_call(
        mlp_back_kernel,
        grid=(STEPS,),
        out_shape=[
            jax.ShapeDtypeStruct((tokens, ff), jnp.bfloat16),
            jax.ShapeDtypeStruct((tokens, ff), jnp.bfloat16),
            jax.ShapeDtypeStruct((tokens, width), jnp.float32),
            jax.ShapeDtypeStruct((tokens, width), jnp.bfloat16),
            jax.ShapeDtypeStruct((8, width), jnp.float32),
            jax.ShapeDtypeStruct(datt_shape, jnp.bfloat16),
        ],
        in_specs=[
            whole_spec(g_low),
            ff_block,
            ff_block,
            whole_spec(middle),
            whole_spec(gain),
            whole_spec(o_w),
            in_block,
            in_block,
            pl.BlockSpec((FF_BLOCK, width), lambda k: (k, 0)),
        ],
        out_specs=[
            ff_block,
            ff_block,
            fixed,
            fixed,
            pl.BlockSpec((8, width), lambda k: (0, 0)),
            pl.BlockSpec(datt_shape, lambda k: (0,) * 5),
        ],
        scratch_shapes=[pltpu.VMEM((tokens, width), jnp.float32)],
        compiler_params=pltpu.CompilerParams(vmem_limit_bytes=48 * MIB),
        name="mlp_back",
    )(g_low, gate, up, middle, gain, o_w, gate_w, up_w, down_w)


def qkv_back_kernel(back_in, cos, ahead, back, w, x, dmiddle, gain, dqkv, dx, dgain, total):
    k = pl.program_id(0)

    @pl.when(k == 0)
    def _():
        total[...] = jnp.zeros_like(total)

    z = back_in[...].reshape(128, PACKED).astype(jnp.float32)
    packed = turn_heads(z, cos[...], -ahead[...], -back[...]).astype(jnp.bfloat16)
    dqkv[...] = packed
    total[...] += f32dot(packed, w[...], ((1,), (1,)))

    @pl.when(k == KV_HEADS - 1)
    def _():
        hidden, dn1 = x[...].astype(jnp.float32), total[...]
        r1 = lax.rsqrt(jnp.mean(hidden * hidden, axis=-1, keepdims=True) + EPS)
        u1 = hidden * r1
        dgain[...] = jnp.broadcast_to(jnp.sum(dn1 * u1, axis=0, keepdims=True), dgain.shape)
        dx[...] = (dmiddle[...] + norm_back(dn1, gain[0:1, :], u1, r1)).astype(jnp.bfloat16)


def project_back(back_in, tables, w, x, dmiddle, gain):
    tokens, width = x.shape
    return pl.pallas_call(
        qkv_back_kernel,
        grid=(KV_HEADS,),
        out_shape=[
            jax.ShapeDtypeStruct((tokens, 2 * width), jnp.bfloat16),
            jax.ShapeDtypeStruct((tokens, width), jnp.bfloat16),
            jax.ShapeDtypeStruct((8, width), jnp.float32),
        ],
        in_specs=[
            pl.BlockSpec((2, 1, tokens // 2, PACKED), lambda k: (0, k, 0, 0)),
            *[whole_spec(t) for t in tables],
            pl.BlockSpec((width, 4 * HEAD), lambda k: (0, k)),
            whole_spec(x),
            whole_spec(dmiddle),
            whole_spec(gain),
        ],
        out_specs=[
            pl.BlockSpec((tokens, 4 * HEAD), lambda k: (0, k)),
            pl.BlockSpec((tokens, width), lambda k: (0, 0)),
            pl.BlockSpec((8, width), lambda k: (0, 0)),
        ],
        scratch_shapes=[pltpu.VMEM((tokens, width), jnp.float32)],
        compiler_params=pltpu.CompilerParams(vmem_limit_bytes=56 * MIB),
        name="project_back",
    )(back_in, *tables, w, x, dmiddle, gain)


def body(
    inputs, prefix, cotangent, attn_gain, w_query, w_key, w_value, w_out, mlp_gain, w_gate, w_up, w_down
):
    seqs, rows, width = inputs.shape
    tokens = seqs * rows
    section = lax.axis_index("section")
    seq = lax.axis_index("seq")
    positions = seq * rows + jnp.arange(rows, dtype=jnp.int32)
    tables = rope_tables(jnp.concatenate([positions, positions]))
    own_prefix = lax.dynamic_slice_in_dim(prefix, seq // 16, 1)

    part = w_query.shape[1]
    qkv_shard = jnp.concatenate(
        [
            w_key[0].reshape(part, KV_HEADS, HEAD),
            w_value[0].reshape(part, KV_HEADS, HEAD),
            w_query[0].reshape(part, KV_HEADS, 2 * HEAD),
        ],
        -1,
    ).reshape(part, 2 * width)
    gain_shard = jnp.concatenate(
        [
            jnp.broadcast_to(attn_gain[0][:, None], (part, LANES)),
            jnp.broadcast_to(mlp_gain[0][:, None], (part, LANES)),
        ],
        -1,
    )
    x0 = inputs.reshape(tokens, width)
    gate_w, up_w, qkv_split, o_w, _, down_w, gains, att = enter(
        own_prefix, x0, tables, [w_gate[0], w_up[0], qkv_shard, w_out[0], gain_shard, w_down[0]]
    )
    gate_w, up_w, qkv_w, o_w, down_w = (
        w.reshape(-1, w.shape[-1]) for w in (gate_w, up_w, qkv_split, o_w, down_w)
    )
    gain_attn, gain_mlp = gains[0], gains[1]

    def feed_forward(att, x):
        return mlp(att.reshape(2, KV_HEADS, 2, 16, PACKED), x, gain_mlp, o_w, gate_w, up_w, down_w)

    out0 = feed_forward(att, x0)[0]
    received = lax.ppermute(out0, "section", [(0, 1)])
    x = jnp.where(section == 0, x0, received)
    normed, *kept, att = attend(own_prefix, x, gain_attn, tables, qkv_split)
    out, attended, middle, normed_two, gate, up, mixed = feed_forward(att, x)

    def feed_forward_back(g_low):
        return mlp_back(g_low, gate, up, middle, gain_mlp, o_w, gate_w, up_w, down_w)

    def attention_back(back, dmiddle):
        back = back.reshape(2, KV_HEADS, rows, PACKED)
        return project_back(back, tables, qkv_w, x, dmiddle, gain_attn)

    g0 = cotangent.reshape(tokens, width)
    _, _, dmiddle, _, _, datt = feed_forward_back(g0)
    back = attend_back(own_prefix, kept, datt.reshape(ORIGINS, 16, PACKED))
    _, dx0, _ = attention_back(back, dmiddle)
    received = lax.ppermute(dx0, "section", [(1, 0)])
    g_low = jnp.where(section == 1, g0, received)

    def outer(a, b):
        a, b = a.reshape(2 * tokens, -1), b.reshape(2 * tokens, -1)
        return lax.dot_general(
            a, b, (((0,), (0,)), ((), ())), preferred_element_type=jnp.float32
        ).astype(jnp.bfloat16)

    dgate, dup, dmiddle, db, dgain_mlp, datt = feed_forward_back(g_low)
    normed_two, mixed, g_half, dgate, dup = pair_up(6, [normed_two, mixed], [g_low, dgate, dup])
    gate_g, up_g, down_g, back = leave(
        own_prefix,
        kept,
        datt.reshape(ORIGINS, 16, PACKED),
        [outer(normed_two, dgate), outer(normed_two, dup), outer(mixed, g_half)],
    )
    dqkv, dx, dgain_attn = attention_back(back, dmiddle)
    dgains = jnp.concatenate([dgain_attn, dgain_mlp], axis=1)
    normed, attended, db, dqkv, dgains = pair_up(7, [normed, attended], [db, dqkv, dgains])
    gain_part = jnp.broadcast_to(
        (dgains[0, 0] + dgains[1, 0]).astype(jnp.bfloat16)[:, None], (width, LANES)
    )
    qkv_g, o_g, gain_g = scatter_attn([outer(normed, dqkv), outer(attended, db), gain_part])
    qkv_g = qkv_g.reshape(1, part, KV_HEADS, PACKED)
    key_g = qkv_g[..., :HEAD].reshape(1, part, -1)
    value_g = qkv_g[..., HEAD : 2 * HEAD].reshape(1, part, -1)
    query_g = qkv_g[..., 2 * HEAD :].reshape(1, part, -1)
    return (
        out.reshape(1, seqs, rows, width),
        dx.reshape(1, seqs, rows, width),
        gain_g[:, 0][None],
        query_g,
        key_g,
        value_g,
        o_g[None],
        gain_g[:, LANES][None],
        gate_g[None],
        up_g[None],
        down_g[None],
    )


def solution(mesh):
    split = ("dp", "seq")
    matrix = P("section", split, None)
    vector = P("section", split)
    rows = P("dp", "seq", None)
    layer = P("section", "dp", "seq", None)
    return jax.shard_map(
        body,
        mesh=mesh,
        in_specs=(
            rows, P("dp"), rows, vector, matrix, matrix, matrix, matrix, vector, matrix, matrix, matrix
        ),
        out_specs=(
            layer, layer, vector, matrix, matrix, matrix, matrix, vector, matrix, matrix, matrix
        ),
        check_vma=False,
    )
```

time: 728 us -> 628 us (0.86)
  Pallas kernels: 635 us -> 547 us
  local copies, waits for them, and re-layouts: 37.6 us -> 26 us
    pallas_call x8 -> x5, Pallas kernels: 517 us -> 429 us  [the longest x1 178 us: enter(): pl.pallas_call(enter_kernel, out_shape=[jax.ShapeDtypeStruct((2, 4, 4, 2...]
    unnamed x78 -> x46, local copies, waits for them, and re-layouts: 26.1 us -> 14.2 us
where the time goes in v3:
time: 628 us; the launch traced here: 622 us
  Pallas kernels  547 us (87%)
  local copies, waits for them, and re-layouts  26 us (4%)
  waiting for transfers between devices  20.5 us (3%)
  matrix products  19.3 us (3%)
    pallas_call x1, Pallas kernels, enter(): pl.pallas_call(enter_kernel, out_shape=[jax.ShapeDtypeStruct((2, 4, 4, 2...  178 us
    pallas_call x1, Pallas kernels, leave(): pl.pallas_call(leave_kernel, out_shape=scatter_shapes(MLP_ARRAYS) + [jax....  114 us
    pallas_call x1, Pallas kernels, scatter_attn(): pl.pallas_call(functools.partial(scatter_kernel, pieces, arrays), out_sha...  51.2 us
    pallas_call x2, Pallas kernels, mlp_back(): pl.pallas_call(mlp_back_kernel, grid=(STEPS,), out_shape=[jax.ShapeDtypeS...  48.1 us
    pallas_call x1, Pallas kernels, attend_back(): pl.pallas_call(attend_back_kernel, out_shape=jax.ShapeDtypeStruct(*RETURN...  44 us
    pallas_call x1, Pallas kernels, attend(): pl.pallas_call(attend_kernel, out_shape=[jax.ShapeDtypeStruct(x.shape, jn...  41.9 us
    pallas_call x2, Pallas kernels, mlp(): pl.pallas_call(mlp_kernel, grid=(STEPS,), out_shape=[jax.ShapeDtypeStruct...  40.5 us
    pallas_call x2, Pallas kernels, project_back(): pl.pallas_call(qkv_back_kernel, grid=(KV_HEADS,), out_shape=[jax.ShapeDty...  20.7 us
  transfers between devices with their start and end apart: 2, of which 2 were waited for; matrix products, arithmetic and copies ran while one was open for 0% of the time, Pallas kernels for 0%

profile of v3, /device:TPU:1, one launch (start us, length us, event | category | flops | bytes accessed | tf_op | source)
XLA Modules:
  0.0 621.6 jit_solution(2251948051160143336)
XLA Ops:
  7.7 1.6 fusion
  9.3 177.5 %enter.1 = (bf16[2,4,4,48,4096]{4,3,2,1,0:T(8,128)(2,1)}, bf16[2,4,4,48,4096]{4,3,2,1,0:T(8,128)(2,1)}, bf16[2,4,4,48,3072]{4,3,2,1,0:T(8,128)(2,1)}, bf16[2,4,4...) custom-call(s32[1]{0:T(128)} %dynamic_slice.3.prefix, ...), custom_call_target="tpu_custom_call" | custom-call | tf_op jit(solution)/shard_map/enter/pallas_call | solution.py:952
  186.8 1.5 slice_bitcast_fusion
  190.2 21.2 %mlp.2 = (bf16[128,1536]{1,0:T(8,128)(2,1)S(1)}, bf16[128,1536]{1,0:T(8,128)(2,1)}, f32[128,1536]{1,0:T(8,128)}, bf16[128,1536]{1,0:T(8,128)(2,1)}, f32[128,4096...) custom-call(bf16[2,8,2,16,384]{4,3,2,1,0:T(8,128)(2,1)S(1)} %bitcast.72, bf16[128,1536]{1,0:T(8,128)(2,1)S(1)} %bitcast.70, ...), custom_call_target="tpu_custom_call" | custom-call | tf_op jit(solution)/shard_map/mlp/pallas_call | solution.py:1224
  211.4 2.3 collective-permute-start
  213.7 8.9 %collective-permute-done = bf16[128,1536]{1,0:T(8,128)(2,1)S(1)} collective-permute-done((bf16[128,1536]{1,0:T(8,128)(2,1)S(1)}, bf16[128,1536]{1,0:T(8,128)(2,1)S(1)}, u32[]{:S(2)}, u32[]{:S(2)}) %collective-permute-start) | collective-permute-done | bytes 393248 | tf_op jit(solution)/shard_map/ppermute | solution.py:1428
  223.4 41.9 %attend.1 = (bf16[128,1536]{1,0:T(8,128)(2,1)}, bf16[2048,128]{1,0:T(8,128)(2,1)}, bf16[2048,128]{1,0:T(8,128)(2,1)}, bf16[2,1024,128]{2,1,0:T(8,128)(2,1)}, bf16[32,16,384]{2,1,0:T(8,128)(2,1)}) custom-call(s32[1]{0:T(128)} %dynamic_slice.3.prefix, bf16[128,1536]{1,0:T(8,128)(2,1)} %broadcast_select_fusion.1.x, f32[8,1536]{1,0:T(8,128)} %get-tuple-element.113.gain, ...), custom_call_target="tpu_custom_call" | custom-call | tf_op jit(solution)/shard_map/attend/pallas_call | solution.py:902
  266.3 19.4 %mlp.3 = (bf16[128,1536]{1,0:T(8,128)(2,1)}, bf16[128,1536]{1,0:T(8,128)(2,1)S(1)}, f32[128,1536]{1,0:T(8,128)S(1)}, bf16[128,1536]{1,0:T(8,128)(2,1)S(1)}, f32[...) custom-call(bf16[2,8,2,16,384]{4,3,2,1,0:T(8,128)(2,1)S(1)} %bitcast.73, ...), custom_call_target="tpu_custom_call" | custom-call | tf_op jit(solution)/shard_map/mlp/pallas_call | solution.py:1224
  287.7 24.6 %mlp_back.2 = (bf16[128,4096]{1,0:T(8,128)(2,1)}, bf16[128,4096]{1,0:T(8,128)(2,1)}, f32[128,1536]{1,0:T(8,128)S(1)}, bf16[128,1536]{1,0:T(8,128)(2,1)}, f32[8,1...) custom-call(bf16[128,1536]{1,0:T(8,128)(2,1)S(1)} %bitcast.71, f32[128,4096]{1,0:T(8,128)} %copy-done.1, ...), custom_call_target="tpu_custom_call" | custom-call | tf_op jit(solution)/shard_map/mlp_back/pallas_call | solution.py:1302
  314.0 44.0 %attend_back.1 = bf16[32,32,384]{2,1,0:T(8,128)(2,1)} custom-call(s32[1]{0:T(128)} %dynamic_slice.3.prefix, bf16[2048,128]{1,0:T(8,128)(2,1)} %get-tuple-element.70.keys, bf16[2048,128]{1,0:T(8,128)(2,1)} %get-tuple-element.71.values, bf16[2,1024,128]{2,1,0:T(8,128)(2,1)} %get-tuple-element.72.queries, bf16[32,16,384]{2,1,0:T(8,128)(2,1)} %bitcast.74), custom_call_target="tpu_custom_call" | custom-call | tf_op jit(solution)/shard_map/attend_back/pallas_call | solution.py:1076
  358.0 10.3 %project_back.2 = (bf16[128,3072]{1,0:T(8,128)(2,1)}, bf16[128,1536]{1,0:T(8,128)(2,1)}, f32[8,1536]{1,0:T(8,128)}) custom-call(bf16[2,8,64,384]{3,2,1,0:T(8,128)(2,1)} %bitcast.99, f32[128,384]{1,0:T(8,128)} %get-tuple-element.117.cos, f32[128,384]{1,0:T(8,128)} %get-tuple-element.116.ahead, f32[128,384]{1,0:T(8,128)} %get-tuple-element.115.back, ...), custom_call_target="tpu_custom_call" | custom-call | tf_op jit(solution)/shard_map/project_back/pallas_call | solution.py:1361
  369.6 11.6 %collective-permute-done.1 = bf16[128,1536]{1,0:T(8,128)(2,1)S(1)} collective-permute-done((bf16[128,1536]{1,0:T(8,128)(2,1)}, bf16[128,1536]{1,0:T(8,128)(2,1)S(1)}, u32[]{:S(2)}, u32[]{:S(2)}) %collective-permute-start.1) | collective-permute-done | bytes 393248 | tf_op jit(solution)/shard_map/ppermute | solution.py:1444
  381.3 23.4 %mlp_back.3 = (bf16[128,4096]{1,0:T(8,128)(2,1)S(1)}, bf16[128,4096]{1,0:T(8,128)(2,1)S(1)}, f32[128,1536]{1,0:T(8,128)S(1)}, bf16[128,1536]{1,0:T(8,128)(2,1)S(...) custom-call(bf16[128,1536]{1,0:T(8,128)(2,1)S(1)} %broadcast_select_fusion.g_low.refs_2_, ...), custom_call_target="tpu_custom_call" | custom-call | tf_op jit(solution)/shard_map/mlp_back/pallas_call | solution.py:1302
  405.7 5.6 pair_up.2
  411.3 4.5 bitcast_convert_fusion.2
  415.8 4.5 bitcast_convert_fusion.1
  420.2 4.5 bitcast_convert_fusion
  424.7 113.9 %leave.1 = (f32[24,4096]{1,0:T(8,128)}, f32[24,4096]{1,0:T(8,128)}, f32[64,1536]{1,0:T(8,128)}, bf16[32,32,384]{2,1,0:T(8,128)(2,1)}) custom-call(s32[1]{0:T(128)} %dynamic_slice.3.prefix, bf16[2048,128]{1,0:T(8,128)(2,1)} %get-tuple-element.70.keys, bf16[2048,128]{1,0:T(8,128)(2,1)} %get-tuple-element.71.values, ...), custom_call_target="tpu_custom_call" | custom-call | tf_op jit(solution)/shard_map/leave/pallas_call | solution.py:1109
  538.7 10.4 %project_back.3 = (bf16[128,3072]{1,0:T(8,128)(2,1)}, bf16[128,1536]{1,0:T(8,128)(2,1)}, f32[8,1536]{1,0:T(8,128)}) custom-call(bf16[2,8,64,384]{3,2,1,0:T(8,128)(2,1)} %bitcast.102, f32[128,384]{1,0:T(8,128)} %get-tuple-element.117.cos, f32[128,384]{1,0:T(8,128)} %get-tuple-element.116.ahead, f32[128,384]{1,0:T(8,128)} %get-tuple-element.115.back, ...), custom_call_target="tpu_custom_call" | custom-call | tf_op jit(solution)/shard_map/project_back/pallas_call | solution.py:1361
  551.0 3.3 pair_up.3
  554.4 2.3 bitcast_convert_fusion.4
  556.7 3.6 bitcast_convert_fusion.3
  561.3 51.2 %scatter_attn.1 = (f32[24,3072]{1,0:T(8,128)}, f32[24,1536]{1,0:T(8,128)}, f32[24,256]{1,0:T(8,128)}) custom-call(bf16[2,4,4,48,1536]{4,3,2,1,0:T(8,128)(2,1)} %bitcast.97, bf16[2,4,4,48,768]{4,3,2,1,0:T(8,128)(2,1)} %bitcast.98, bf16[2,4,4,48,128]{4,3,2,1,0:T(8,128)(2,1)} %broadcast_in_dim.71.refs_2_), custom_call_target="tpu_custom_call" | custom-call | tf_op jit(solution)/shard_map/scatter_attn/pallas_call | solution.py:624
  617.3 1.6 copy.44
  (71 shorter events, 26.8 us)
Async XLA Ops:
  188.2 1.0 copy-start.2
  189.2 1.0 copy-start.8
  190.2 32.3 %copy-start.3 = (bf16[2,64,1536]{2,1,0:T(8,128)(2,1)S(1)}, bf16[2,64,1536]{2,1,0:T(8,128)(2,1)}, u32[]{:S(2)}) copy-start(bf16[2,64,1536]{2,1,0:T(8,128)(2,1)} %param.12) | copy-start | bytes 1179652
  211.4 11.2 %collective-permute-start = (bf16[128,1536]{1,0:T(8,128)(2,1)S(1)}, bf16[128,1536]{1,0:T(8,128)(2,1)S(1)}, u32[]{:S(2)}, u32[]{:S(2)}) collective-permute-start(bf16[128,1536]{1,0:T(8,128)(2,1)S(1)} %get-tuple-element.66), channel_id=1, source_target_pairs={{0,64},{1,65},{2,66},{3,67},{4,68},{5,69},{6,70},{7,71},{8,72},{9,... | collective-permute-start | bytes 1179656 | tf_op jit(solution)/shard_map/ppermute | solution.py:1428
  223.4 41.9 %copy-start = (bf16[128,1536]{1,0:T(8,128)(2,1)S(1)}, bf16[128,1536]{1,0:T(8,128)(2,1)}, u32[]{:S(2)}) copy-start(bf16[128,1536]{1,0:T(8,128)(2,1)} %broadcast_select_fusion.1.x) | copy-start | bytes 1179652
  265.3 1.0 copy-start.9
  266.3 21.4 %copy-start.4 = (bf16[2,64,1536]{2,1,0:T(8,128)(2,1)S(1)}, bf16[2,64,1536]{2,1,0:T(8,128)(2,1)}, u32[]{:S(2)}) copy-start(bf16[2,64,1536]{2,1,0:T(8,128)(2,1)} %param.14) | copy-start | bytes 1179652
  285.7 1.3 copy-start.1
  287.0 0.7 copy-start.14
  312.3 0.9 copy-start.6
  313.2 0.7 copy-start.13
  368.3 12.9 %collective-permute-start.1 = (bf16[128,1536]{1,0:T(8,128)(2,1)}, bf16[128,1536]{1,0:T(8,128)(2,1)S(1)}, u32[]{:S(2)}, u32[]{:S(2)}) collective-permute-start(bf16[128,1536]{1,0:T(8,128)(2,1)} %get-tuple-element.78), channel_id=1, source_target_pairs={{64,0},{65,1},{66,2},{67,3},{68,4},{69,5},{70,6},{71,7},{72,8},{73... | collective-permute-start | bytes 1179656 | tf_op jit(solution)/shard_map/ppermute | solution.py:1444
  381.3 24.4 %copy-start.15 = (bf16[128,1536]{1,0:T(8,128)(2,1)S(1)}, bf16[128,1536]{1,0:T(8,128)(2,1)}, u32[]{:S(2)}) copy-start(bf16[128,1536]{1,0:T(8,128)(2,1)} %copy-done.14) | copy-start | bytes 1179652
  404.8 0.9 copy-start.5
  405.7 10.1 %copy-start.11 = (bf16[128,1536]{1,0:T(8,128)(2,1)}, bf16[128,1536]{1,0:T(8,128)(2,1)S(1)}, u32[]{:S(2)}) copy-start(bf16[128,1536]{1,0:T(8,128)(2,1)S(1)} %get-tuple-element.94.refs_2_) | copy-start | bytes 1179652
  405.7 10.1 %copy-start.16 = (bf16[2,8,2,16,384]{4,3,2,1,0:T(8,128)(2,1)}, bf16[2,8,2,16,384]{4,3,2,1,0:T(8,128)(2,1)S(1)}, u32[]{:S(2)}) copy-start(bf16[2,8,2,16,384]{4,3,2,1,0:T(8,128)(2,1)S(1)} %get-tuple-element.79) | copy-start | bytes 1179652
  538.6 11.2 %copy-start.10 = (bf16[128,1536]{1,0:T(8,128)(2,1)S(1)}, bf16[128,1536]{1,0:T(8,128)(2,1)}, u32[]{:S(2)}) copy-start(bf16[128,1536]{1,0:T(8,128)(2,1)} %get-tuple-element.92.refs_0_) | copy-start | bytes 1179652
  538.6 11.2 %copy-start.12 = (bf16[128,1536]{1,0:T(8,128)(2,1)S(1)}, bf16[128,1536]{1,0:T(8,128)(2,1)}, u32[]{:S(2)}) copy-start(bf16[128,1536]{1,0:T(8,128)(2,1)} %copy-done.11) | copy-start | bytes 1179652
  549.8 1.1 copy-start.7
  560.3 58.6 %copy-start.19 = (f32[24,4096]{1,0:T(8,128)S(1)}, f32[24,4096]{1,0:T(8,128)}, u32[]{:S(2)}) copy-start(f32[24,4096]{1,0:T(8,128)} %get-tuple-element.106) | copy-start | bytes 1179652
  560.3 59.3 %copy-start.18 = (f32[24,4096]{1,0:T(8,128)S(1)}, f32[24,4096]{1,0:T(8,128)}, u32[]{:S(2)}) copy-start(f32[24,4096]{1,0:T(8,128)} %get-tuple-element.107) | copy-start | bytes 1179652
  560.3 60.1 %copy-start.17 = (f32[64,1536]{1,0:T(8,128)S(1)}, f32[64,1536]{1,0:T(8,128)}, u32[]{:S(2)}) copy-start(f32[64,1536]{1,0:T(8,128)} %get-tuple-element.108) | copy-start | bytes 1179652

commit v4 on v3

--- a/solution.py
+++ b/solution.py
@@ -35,33 +35,35 @@
     (GAIN, 0, 128, "y", 1, -1),
 )
 GATHER_PIECES = QKV_PIECES + (
+    (GATE, 1024, 1024, "y", -1, None),
+    (UP, 1024, 1024, "z", -1, None),
     (OUT, 0, 384, "y", -1, 1),
     (OUT, 384, 384, "z", -1, 1),
-    (GATE, 0, 512, "y", 1, -1),
-    (GATE, 512, 1536, "y", -1, None),
-    (UP, 0, 512, "z", 1, -1),
-    (UP, 512, 1536, "z", -1, None),
+    (GATE, 0, 1024, "y", 1, -1),
+    (UP, 0, 1024, "z", 1, -1),
     (DOWN, 0, 384, "y", 1, 1),
     (DOWN, 384, 384, "z", 1, 1),
 )
-ATTN_PIECES = (
-    (QKV, 0, 512, "y", 1, 1),
-    (QKV, 512, 256, "y", -1, -1),
-    (QKV, 768, 512, "z", 1, 1),
-    (QKV, 1280, 256, "z", -1, -1),
+LAST_ARRAYS = (QKV, GAIN)
+LAST_PIECES = (
+    (QKV, 0, 256, "y", 1, 1),
+    (QKV, 768, 256, "z", 1, 1),
+    (QKV, 256, 256, "y", -1, -1),
+    (QKV, 1024, 256, "z", -1, -1),
     (GAIN, 0, 128, "y", -1, -1),
-    (OUT, 0, 384, "y", -1, None),
-    (OUT, 384, 384, "z", -1, None),
+    (QKV, 512, 256, "y", 1, None),
+    (QKV, 1280, 256, "z", 1, None),
 )
-MLP_PIECES = (
+MAIN_ARRAYS = (GATE, UP, OUT, DOWN)
+MAIN_PIECES = (
     (GATE, 0, 1024, "y", 1, 1),
     (UP, 0, 1024, "z", 1, 1),
     (DOWN, 0, 384, "y", -1, -1),
     (DOWN, 384, 384, "z", -1, -1),
-    (GATE, 1024, 512, "y", 1, None),
-    (GATE, 1536, 512, "y", -1, None),
-    (UP, 1024, 512, "z", 1, None),
-    (UP, 1536, 512, "z", -1, None),
+    (OUT, 0, 384, "y", -1, None),
+    (OUT, 384, 384, "z", -1, None),
+    (GATE, 1024, 1024, "y", 1, None),
+    (UP, 1024, 1024, "z", 1, None),
 )
 OTHER = {"y": "z", "z": "y"}
 
@@ -431,10 +433,14 @@
             )
         for i in self.of(block, False):
             way = self.way(i, block)
-            for k, (by, ref) in enumerate(((way, self.mid[i]), (0, self.own[i]))):
-                cp = pltpu.make_async_copy(self.column(i, block, by), ref.at[block], self.load.at[k, i, block])
-                cp.start()
-                self.loads[i, block, k] = cp
+            self.fetch(i, block, 1, 0, self.own[i].at[block])
+            if block == 0:
+                self.fetch(i, block, 0, way, self.mid[i])
+
+    def fetch(self, i, block, k, by, ref):
+        cp = pltpu.make_async_copy(self.column(i, block, by), ref, self.load.at[k, i, block])
+        cp.start()
+        self.loads[i, block, k] = cp
 
     def start_crossed(self):
         for k in range(2):
@@ -454,9 +460,11 @@
                 mid = self.ours[i].at[2]
             else:
                 self.loads[i, block, 0].wait()
-                mid = self.mid[i].at[block]
+                mid = self.mid[i]
             near = self.near[i].at[slot]
             add_into(near, mid)
+            if block == 0:
+                self.fetch(i, 1, 0, self.way(i, 1), mid)
             there = self.me.step(OTHER[self.pieces[i][3]], self.way(i, block))
             self.one[i, block, 2] = self.send(i, block, 2, near, self.last[i].at[slot], there)
 
@@ -529,13 +537,31 @@
     def hand_out(self):
         me = self.me
         copies = []
+
+        def give(k, first, width, out):
+            rows = out.shape[0]
+            lanes = pl.ds(first, width)
+            mine = self.total[k].at[pl.ds(pl.multiple_of(me.c * rows, 8), rows), lanes]
+            theirs = self.total[k].at[pl.ds(pl.multiple_of((1 - me.c) * rows, 8), rows), lanes]
+            place = out.at[:, pl.ds(pl.multiple_of(me.c * width, LANES), width)]
+            n = len(copies) // 2
+            copies.append(pltpu.make_async_copy(mine, place, self.keep.at[n]))
+            copies.append(remote(theirs, place, self.fin.at[0, n], self.fin.at[1, n], me.sibling()))
+
         for array, k in self.at.items():
-            rows, width = ARRAYS[array]
-            mine = self.total[k].at[pl.ds(pl.multiple_of(me.c * rows, 8), rows)]
-            theirs = self.total[k].at[pl.ds(pl.multiple_of((1 - me.c) * rows, 8), rows)]
-            place = self.outs[k].at[:, pl.ds(pl.multiple_of(me.c * width, LANES), width)]
-            copies.append(pltpu.make_async_copy(mine, place, self.keep.at[k]))
-            copies.append(remote(theirs, place, self.fin.at[0, k], self.fin.at[1, k], me.sibling()))
+            width = ARRAYS[array][1]
+            if array == QKV:
+                total = self.total[k]
+                groups = [split_four(total[:, PACKED * g : PACKED * (g + 1)]) for g in range(4)]
+                total[:, 0:PACKED] = pack_four([heads[0] for heads in groups])
+                total[:, PACKED : 2 * PACKED] = pack_four([heads[1] for heads in groups])
+                for pair in range(2):
+                    queries = [heads[h] for heads in groups[2 * pair : 2 * pair + 2] for h in (2, 3)]
+                    total[:, PACKED * (2 + pair) : PACKED * (3 + pair)] = pack_four(queries)
+                for j, (first, part) in enumerate(((0, PACKED), (PACKED, PACKED), (2 * PACKED, 2 * PACKED))):
+                    give(k, first, part, self.outs[k][j])
+            else:
+                give(k, 0, width, self.outs[k])
         for cp in copies:
             cp.start()
         for cp in copies:
@@ -549,20 +575,29 @@
     scatter.start(0)
     scatter.start(1)
     yield
-    scatter.hop(0, False)
-    scatter.start_crossed()
-    scatter.hop(1, False)
-    scatter.turn(0, False)
-    scatter.hop_two(0, False)
-    scatter.hop(1, True)
-    scatter.finish(0, False)
-    scatter.turn(1, False)
-    scatter.hop_two(1, False)
-    scatter.turn(1, True)
-    scatter.finish(1, False)
-    scatter.hop_two(1, True)
-    scatter.finish(1, True)
-    scatter.hand_out()
+    for stage in (
+        lambda: scatter.hop(0, False),
+        scatter.start_crossed,
+        lambda: scatter.hop(1, False),
+        lambda: scatter.turn(0, False),
+        lambda: scatter.hop_two(0, False),
+        lambda: scatter.hop(1, True),
+        lambda: scatter.finish(0, False),
+        lambda: scatter.turn(1, False),
+        lambda: scatter.hop_two(1, False),
+        lambda: scatter.turn(1, True),
+        lambda: scatter.finish(1, False),
+        lambda: scatter.hop_two(1, True),
+        lambda: scatter.finish(1, True),
+        scatter.hand_out,
+    ):
+        stage()
+        yield
+
+
+def advance(steps, count):
+    for _ in range(count):
+        next(steps)
 
 
 def scatter_scratch(pieces, arrays):
@@ -575,8 +610,8 @@
         return [pltpu.VMEM((1 if one else 2, *lead, *shape), bf16) for _ in range(count) for shape, one in zip(shapes, crossing)]
 
     held = [
-        pltpu.VMEM((1, 16, LANES) if one else (2, 4, *shape), bf16)
-        for _ in range(2)
+        pltpu.VMEM((1, 16, LANES) if one else (*lead, *shape), bf16)
+        for lead in ((4,), (2, 4))
         for shape, one in zip(shapes, crossing)
     ]
     whole = [pltpu.VMEM((4, 4, *shape), bf16) for _ in range(2) for shape, one in zip(shapes, crossing) if one]
@@ -592,8 +627,8 @@
             pltpu.SemaphoreType.DMA((n, 2, 6)),
             pltpu.SemaphoreType.DMA((n, 2, 6)),
             pltpu.SemaphoreType.DMA((2, n, 4)),
-            pltpu.SemaphoreType.DMA((2, m)),
-            pltpu.SemaphoreType.DMA((m,)),
+            pltpu.SemaphoreType.DMA((2, m + 2)),
+            pltpu.SemaphoreType.DMA((m + 2,)),
         ]
     )
 
@@ -604,34 +639,6 @@
 
 def in_shards(parts, arrays):
     return [part.reshape(2, 4, 4, 2 * ARRAYS[a][0], ARRAYS[a][1]) for part, a in zip(parts, arrays, strict=True)]
-
-
-ATTN_ARRAYS = (QKV, OUT, GAIN)
-MLP_ARRAYS = (GATE, UP, DOWN)
-
-
-def scatter_kernel(pieces, arrays, *refs):
-    m = len(arrays)
-    me = Place()
-    scatter = Scatter(me, pieces, arrays, refs[:m], refs[m : 2 * m], refs[2 * m :])
-    meet(scatter.neighbours())
-    for _ in scatter_steps(scatter):
-        pass
-
-
-def scatter_attn(parts):
-    pieces, arrays = ATTN_PIECES, ATTN_ARRAYS
-    return pl.pallas_call(
-        functools.partial(scatter_kernel, pieces, arrays),
-        out_shape=scatter_shapes(arrays),
-        in_specs=[ANY] * len(arrays),
-        out_specs=[ANY] * len(arrays),
-        scratch_shapes=scatter_scratch(pieces, arrays),
-        compiler_params=pltpu.CompilerParams(
-            collective_id=2, has_side_effects=True, vmem_limit_bytes=56 * MIB
-        ),
-        name="scatter_attn",
-    )(*in_shards(parts, arrays))
 
 
 ORIGINS = 32
@@ -1086,37 +1093,158 @@
     )(prefix, *kept, src)
 
 
-def leave_kernel(prefix, keys, values, queries, src, *refs):
-    m, n = len(MLP_ARRAYS), len(ATTEND_BACK_SCRATCH)
-    ins, outs, dst = refs[:m], refs[m : 2 * m], refs[2 * m]
-    scratch = refs[2 * m + 1 :]
+def norm_back(dn, gain, u, r):
+    scaled = dn * gain
+    return r * (scaled - u * jnp.mean(scaled * u, axis=-1, keepdims=True))
+
+
+def projections_back(me, back, tables, w, x, dmiddle, gain, dqkv, dx, total, held, held_sem):
+    cos, ahead, behind = tables
+
+    def fetch(g, slot):
+        lanes = pl.ds(pl.multiple_of(g * PACKED, LANES), PACKED)
+        return pltpu.make_async_copy(w.at[:, :, :, :, lanes], held.at[slot], held_sem.at[slot])
+
+    fetch(0, 0).start()
+    total[...] = jnp.zeros_like(total)
+
+    def step(g, carry):
+        slot = lax.rem(g, 2)
+        fetch(g, slot).wait()
+
+        @pl.when(g + 1 < KV_HEADS)
+        def _():
+            fetch(g + 1, 1 - slot).start()
+
+        parts = [back[(part // 2) * 16 + g * 2 + part % 2] for part in range(4)]
+        z = jnp.concatenate(parts, axis=0).astype(jnp.float32)
+        z = turn_heads(z, cos[...], -ahead[...], -behind[...]).astype(jnp.bfloat16)
+        dqkv[g] = z
+        total[...] += f32dot(z, held[slot].reshape(x.shape[1], PACKED), ((1,), (1,)))
+        return carry
+
+    lax.fori_loop(0, KV_HEADS, step, 0)
+    hidden, dn1 = x[...].astype(jnp.float32), total[...]
+    r1 = lax.rsqrt(jnp.mean(hidden * hidden, axis=-1, keepdims=True) + EPS)
+    u1 = hidden * r1
+    dx[...] = (dmiddle[...] + norm_back(dn1, gain[0:1, :], u1, r1)).astype(jnp.bfloat16)
+    return jnp.sum(dn1 * u1, axis=0, keepdims=True)
+
+
+def leave_kernel(
+    prefix, keys, values, queries, src, x, dmiddle, normed, gain, dgain_mlp, cos, ahead, behind, w, *refs
+):
+    m = len(MAIN_ARRAYS)
+    ins, refs = refs[:m], refs[m:]
+    outs, refs = refs[:m], refs[m:]
+    last_outs, gain_out, dx, qkv_part, gain_part = refs[:3], refs[3], refs[4], refs[5], refs[6]
+    scratch = refs[7:]
+    (back, dqkv, total, held, held_sem, normed_s, dqkv_s, dgain_give, dgain_got, stage, column) = scratch[:11]
+    pair, out_sem = scratch[11:13]
+    scratch = scratch[13:]
+    n = len(ATTEND_BACK_SCRATCH)
+    k = n + len(scatter_scratch(MAIN_PIECES, MAIN_ARRAYS))
     me = Place()
-    scatter = Scatter(me, MLP_PIECES, MLP_ARRAYS, ins, outs, scratch[n:])
-    attention = AttendBack(me, prefix, keys, values, queries, src, dst, scratch[:n]).steps()
+    main = scatter_steps(Scatter(me, MAIN_PIECES, MAIN_ARRAYS, ins, outs, scratch[n:k]))
+    last = scatter_steps(
+        Scatter(me, LAST_PIECES, LAST_ARRAYS, (qkv_part, gain_part), (last_outs, gain_out), scratch[k:])
+    )
+    attention = AttendBack(me, prefix, keys, values, queries, src, back, scratch[:n]).steps()
     meet_plane(me, [me.dp_peer()])
-    sums = scatter_steps(scatter)
     next(attention)
-    next(sums)
+    next(main)
     next(attention)
-    for _ in sums:
-        pass
+    advance(main, 2)
     for _ in attention:
         pass
-
-
-def leave(prefix, kept, src, parts):
-    m = len(MLP_ARRAYS)
+    dgain = projections_back(
+        me, back, (cos, ahead, behind), w, x, dmiddle, gain, dqkv, dx, total, held, held_sem
+    )
+    half = KV_HEADS // 2
+    dgain = jnp.broadcast_to(dgain, dgain_give.shape)
+    dgain_give[...] = jnp.where(me.c == 0, dgain_mlp[...], dgain)
+    copies = [
+        remote(normed, normed_s, pair.at[0, 0], pair.at[1, 0], me.sibling()),
+        remote(dqkv.at[pl.ds((1 - me.c) * half, half)], dqkv_s, pair.at[0, 1], pair.at[1, 1], me.sibling()),
+        remote(dgain_give, dgain_got, pair.at[0, 2], pair.at[1, 2], me.sibling()),
+    ]
+    for cp in copies:
+        cp.start()
+    next(main)
+    for cp in copies:
+        cp.wait()
+    rows = jnp.where(me.c == 0, dgain, dgain_mlp[...]) + dgain_got[...]
+    first = (lax.broadcasted_iota(jnp.int32, (8, LANES), 0) == 0).astype(jnp.bfloat16)
+    gains = f32dot(rows.astype(jnp.bfloat16), first, ((0,), (0,))).astype(jnp.bfloat16)
+    column[...] = gains.reshape(column.shape)
+    writes = [pltpu.make_async_copy(column, gain_part, out_sem.at[2])]
+    writes[0].start()
+    right = jnp.concatenate(
+        [jnp.concatenate([dqkv[me.c * half + g], dqkv_s[g]], axis=0) for g in range(half)], axis=1
+    )
+    for r in range(4):
+        lanes = slice(PACKED * r, PACKED * (r + 1))
+        left = jnp.concatenate([normed[:, lanes], normed_s[:, lanes]], axis=0)
+        sums = f32dot(left, right, ((0,), (0,))).astype(jnp.bfloat16)
+        if r:
+            writes[r].wait()
+        stage[...] = sums.reshape(stage.shape)
+        cp = pltpu.make_async_copy(stage, qkv_part.at[r // 2, pl.ds(2 * (r % 2), 2)], out_sem.at[r % 2])
+        cp.start()
+        writes.append(cp)
+    for cp in (writes[0], writes[4]):
+        cp.wait()
+    next(last)
+    advance(main, 2)
+    advance(last, 2)
+    advance(main, 2)
+    advance(last, 2)
+    advance(main, 2)
+    advance(last, 2)
+    advance(main, 2)
+    advance(last, 2)
+    advance(main, 2)
+    advance(last, 6)
+    advance(main, 1)
+
+
+def leave(prefix, kept, src, x, dmiddle, normed, gain, dgain_mlp, tables, w, parts):
+    m = len(MAIN_ARRAYS)
+    width = x.shape[1]
+    bf16, f32 = jnp.bfloat16, jnp.float32
+    rows, half = ARRAYS[QKV]
     return pl.pallas_call(
         leave_kernel,
-        out_shape=scatter_shapes(MLP_ARRAYS) + [jax.ShapeDtypeStruct(*RETURNED)],
-        in_specs=[SMEM] + [VMEM] * 4 + [ANY] * m,
-        out_specs=[ANY] * m + [VMEM],
-        scratch_shapes=ATTEND_BACK_SCRATCH + scatter_scratch(MLP_PIECES, MLP_ARRAYS),
+        out_shape=scatter_shapes(MAIN_ARRAYS)
+        + [jax.ShapeDtypeStruct((rows, size), f32) for size in (half // 2, half // 2, half)]
+        + scatter_shapes((GAIN,))
+        + [jax.ShapeDtypeStruct(x.shape, bf16)]
+        + [jax.ShapeDtypeStruct((2, 4, 4, 2 * rows, size), bf16) for size in (half, LANES)],
+        in_specs=[SMEM] + [VMEM] * 12 + [ANY] * (1 + m),
+        out_specs=[ANY] * (m + 4) + [VMEM] + [ANY] * 2,
+        scratch_shapes=[
+            pltpu.VMEM(*RETURNED),
+            pltpu.VMEM((KV_HEADS, x.shape[0], PACKED), bf16),
+            pltpu.VMEM(x.shape, f32),
+            pltpu.VMEM((2, 2, 4, 4, 48, PACKED), bf16),
+            pltpu.SemaphoreType.DMA((2,)),
+            pltpu.VMEM(x.shape, bf16),
+            pltpu.VMEM((KV_HEADS // 2, x.shape[0], PACKED), bf16),
+            pltpu.VMEM((8, width), f32),
+            pltpu.VMEM((8, width), f32),
+            pltpu.VMEM((2, 4, 48, half), bf16),
+            pltpu.VMEM((2, 4, 4, 48, LANES), bf16),
+            pltpu.SemaphoreType.DMA((2, 3)),
+            pltpu.SemaphoreType.DMA((3,)),
+        ]
+        + ATTEND_BACK_SCRATCH
+        + scatter_scratch(MAIN_PIECES, MAIN_ARRAYS)
+        + scatter_scratch(LAST_PIECES, LAST_ARRAYS),
         compiler_params=pltpu.CompilerParams(
             collective_id=5, has_side_effects=True, vmem_limit_bytes=62 * MIB
         ),
         name="leave",
-    )(prefix, *kept, src, *in_shards(parts, MLP_ARRAYS))
+    )(prefix, *kept, src, x, dmiddle, normed, gain, dgain_mlp, *tables, w, *in_shards(parts, MAIN_ARRAYS))
 
 
 def pair_kernel(whole_count, *refs):
@@ -1247,11 +1375,6 @@
         compiler_params=pltpu.CompilerParams(vmem_limit_bytes=48 * MIB),
         name="mlp",
     )(att, x, gain, o_w, gate_w, up_w, down_w)
-
-
-def norm_back(dn, gain, u, r):
-    scaled = dn * gain
-    return r * (scaled - u * jnp.mean(scaled * u, axis=-1, keepdims=True))
 
 
 def mlp_back_kernel(
@@ -1385,6 +1508,25 @@
     )(back_in, *tables, w, x, dmiddle, gain)
 
 
+def hand_over_kernel(*refs):
+    n = len(refs) // 2
+    for src, dst in zip(refs[:n], refs[n:], strict=True):
+        dst[0] = src[...]
+
+
+def hand_over(results):
+    n = len(results)
+    return pl.pallas_call(
+        hand_over_kernel,
+        grid=(1,),
+        out_shape=[jax.ShapeDtypeStruct((1, *a.shape), a.dtype) for a in results],
+        in_specs=[pl.BlockSpec(a.shape, lambda k: (0, 0)) for a in results],
+        out_specs=[pl.BlockSpec((1, *a.shape), lambda k: (0, 0, 0)) for a in results],
+        compiler_params=pltpu.CompilerParams(vmem_limit_bytes=60 * MIB),
+        name="hand_over",
+    )(*results)
+
+
 def body(
     inputs, prefix, cotangent, attn_gain, w_query, w_key, w_value, w_out, mlp_gain, w_gate, w_up, w_down
 ):
@@ -1451,24 +1593,25 @@
         ).astype(jnp.bfloat16)
 
     dgate, dup, dmiddle, db, dgain_mlp, datt = feed_forward_back(g_low)
-    normed_two, mixed, g_half, dgate, dup = pair_up(6, [normed_two, mixed], [g_low, dgate, dup])
-    gate_g, up_g, down_g, back = leave(
+    normed_two, mixed, attended, g_half, dgate, dup, db = pair_up(
+        6, [normed_two, mixed, attended], [g_low, dgate, dup, db]
+    )
+    gate_g, up_g, o_g, down_g, key_g, value_g, query_g, gain_g, dx, _, _ = leave(
         own_prefix,
         kept,
         datt.reshape(ORIGINS, 16, PACKED),
-        [outer(normed_two, dgate), outer(normed_two, dup), outer(mixed, g_half)],
+        x,
+        dmiddle,
+        normed,
+        gain_attn,
+        dgain_mlp,
+        tables,
+        qkv_split,
+        [outer(normed_two, dgate), outer(normed_two, dup), outer(attended, db), outer(mixed, g_half)],
     )
-    dqkv, dx, dgain_attn = attention_back(back, dmiddle)
-    dgains = jnp.concatenate([dgain_attn, dgain_mlp], axis=1)
-    normed, attended, db, dqkv, dgains = pair_up(7, [normed, attended], [db, dqkv, dgains])
-    gain_part = jnp.broadcast_to(
-        (dgains[0, 0] + dgains[1, 0]).astype(jnp.bfloat16)[:, None], (width, LANES)
+    dx, query_g, key_g, value_g, o_g, gate_g, up_g, down_g = hand_over(
+        [dx, query_g, key_g, value_g, o_g, gate_g, up_g, down_g]
     )
-    qkv_g, o_g, gain_g = scatter_attn([outer(normed, dqkv), outer(attended, db), gain_part])
-    qkv_g = qkv_g.reshape(1, part, KV_HEADS, PACKED)
-    key_g = qkv_g[..., :HEAD].reshape(1, part, -1)
-    value_g = qkv_g[..., HEAD : 2 * HEAD].reshape(1, part, -1)
-    query_g = qkv_g[..., 2 * HEAD :].reshape(1, part, -1)
     return (
         out.reshape(1, seqs, rows, width),
         dx.reshape(1, seqs, rows, width),
@@ -1476,11 +1619,11 @@
         query_g,
         key_g,
         value_g,
-        o_g[None],
+        o_g,
         gain_g[:, LANES][None],
-        gate_g[None],
-        up_g[None],
-        down_g[None],
+        gate_g,
+        up_g,
+        down_g,
     )
 
 

time: 628 us -> 595 us (0.947)
  Pallas kernels: 547 us -> 528 us
  local copies, waits for them, and re-layouts: 26 us -> 16.5 us
    pallas_call x2 -> x1, Pallas kernels: 20.7 us -> 10.3 us  [project_back(): pl.pallas_call(qkv_back_kernel, grid=(KV_HEADS,), out_shape=[jax.ShapeDty...]
    pallas_call x1, Pallas kernels: 178 us -> 170 us  [enter(): pl.pallas_call(enter_kernel, out_shape=[jax.ShapeDtypeStruct((2, 4, 4, 2...]
    unnamed x46 -> x29, local copies, waits for them, and re-layouts: 14.2 us -> 8.2 us
    dot_general x5 -> x4, matrix products: 19.3 us -> 15.7 us  [outer(): lax.dot_general(a, b, (((0,), (0,)), ((), ())), preferred_element_type=jn...]
where the time goes in v4:
time: 595 us; the launch traced here: 589 us
  Pallas kernels  528 us (89%)
  waiting for transfers between devices  20.3 us (3%)
  local copies, waits for them, and re-layouts  16.5 us (3%)
  matrix products  15.7 us (3%)
    pallas_call x1, Pallas kernels, enter(): pl.pallas_call(enter_kernel, out_shape=[jax.ShapeDtypeStruct((2, 4, 4, 2...  170 us
    pallas_call x1, Pallas kernels, leave(): pl.pallas_call(leave_kernel, out_shape=scatter_shapes(MAIN_ARRAYS) + [jax...  164 us
    pallas_call x2, Pallas kernels, mlp_back(): pl.pallas_call(mlp_back_kernel, grid=(STEPS,), out_shape=[jax.ShapeDtypeS...  48.1 us
    pallas_call x1, Pallas kernels, attend_back(): pl.pallas_call(attend_back_kernel, out_shape=jax.ShapeDtypeStruct(*RETURN...  43.4 us
    pallas_call x1, Pallas kernels, attend(): pl.pallas_call(attend_kernel, out_shape=[jax.ShapeDtypeStruct(x.shape, jn...  42.2 us
    pallas_call x2, Pallas kernels, mlp(): pl.pallas_call(mlp_kernel, grid=(STEPS,), out_shape=[jax.ShapeDtypeStruct...  40.7 us
    dot_general x4, matrix products, outer(): lax.dot_general(a, b, (((0,), (0,)), ((), ())), preferred_element_type=jn...  15.7 us
  transfers between devices with their start and end apart: 2, of which 2 were waited for; matrix products, arithmetic and copies ran while one was open for 0% of the time, Pallas kernels for 0%

profile of v4, /device:TPU:1, one launch (start us, length us, event | category | flops | bytes accessed | tf_op | source)
XLA Modules:
  0.0 588.6 jit_solution(15731018160622330136)
XLA Ops:
  4.4 1.2 dynamic_slice.3.prefix
  7.7 1.6 fusion
  9.3 170.1 %enter.1 = (bf16[2,4,4,48,4096]{4,3,2,1,0:T(8,128)(2,1)}, bf16[2,4,4,48,4096]{4,3,2,1,0:T(8,128)(2,1)}, bf16[2,4,4,48,3072]{4,3,2,1,0:T(8,128)(2,1)}, bf16[2,4,4...) custom-call(s32[1]{0:T(128)} %dynamic_slice.3.prefix, ...), custom_call_target="tpu_custom_call" | custom-call | tf_op jit(solution)/shard_map/enter/pallas_call | solution.py:959
  179.4 1.5 slice_bitcast_fusion
  182.9 21.2 %mlp.2 = (bf16[128,1536]{1,0:T(8,128)(2,1)S(1)}, bf16[128,1536]{1,0:T(8,128)(2,1)}, f32[128,1536]{1,0:T(8,128)}, bf16[128,1536]{1,0:T(8,128)(2,1)}, f32[128,4096...) custom-call(bf16[2,8,2,16,384]{4,3,2,1,0:T(8,128)(2,1)S(1)} %bitcast.54, bf16[128,1536]{1,0:T(8,128)(2,1)S(1)} %bitcast.51, ...), custom_call_target="tpu_custom_call" | custom-call | tf_op jit(solution)/shard_map/mlp/pallas_call | solution.py:1352
  204.1 2.4 collective-permute-start
  206.5 8.6 %collective-permute-done = bf16[128,1536]{1,0:T(8,128)(2,1)S(1)} collective-permute-done((bf16[128,1536]{1,0:T(8,128)(2,1)S(1)}, bf16[128,1536]{1,0:T(8,128)(2,1)S(1)}, u32[]{:S(2)}, u32[]{:S(2)}) %collective-permute-start) | collective-permute-done | bytes 393248 | tf_op jit(solution)/shard_map/ppermute | solution.py:1570
  216.0 42.2 %attend.1 = (bf16[128,1536]{1,0:T(8,128)(2,1)}, bf16[2048,128]{1,0:T(8,128)(2,1)}, bf16[2048,128]{1,0:T(8,128)(2,1)}, bf16[2,1024,128]{2,1,0:T(8,128)(2,1)}, bf16[32,16,384]{2,1,0:T(8,128)(2,1)}) custom-call(s32[1]{0:T(128)} %dynamic_slice.3.prefix, bf16[128,1536]{1,0:T(8,128)(2,1)} %broadcast_select_fusion.1.x, f32[8,1536]{1,0:T(8,128)} %get-tuple-element.119.gain, ...), custom_call_target="tpu_custom_call" | custom-call | tf_op jit(solution)/shard_map/attend/pallas_call | solution.py:909
  259.2 19.4 %mlp.3 = (bf16[128,1536]{1,0:T(8,128)(2,1)}, bf16[128,1536]{1,0:T(8,128)(2,1)S(1)}, f32[128,1536]{1,0:T(8,128)S(1)}, bf16[128,1536]{1,0:T(8,128)(2,1)S(1)}, f32[...) custom-call(bf16[2,8,2,16,384]{4,3,2,1,0:T(8,128)(2,1)S(1)} %bitcast.55, ...), custom_call_target="tpu_custom_call" | custom-call | tf_op jit(solution)/shard_map/mlp/pallas_call | solution.py:1352
  278.7 1.3 copy-done.1
  280.7 24.6 %mlp_back.2 = (bf16[128,4096]{1,0:T(8,128)(2,1)}, bf16[128,4096]{1,0:T(8,128)(2,1)}, f32[128,1536]{1,0:T(8,128)S(1)}, bf16[128,1536]{1,0:T(8,128)(2,1)}, f32[8,1...) custom-call(bf16[128,1536]{1,0:T(8,128)(2,1)S(1)} %bitcast.52, f32[128,4096]{1,0:T(8,128)} %copy-done.1, ...), custom_call_target="tpu_custom_call" | custom-call | tf_op jit(solution)/shard_map/mlp_back/pallas_call | solution.py:1425
  307.0 43.4 %attend_back.1 = bf16[32,32,384]{2,1,0:T(8,128)(2,1)} custom-call(s32[1]{0:T(128)} %dynamic_slice.3.prefix, bf16[2048,128]{1,0:T(8,128)(2,1)} %get-tuple-element.74.keys, bf16[2048,128]{1,0:T(8,128)(2,1)} %get-tuple-element.75.values, bf16[2,1024,128]{2,1,0:T(8,128)(2,1)} %get-tuple-element.76.queries, bf16[32,16,384]{2,1,0:T(8,128)(2,1)} %bitcast.56), custom_call_target="tpu_custom_call" | custom-call | tf_op jit(solution)/shard_map/attend_back/pallas_call | solution.py:1083
  350.4 10.3 %project_back.1 = (bf16[128,3072]{1,0:T(8,128)(2,1)}, bf16[128,1536]{1,0:T(8,128)(2,1)}, f32[8,1536]{1,0:T(8,128)}) custom-call(bf16[2,8,64,384]{3,2,1,0:T(8,128)(2,1)} %bitcast.78, f32[128,384]{1,0:T(8,128)} %get-tuple-element.123.cos, f32[128,384]{1,0:T(8,128)} %get-tuple-element.122.ahead, f32[128,384]{1,0:T(8,128)} %get-tuple-element.121.back.behind, ...), custom_call_target="tpu_custom_call" | custom-call | tf_op jit(solution)/shard_map/project_back/pallas_call | solution.py:1484
  360.7 1.3 collective-permute-start.1
  362.0 11.7 %collective-permute-done.1 = bf16[128,1536]{1,0:T(8,128)(2,1)S(1)} collective-permute-done((bf16[128,1536]{1,0:T(8,128)(2,1)}, bf16[128,1536]{1,0:T(8,128)(2,1)S(1)}, u32[]{:S(2)}, u32[]{:S(2)}) %collective-permute-start.1) | collective-permute-done | bytes 393248 | tf_op jit(solution)/shard_map/ppermute | solution.py:1586
  373.8 23.4 %mlp_back.3 = (bf16[128,4096]{1,0:T(8,128)(2,1)S(1)}, bf16[128,4096]{1,0:T(8,128)(2,1)S(1)}, f32[128,1536]{1,0:T(8,128)S(1)}, bf16[128,1536]{1,0:T(8,128)(2,1)S(...) custom-call(bf16[128,1536]{1,0:T(8,128)(2,1)S(1)} %broadcast_select_fusion.g_low.refs_3_, ...), custom_call_target="tpu_custom_call" | custom-call | tf_op jit(solution)/shard_map/mlp_back/pallas_call | solution.py:1425
  398.1 6.4 %pair_up.1 = (bf16[2,128,1536]{2,1,0:T(8,128)(2,1)S(1)}, bf16[2,128,4096]{2,1,0:T(8,128)(2,1)S(1)}, bf16[2,128,1536]{2,1,0:T(8,128)(2,1)S(1)}, bf16[2,128,768]{2...) custom-call(bf16[128,1536]{1,0:T(8,128)(2,1)S(1)} %copy-done.11, ...), custom_call_target="tpu_custom_call" | custom-call | tf_op jit(solution)/shard_map/pair_up/pallas_call | solution.py:1275
  404.5 4.5 bitcast_convert_fusion.2
  409.0 4.4 bitcast_convert_fusion.1
  413.5 2.3 bitcast_convert_fusion.3
  415.8 4.5 bitcast_convert_fusion
  420.2 163.7 %leave.1 = (f32[24,4096]{1,0:T(8,128)}, f32[24,4096]{1,0:T(8,128)}, f32[24,1536]{1,0:T(8,128)}, f32[64,1536]{1,0:T(8,128)}, f32[24,768]{1,0:T(8,128)}, /*index=5...) custom-call(s32[1]{0:T(128)} %dynamic_slice.3.prefix, ...), custom_call_target="tpu_custom_call" | custom-call | tf_op jit(solution)/shard_map/leave/pallas_call | solution.py:1216
  584.0 1.4 slice_reduce_fusion
  585.3 2.8 hand_over.1
  (42 shorter events, 12.9 us)
Async XLA Ops:
  180.9 1.0 copy-start.2
  181.9 1.0 copy-start.8
  182.9 32.3 %copy-start.3 = (bf16[2,64,1536]{2,1,0:T(8,128)(2,1)S(1)}, bf16[2,64,1536]{2,1,0:T(8,128)(2,1)}, u32[]{:S(2)}) copy-start(bf16[2,64,1536]{2,1,0:T(8,128)(2,1)} %param.12) | copy-start | bytes 1179652
  204.1 11.1 %collective-permute-start = (bf16[128,1536]{1,0:T(8,128)(2,1)S(1)}, bf16[128,1536]{1,0:T(8,128)(2,1)S(1)}, u32[]{:S(2)}, u32[]{:S(2)}) collective-permute-start(bf16[128,1536]{1,0:T(8,128)(2,1)S(1)} %get-tuple-element.70), channel_id=1, source_target_pairs={{0,64},{1,65},{2,66},{3,67},{4,68},{5,69},{6,70},{7,71},{8,72},{9,... | collective-permute-start | bytes 1179656 | tf_op jit(solution)/shard_map/ppermute | solution.py:1570
  216.0 42.2 %copy-start = (bf16[128,1536]{1,0:T(8,128)(2,1)S(1)}, bf16[128,1536]{1,0:T(8,128)(2,1)}, u32[]{:S(2)}) copy-start(bf16[128,1536]{1,0:T(8,128)(2,1)} %broadcast_select_fusion.1.x) | copy-start | bytes 1179652
  258.2 1.0 copy-start.9
  259.2 21.5 %copy-start.4 = (bf16[2,64,1536]{2,1,0:T(8,128)(2,1)S(1)}, bf16[2,64,1536]{2,1,0:T(8,128)(2,1)}, u32[]{:S(2)}) copy-start(bf16[2,64,1536]{2,1,0:T(8,128)(2,1)} %param.14) | copy-start | bytes 1179652
  278.7 1.3 copy-start.1
  280.0 0.7 copy-start.10
  305.3 0.9 copy-start.5
  306.2 0.7 copy-start.12
  360.7 13.0 %collective-permute-start.1 = (bf16[128,1536]{1,0:T(8,128)(2,1)}, bf16[128,1536]{1,0:T(8,128)(2,1)S(1)}, u32[]{:S(2)}, u32[]{:S(2)}) collective-permute-start(bf16[128,1536]{1,0:T(8,128)(2,1)} %get-tuple-element.82), channel_id=1, source_target_pairs={{64,0},{65,1},{66,2},{67,3},{68,4},{69,5},{70,6},{71,7},{72,8},{73... | collective-permute-start | bytes 1179656 | tf_op jit(solution)/shard_map/ppermute | solution.py:1586
  373.7 24.3 %copy-start.11 = (bf16[128,1536]{1,0:T(8,128)(2,1)S(1)}, bf16[128,1536]{1,0:T(8,128)(2,1)}, u32[]{:S(2)}) copy-start(bf16[128,1536]{1,0:T(8,128)(2,1)} %copy-done.10) | copy-start | bytes 1179652
  397.2 0.9 copy-start.6
  398.1 10.9 %copy-start.7 = (bf16[2,8,2,16,384]{4,3,2,1,0:T(8,128)(2,1)}, bf16[2,8,2,16,384]{4,3,2,1,0:T(8,128)(2,1)S(1)}, u32[]{:S(2)}) copy-start(bf16[2,8,2,16,384]{4,3,2,1,0:T(8,128)(2,1)S(1)} %get-tuple-element.83) | copy-start | bytes 1179652
  398.1 10.9 %copy-start.13 = (f32[8,1536]{1,0:T(8,128)}, f32[8,1536]{1,0:T(8,128)S(1)}, u32[]{:S(2)}) copy-start(f32[8,1536]{1,0:T(8,128)S(1)} %get-tuple-element.86.dgain_mlp) | copy-start | bytes 147460

commit v5 on v4

--- a/solution.py
+++ b/solution.py
@@ -34,9 +34,11 @@
     (QKV, 1280, 256, "z", -1, -1),
     (GAIN, 0, 128, "y", 1, -1),
 )
-GATHER_PIECES = QKV_PIECES + (
+CROSSING_PIECES = (
     (GATE, 1024, 1024, "y", -1, None),
     (UP, 1024, 1024, "z", -1, None),
+)
+REST_PIECES = (
     (OUT, 0, 384, "y", -1, 1),
     (OUT, 384, 384, "z", -1, 1),
     (GATE, 0, 1024, "y", 1, -1),
@@ -44,6 +46,7 @@
     (DOWN, 0, 384, "y", 1, 1),
     (DOWN, 384, 384, "z", 1, 1),
 )
+GATHER_PIECES = QKV_PIECES + CROSSING_PIECES + REST_PIECES
 LAST_ARRAYS = (QKV, GAIN)
 LAST_PIECES = (
     (QKV, 0, 256, "y", 1, 1),
@@ -95,6 +98,9 @@
     def sibling(self):
         return (self.s, self.d, self.q + 1 - 2 * self.c)
 
+    def section_peer(self):
+        return (1 - self.s, self.d, self.q)
+
     def dp_peer(self):
         return (self.s, 1 - self.d, self.q)
 
@@ -112,7 +118,25 @@
     )
 
 
-EARLY = len(QKV_PIECES)
+class Handover:
+    def __init__(self, me, source, made, own, result, sems):
+        self.me, self.source, self.own, self.result = me, source, own, result
+        self.copy = remote(made, result, sems.at[0], sems.at[1], me.section_peer())
+
+    def start(self):
+        @pl.when(self.me.s == self.source)
+        def _():
+            self.copy.start()
+            self.result[...] = self.own[...]
+
+    def wait(self):
+        @pl.when(self.me.s == self.source)
+        def _():
+            self.copy.wait_send()
+
+        @pl.when(self.me.s != self.source)
+        def _():
+            self.copy.wait_recv()
 
 
 class Gather:
@@ -193,15 +217,17 @@
             cp.start()
             self.swaps[a] = cp
 
-    def join(self, a):
-        me, width = self.me, ARRAYS[a][1]
-        self.swaps[a].wait()
-        start = pl.multiple_of(me.c * width, LANES)
-        mine = self.ins[a][:, pl.ds(start, width)].astype(jnp.float32)
-        theirs = self.got[a][...]
-        low = jnp.where(me.c == 0, mine, theirs)
-        high = jnp.where(me.c == 0, theirs, mine)
-        self.chip[a][...] = jnp.concatenate([low, high], axis=0).astype(jnp.bfloat16)
+    def join(self, *arrays):
+        me = self.me
+        for a in arrays:
+            width = ARRAYS[a][1]
+            self.swaps[a].wait()
+            start = pl.multiple_of(me.c * width, LANES)
+            mine = self.ins[a][:, pl.ds(start, width)].astype(jnp.float32)
+            theirs = self.got[a][...]
+            low = jnp.where(me.c == 0, mine, theirs)
+            high = jnp.where(me.c == 0, theirs, mine)
+            self.chip[a][...] = jnp.concatenate([low, high], axis=0).astype(jnp.bfloat16)
 
     def start(self, pieces):
         me = self.me
@@ -285,67 +311,20 @@
 )
 
 
-def gather_steps(gather):
-    early = range(EARLY)
-    late = range(EARLY, len(GATHER_PIECES))
-    gather.swap()
-    for a in (QKV, GAIN):
-        gather.join(a)
-    gather.start(early)
-    for a in (OUT, GATE, UP, DOWN):
-        gather.join(a)
-    gather.start(late)
-    gather.hop(early, 0, False)
-    gather.turn(early, 0)
-    gather.start_other(early)
-    gather.hop(late, 0, False)
-    gather.hop(early, 1, False)
-    gather.turn(early, 1)
-    gather.turn(late, 0)
-    gather.start_other(late)
-    gather.hop(early, 0, True)
-    gather.hop(late, 1, False)
-    gather.hop(early, 1, True)
-    gather.finish(early, 0)
-    gather.hop(late, 0, True)
-    gather.turn(late, 1)
-    gather.finish(early, 1)
-    gather.shown(early)
-    yield
-    gather.finish(late, 0)
-    gather.cross(late, range(4))
-    gather.hop(late, 1, True)
-    yield
-    gather.finish(late, 1)
-    gather.cross(late, range(4, 7))
-    gather.shown(late)
-    gather.drain()
-
-
 def add_into(total, term):
-    chunks = total.shape[1] // 16
-
-    def step(k, carry):
-        j = lax.div(k, chunks)
-        rows = pl.ds(pl.multiple_of(lax.rem(k, chunks) * 16, 16), 16)
-        both = total[j, rows, :].astype(jnp.float32) + term[j, rows, :].astype(jnp.float32)
-        total[j, rows, :] = both.astype(jnp.bfloat16)
+    def step(j, carry):
+        total[j] = total[j] + term[j]
         return carry
 
-    lax.fori_loop(0, total.shape[0] * chunks, step, 0)
+    lax.fori_loop(0, total.shape[0], step, 0)
 
 
 def add_two(total, left, right):
-    chunks = total.shape[1] // 16
-
-    def step(k, carry):
-        j = lax.div(k, chunks)
-        rows = pl.ds(pl.multiple_of(lax.rem(k, chunks) * 16, 16), 16)
-        parts = [ref[j, rows, :].astype(jnp.float32) for ref in (total, left, right)]
-        total[j, rows, :] = (parts[0] + (parts[1] + parts[2])).astype(jnp.bfloat16)
+    def step(j, carry):
+        total[j] = total[j] + (left[j] + right[j])
         return carry
 
-    lax.fori_loop(0, total.shape[0] * chunks, step, 0)
+    lax.fori_loop(0, total.shape[0], step, 0)
 
 
 class Scatter:
@@ -568,36 +547,6 @@
             cp.wait()
         for cp in self.pending:
             cp.wait_send()
-
-
-def scatter_steps(scatter):
-    scatter.start_crossing()
-    scatter.start(0)
-    scatter.start(1)
-    yield
-    for stage in (
-        lambda: scatter.hop(0, False),
-        scatter.start_crossed,
-        lambda: scatter.hop(1, False),
-        lambda: scatter.turn(0, False),
-        lambda: scatter.hop_two(0, False),
-        lambda: scatter.hop(1, True),
-        lambda: scatter.finish(0, False),
-        lambda: scatter.turn(1, False),
-        lambda: scatter.hop_two(1, False),
-        lambda: scatter.turn(1, True),
-        lambda: scatter.finish(1, False),
-        lambda: scatter.hop_two(1, True),
-        lambda: scatter.finish(1, True),
-        scatter.hand_out,
-    ):
-        stage()
-        yield
-
-
-def advance(steps, count):
-    for _ in range(count):
-        next(steps)
 
 
 def scatter_scratch(pieces, arrays):
@@ -850,7 +799,7 @@
                 ready += 1
             k = self.keys[pl.ds(0, count), :]
             v = self.values[pl.ds(0, count), :]
-            allowed = block_mask(block, count, self.me.c, self.prefix[0])
+            allowed = block_mask(block, count, self.me.c, self.prefix[lax.div(self.me.q, 16)])
             quarters = []
             for h in range(2):
                 q = self.queries[h, pl.ds(block * BLOCK * 32, BLOCK * 32), :]
@@ -892,9 +841,14 @@
 ATTENDED = ((ORIGINS, 16, PACKED), jnp.bfloat16)
 
 
-def attend_kernel(prefix, x, gain, cos, ahead, back, w, normed, keys, values, queries, dst, *scratch):
+def attend_kernel(
+    prefix, made, own, gain, cos, ahead, back, w, x, normed, keys, values, queries, dst, handed, *scratch
+):
     me = Place()
-    meet_plane(me)
+    meet_plane(me, [me.section_peer()])
+    handover = Handover(me, 0, made, own, x, handed)
+    handover.start()
+    handover.wait()
     bundle, held, held_sem = scratch[:3]
     attention = Attend(me, prefix, bundle, dst, keys, values, queries, scratch[3:])
     project_and_send(
@@ -905,20 +859,20 @@
     attention.drain()
 
 
-def attend(prefix, x, gain, tables, w):
+def attend(prefix, made, own, gain, tables, w):
     return pl.pallas_call(
         attend_kernel,
-        out_shape=[jax.ShapeDtypeStruct(x.shape, jnp.bfloat16)]
+        out_shape=[jax.ShapeDtypeStruct(own.shape, jnp.bfloat16)] * 2
         + [jax.ShapeDtypeStruct(*kept) for kept in KEPT]
         + [jax.ShapeDtypeStruct(*ATTENDED)],
-        in_specs=[SMEM] + [VMEM] * 5 + [ANY],
-        out_specs=[VMEM] * 5,
-        scratch_shapes=PROJECT_SCRATCH + ATTEND_SCRATCH,
+        in_specs=[SMEM] + [VMEM] * 6 + [ANY],
+        out_specs=[VMEM] * 6,
+        scratch_shapes=[pltpu.SemaphoreType.DMA((2,))] + PROJECT_SCRATCH + ATTEND_SCRATCH,
         compiler_params=pltpu.CompilerParams(
             collective_id=3, has_side_effects=True, vmem_limit_bytes=60 * MIB
         ),
         name="attend",
-    )(prefix, x, gain, *tables, w)
+    )(prefix, made, own, gain, *tables, w)
 
 
 def enter_kernel(prefix, x, cos, ahead, back, *refs):
@@ -933,23 +887,60 @@
     attention = Attend(me, prefix, bundle, dst, keys, values, queries, rest[3:k])
     gather = Gather(me, ins, outs, rest[k:])
     meet_plane(me, [me.dp_peer()])
-    steps = gather_steps(gather)
-    next(steps)
-    cp = pltpu.make_async_copy(outs[GAIN], column, column_sem.at[0])
-    cp.start()
-    cp.wait()
-    first = (lax.broadcasted_iota(jnp.int32, (8, LANES), 1) == 0).astype(jnp.bfloat16)
-    for half in range(2):
-        one = column[:, :, :, :, half * LANES : (half + 1) * LANES].reshape(x.shape[1], LANES)
-        gains[half] = f32dot(first, one, ((1,), (1,)))
-    project_and_send(
-        x, gains[0, 0:1, :], outs[QKV], (cos, ahead, back), normed, bundle, held, held_sem, attention.coming
-    )
+
+    def project():
+        cp = pltpu.make_async_copy(outs[GAIN], column, column_sem.at[0])
+        cp.start()
+        cp.wait()
+        first = (lax.broadcasted_iota(jnp.int32, (8, LANES), 1) == 0).astype(jnp.bfloat16)
+        for half in range(2):
+            one = column[:, :, :, :, half * LANES : (half + 1) * LANES].reshape(x.shape[1], LANES)
+            gains[half] = f32dot(first, one, ((1,), (1,)))
+        tables = (cos, ahead, back)
+        project_and_send(
+            x, gains[0, 0:1, :], outs[QKV], tables, normed, bundle, held, held_sem, attention.coming
+        )
+
+    first, second = len(QKV_PIECES), len(QKV_PIECES + CROSSING_PIECES)
+    early, crossing, rest = range(first), range(first, second), range(second, len(GATHER_PIECES))
+    gather.swap()
+    gather.join(QKV, GAIN)
+    gather.start(early)
+    gather.join(GATE, UP)
+    gather.join(OUT, DOWN)
+    gather.start(crossing)
+    gather.start(rest)
+    gather.hop(early, 0, False)
+    gather.turn(early, 0)
+    gather.start_other(early)
+    gather.hop(crossing, 0, False)
+    gather.hop(rest, 0, False)
+    gather.hop(early, 1, False)
+    gather.turn(early, 1)
+    gather.turn(crossing, 0)
+    gather.turn(rest, 0)
+    gather.start_other(rest)
+    gather.hop(early, 0, True)
+    gather.hop(rest, 1, False)
+    gather.hop(early, 1, True)
+    gather.finish(early, 0)
+    gather.hop(crossing, 0, True)
+    gather.hop(rest, 0, True)
+    gather.turn(rest, 1)
+    gather.finish(early, 1)
+    gather.shown(early)
+    project()
     attention.receive()
-    next(steps)
+    gather.finish(crossing, 0)
+    gather.finish(rest, 0)
+    gather.cross(crossing, range(4))
+    gather.hop(rest, 1, True)
     attention.compute()
-    for _ in steps:
-        pass
+    gather.finish(rest, 1)
+    gather.cross(crossing, range(4, 7))
+    gather.shown(crossing)
+    gather.shown(rest)
+    gather.drain()
     attention.drain()
 
 
@@ -1010,7 +1001,7 @@
         spread = pl.ds(0, count // 64)
         k = self.keys[pl.ds(0, count), :]
         v = self.values[pl.ds(0, count), :]
-        allowed = block_mask(block, count, self.me.c, self.prefix[0])
+        allowed = block_mask(block, count, self.me.c, self.prefix[lax.div(self.me.q, 16)])
         quarters = split_four(self.datt[group(block)].reshape(BLOCK * 16, PACKED).astype(jnp.float32))
         inside = lax.broadcasted_iota(jnp.int32, (BLOCK * 32, LANES), 1) < HEAD
         for h in range(2):
@@ -1039,6 +1030,7 @@
         self.coming.start_all()
         yield
         self.coming.arrived(0, ORIGINS)
+        yield
         self.block(3)
         self.share(3)
         self.block(2)
@@ -1072,27 +1064,6 @@
 RETURNED = ((ORIGINS, 32, PACKED), jnp.bfloat16)
 
 
-def attend_back_kernel(prefix, keys, values, queries, src, dst, *scratch):
-    me = Place()
-    meet_plane(me)
-    for _ in AttendBack(me, prefix, keys, values, queries, src, dst, scratch).steps():
-        pass
-
-
-def attend_back(prefix, kept, src):
-    return pl.pallas_call(
-        attend_back_kernel,
-        out_shape=jax.ShapeDtypeStruct(*RETURNED),
-        in_specs=[SMEM] + [VMEM] * 4,
-        out_specs=VMEM,
-        scratch_shapes=ATTEND_BACK_SCRATCH,
-        compiler_params=pltpu.CompilerParams(
-            collective_id=4, has_side_effects=True, vmem_limit_bytes=60 * MIB
-        ),
-        name="attend_back",
-    )(prefix, *kept, src)
-
-
 def norm_back(dn, gain, u, r):
     scaled = dn * gain
     return r * (scaled - u * jnp.mean(scaled * u, axis=-1, keepdims=True))
@@ -1129,6 +1100,44 @@
     u1 = hidden * r1
     dx[...] = (dmiddle[...] + norm_back(dn1, gain[0:1, :], u1, r1)).astype(jnp.bfloat16)
     return jnp.sum(dn1 * u1, axis=0, keepdims=True)
+
+
+def attend_back_kernel(
+    prefix, keys, values, queries, src, x, dmiddle, gain, own, cos, ahead, behind, w, result, handed, *scratch
+):
+    me = Place()
+    back, dqkv, dx, total, held, held_sem = scratch[:6]
+    meet_plane(me, [me.section_peer()])
+    for _ in AttendBack(me, prefix, keys, values, queries, src, back, scratch[6:]).steps():
+        pass
+    projections_back(me, back, (cos, ahead, behind), w, x, dmiddle, gain, dqkv, dx, total, held, held_sem)
+    handover = Handover(me, 1, dx, own, result, handed)
+    handover.start()
+    handover.wait()
+
+
+def attend_back(prefix, kept, src, x, dmiddle, gain, own, tables, w):
+    bf16 = jnp.bfloat16
+    return pl.pallas_call(
+        attend_back_kernel,
+        out_shape=jax.ShapeDtypeStruct(x.shape, bf16),
+        in_specs=[SMEM] + [VMEM] * 11 + [ANY],
+        out_specs=VMEM,
+        scratch_shapes=[
+            pltpu.SemaphoreType.DMA((2,)),
+            pltpu.VMEM(*RETURNED),
+            pltpu.VMEM((KV_HEADS, x.shape[0], PACKED), bf16),
+            pltpu.VMEM(x.shape, bf16),
+            pltpu.VMEM(x.shape, jnp.float32),
+            pltpu.VMEM((2, 2, 4, 4, 48, PACKED), bf16),
+            pltpu.SemaphoreType.DMA((2,)),
+        ]
+        + ATTEND_BACK_SCRATCH,
+        compiler_params=pltpu.CompilerParams(
+            collective_id=4, has_side_effects=True, vmem_limit_bytes=60 * MIB
+        ),
+        name="attend_back",
+    )(prefix, *kept, src, x, dmiddle, gain, own, *tables, w)
 
 
 def leave_kernel(
@@ -1145,67 +1154,94 @@
     n = len(ATTEND_BACK_SCRATCH)
     k = n + len(scatter_scratch(MAIN_PIECES, MAIN_ARRAYS))
     me = Place()
-    main = scatter_steps(Scatter(me, MAIN_PIECES, MAIN_ARRAYS, ins, outs, scratch[n:k]))
-    last = scatter_steps(
-        Scatter(me, LAST_PIECES, LAST_ARRAYS, (qkv_part, gain_part), (last_outs, gain_out), scratch[k:])
-    )
+    main = Scatter(me, MAIN_PIECES, MAIN_ARRAYS, ins, outs, scratch[n:k])
+    last = Scatter(me, LAST_PIECES, LAST_ARRAYS, (qkv_part, gain_part), (last_outs, gain_out), scratch[k:])
     attention = AttendBack(me, prefix, keys, values, queries, src, back, scratch[:n]).steps()
+    half = KV_HEADS // 2
+    shown = []
+
+    def project():
+        dgain = projections_back(
+            me, back, (cos, ahead, behind), w, x, dmiddle, gain, dqkv, dx, total, held, held_sem
+        )
+        dgain = jnp.broadcast_to(dgain, dgain_give.shape)
+        dgain_give[...] = jnp.where(me.c == 0, dgain_mlp[...], dgain)
+        shown.append(dgain)
+        shown.extend([
+            remote(normed, normed_s, pair.at[0, 0], pair.at[1, 0], me.sibling()),
+            remote(dqkv.at[pl.ds((1 - me.c) * half, half)], dqkv_s, pair.at[0, 1], pair.at[1, 1], me.sibling()),
+            remote(dgain_give, dgain_got, pair.at[0, 2], pair.at[1, 2], me.sibling()),
+        ])
+        for cp in shown[1:]:
+            cp.start()
+
+    def weigh():
+        dgain = shown[0]
+        for cp in shown[1:]:
+            cp.wait()
+        rows = jnp.where(me.c == 0, dgain, dgain_mlp[...]) + dgain_got[...]
+        first = (lax.broadcasted_iota(jnp.int32, (8, LANES), 0) == 0).astype(jnp.bfloat16)
+        gains = f32dot(rows.astype(jnp.bfloat16), first, ((0,), (0,))).astype(jnp.bfloat16)
+        column[...] = gains.reshape(column.shape)
+        writes = [pltpu.make_async_copy(column, gain_part, out_sem.at[2])]
+        writes[0].start()
+        right = jnp.concatenate(
+            [jnp.concatenate([dqkv[me.c * half + g], dqkv_s[g]], axis=0) for g in range(half)], axis=1
+        )
+        for r in range(4):
+            lanes = slice(PACKED * r, PACKED * (r + 1))
+            left = jnp.concatenate([normed[:, lanes], normed_s[:, lanes]], axis=0)
+            sums = f32dot(left, right, ((0,), (0,))).astype(jnp.bfloat16)
+            if r:
+                writes[r].wait()
+            stage[...] = sums.reshape(stage.shape)
+            cp = pltpu.make_async_copy(stage, qkv_part.at[r // 2, pl.ds(2 * (r % 2), 2)], out_sem.at[r % 2])
+            cp.start()
+            writes.append(cp)
+        for cp in (writes[0], writes[4]):
+            cp.wait()
+
     meet_plane(me, [me.dp_peer()])
-    next(attention)
-    next(main)
-    next(attention)
-    advance(main, 2)
-    for _ in attention:
-        pass
-    dgain = projections_back(
-        me, back, (cos, ahead, behind), w, x, dmiddle, gain, dqkv, dx, total, held, held_sem
-    )
-    half = KV_HEADS // 2
-    dgain = jnp.broadcast_to(dgain, dgain_give.shape)
-    dgain_give[...] = jnp.where(me.c == 0, dgain_mlp[...], dgain)
-    copies = [
-        remote(normed, normed_s, pair.at[0, 0], pair.at[1, 0], me.sibling()),
-        remote(dqkv.at[pl.ds((1 - me.c) * half, half)], dqkv_s, pair.at[0, 1], pair.at[1, 1], me.sibling()),
-        remote(dgain_give, dgain_got, pair.at[0, 2], pair.at[1, 2], me.sibling()),
-    ]
-    for cp in copies:
-        cp.start()
-    next(main)
-    for cp in copies:
-        cp.wait()
-    rows = jnp.where(me.c == 0, dgain, dgain_mlp[...]) + dgain_got[...]
-    first = (lax.broadcasted_iota(jnp.int32, (8, LANES), 0) == 0).astype(jnp.bfloat16)
-    gains = f32dot(rows.astype(jnp.bfloat16), first, ((0,), (0,))).astype(jnp.bfloat16)
-    column[...] = gains.reshape(column.shape)
-    writes = [pltpu.make_async_copy(column, gain_part, out_sem.at[2])]
-    writes[0].start()
-    right = jnp.concatenate(
-        [jnp.concatenate([dqkv[me.c * half + g], dqkv_s[g]], axis=0) for g in range(half)], axis=1
-    )
-    for r in range(4):
-        lanes = slice(PACKED * r, PACKED * (r + 1))
-        left = jnp.concatenate([normed[:, lanes], normed_s[:, lanes]], axis=0)
-        sums = f32dot(left, right, ((0,), (0,))).astype(jnp.bfloat16)
-        if r:
-            writes[r].wait()
-        stage[...] = sums.reshape(stage.shape)
-        cp = pltpu.make_async_copy(stage, qkv_part.at[r // 2, pl.ds(2 * (r % 2), 2)], out_sem.at[r % 2])
-        cp.start()
-        writes.append(cp)
-    for cp in (writes[0], writes[4]):
-        cp.wait()
-    next(last)
-    advance(main, 2)
-    advance(last, 2)
-    advance(main, 2)
-    advance(last, 2)
-    advance(main, 2)
-    advance(last, 2)
-    advance(main, 2)
-    advance(last, 2)
-    advance(main, 2)
-    advance(last, 6)
-    advance(main, 1)
+    next(attention, None)
+    main.start_crossing()
+    next(attention, None)
+    main.start(0)
+    next(attention, None)
+    main.hop(0, False)
+    main.start(1)
+    main.start_crossed()
+    next(attention, None)
+    project()
+    main.turn(0, False)
+    main.hop(1, False)
+    weigh()
+    last.start_crossing()
+    last.start(0)
+    main.hop_two(0, False)
+    last.start(1)
+    main.finish(0, False)
+    main.hop(1, True)
+    last.hop(0, False)
+    main.turn(1, False)
+    last.start_crossed()
+    last.hop(1, False)
+    main.hop_two(1, False)
+    last.turn(0, False)
+    main.turn(1, True)
+    last.hop_two(0, False)
+    last.hop(1, True)
+    main.finish(1, False)
+    last.finish(0, False)
+    last.turn(1, False)
+    main.hop_two(1, True)
+    last.hop_two(1, False)
+    last.turn(1, True)
+    main.finish(1, True)
+    last.finish(1, False)
+    last.hop_two(1, True)
+    last.finish(1, True)
+    last.hand_out()
+    main.hand_out()
 
 
 def leave(prefix, kept, src, x, dmiddle, normed, gain, dgain_mlp, tables, w, parts):
@@ -1372,7 +1408,7 @@
         ],
         out_specs=[fixed, fixed, fixed, fixed, ff_block, ff_block, ff_block],
         scratch_shapes=[pltpu.VMEM((tokens, width), jnp.float32)],
-        compiler_params=pltpu.CompilerParams(vmem_limit_bytes=48 * MIB),
+        compiler_params=pltpu.CompilerParams(vmem_limit_bytes=60 * MIB),
         name="mlp",
     )(att, x, gain, o_w, gate_w, up_w, down_w)
 
@@ -1458,54 +1494,34 @@
     )(g_low, gate, up, middle, gain, o_w, gate_w, up_w, down_w)
 
 
-def qkv_back_kernel(back_in, cos, ahead, back, w, x, dmiddle, gain, dqkv, dx, dgain, total):
-    k = pl.program_id(0)
-
-    @pl.when(k == 0)
-    def _():
-        total[...] = jnp.zeros_like(total)
-
-    z = back_in[...].reshape(128, PACKED).astype(jnp.float32)
-    packed = turn_heads(z, cos[...], -ahead[...], -back[...]).astype(jnp.bfloat16)
-    dqkv[...] = packed
-    total[...] += f32dot(packed, w[...], ((1,), (1,)))
-
-    @pl.when(k == KV_HEADS - 1)
-    def _():
-        hidden, dn1 = x[...].astype(jnp.float32), total[...]
-        r1 = lax.rsqrt(jnp.mean(hidden * hidden, axis=-1, keepdims=True) + EPS)
-        u1 = hidden * r1
-        dgain[...] = jnp.broadcast_to(jnp.sum(dn1 * u1, axis=0, keepdims=True), dgain.shape)
-        dx[...] = (dmiddle[...] + norm_back(dn1, gain[0:1, :], u1, r1)).astype(jnp.bfloat16)
-
-
-def project_back(back_in, tables, w, x, dmiddle, gain):
-    tokens, width = x.shape
+def outer_kernel(normed_two, attended, mixed, dgate, dup, db, g, gate, up, out, down):
+    def rows(ref):
+        return ref[...].reshape(2 * ref.shape[1], ref.shape[2])
+
+    left = rows(normed_two)
+    gate[...] = f32dot(left, rows(dgate), ((0,), (0,))).astype(jnp.bfloat16)
+    up[...] = f32dot(left, rows(dup), ((0,), (0,))).astype(jnp.bfloat16)
+    out[...] = f32dot(rows(attended), rows(db), ((0,), (0,))).astype(jnp.bfloat16)
+    down[...] = f32dot(rows(mixed), rows(g), ((0,), (0,))).astype(jnp.bfloat16)
+
+
+def outer_products(normed_two, attended, mixed, dgate, dup, db, g):
+    steps = 4
+    pairs = ((normed_two, dgate), (normed_two, dup), (attended, db), (mixed, g))
+
+    def part(a):
+        return pl.BlockSpec((*a.shape[:2], a.shape[2] // steps), lambda k: (0, 0, k))
+
     return pl.pallas_call(
-        qkv_back_kernel,
-        grid=(KV_HEADS,),
-        out_shape=[
-            jax.ShapeDtypeStruct((tokens, 2 * width), jnp.bfloat16),
-            jax.ShapeDtypeStruct((tokens, width), jnp.bfloat16),
-            jax.ShapeDtypeStruct((8, width), jnp.float32),
-        ],
-        in_specs=[
-            pl.BlockSpec((2, 1, tokens // 2, PACKED), lambda k: (0, k, 0, 0)),
-            *[whole_spec(t) for t in tables],
-            pl.BlockSpec((width, 4 * HEAD), lambda k: (0, k)),
-            whole_spec(x),
-            whole_spec(dmiddle),
-            whole_spec(gain),
-        ],
-        out_specs=[
-            pl.BlockSpec((tokens, 4 * HEAD), lambda k: (0, k)),
-            pl.BlockSpec((tokens, width), lambda k: (0, 0)),
-            pl.BlockSpec((8, width), lambda k: (0, 0)),
-        ],
-        scratch_shapes=[pltpu.VMEM((tokens, width), jnp.float32)],
-        compiler_params=pltpu.CompilerParams(vmem_limit_bytes=56 * MIB),
-        name="project_back",
-    )(back_in, *tables, w, x, dmiddle, gain)
+        outer_kernel,
+        grid=(steps,),
+        out_shape=[jax.ShapeDtypeStruct((a.shape[2], b.shape[2]), jnp.bfloat16) for a, b in pairs],
+        in_specs=[part(a) for a in (normed_two, attended, mixed)]
+        + [whole_spec(b) for b in (dgate, dup, db, g)],
+        out_specs=[pl.BlockSpec((a.shape[2] // steps, b.shape[2]), lambda k: (k, 0)) for a, b in pairs],
+        compiler_params=pltpu.CompilerParams(vmem_limit_bytes=40 * MIB),
+        name="outer_products",
+    )(normed_two, attended, mixed, dgate, dup, db, g)
 
 
 def hand_over_kernel(*refs):
@@ -1532,11 +1548,9 @@
 ):
     seqs, rows, width = inputs.shape
     tokens = seqs * rows
-    section = lax.axis_index("section")
     seq = lax.axis_index("seq")
     positions = seq * rows + jnp.arange(rows, dtype=jnp.int32)
     tables = rope_tables(jnp.concatenate([positions, positions]))
-    own_prefix = lax.dynamic_slice_in_dim(prefix, seq // 16, 1)
 
     part = w_query.shape[1]
     qkv_shard = jnp.concatenate(
@@ -1556,48 +1570,33 @@
     )
     x0 = inputs.reshape(tokens, width)
     gate_w, up_w, qkv_split, o_w, _, down_w, gains, att = enter(
-        own_prefix, x0, tables, [w_gate[0], w_up[0], qkv_shard, w_out[0], gain_shard, w_down[0]]
+        prefix, x0, tables, [w_gate[0], w_up[0], qkv_shard, w_out[0], gain_shard, w_down[0]]
     )
-    gate_w, up_w, qkv_w, o_w, down_w = (
-        w.reshape(-1, w.shape[-1]) for w in (gate_w, up_w, qkv_split, o_w, down_w)
-    )
+    gate_w, up_w, o_w, down_w = (w.reshape(-1, w.shape[-1]) for w in (gate_w, up_w, o_w, down_w))
     gain_attn, gain_mlp = gains[0], gains[1]
 
     def feed_forward(att, x):
         return mlp(att.reshape(2, KV_HEADS, 2, 16, PACKED), x, gain_mlp, o_w, gate_w, up_w, down_w)
 
     out0 = feed_forward(att, x0)[0]
-    received = lax.ppermute(out0, "section", [(0, 1)])
-    x = jnp.where(section == 0, x0, received)
-    normed, *kept, att = attend(own_prefix, x, gain_attn, tables, qkv_split)
+    x, normed, *kept, att = attend(prefix, out0, x0, gain_attn, tables, qkv_split)
     out, attended, middle, normed_two, gate, up, mixed = feed_forward(att, x)
 
     def feed_forward_back(g_low):
         return mlp_back(g_low, gate, up, middle, gain_mlp, o_w, gate_w, up_w, down_w)
 
-    def attention_back(back, dmiddle):
-        back = back.reshape(2, KV_HEADS, rows, PACKED)
-        return project_back(back, tables, qkv_w, x, dmiddle, gain_attn)
-
     g0 = cotangent.reshape(tokens, width)
     _, _, dmiddle, _, _, datt = feed_forward_back(g0)
-    back = attend_back(own_prefix, kept, datt.reshape(ORIGINS, 16, PACKED))
-    _, dx0, _ = attention_back(back, dmiddle)
-    received = lax.ppermute(dx0, "section", [(1, 0)])
-    g_low = jnp.where(section == 1, g0, received)
-
-    def outer(a, b):
-        a, b = a.reshape(2 * tokens, -1), b.reshape(2 * tokens, -1)
-        return lax.dot_general(
-            a, b, (((0,), (0,)), ((), ())), preferred_element_type=jnp.float32
-        ).astype(jnp.bfloat16)
+    g_low = attend_back(
+        prefix, kept, datt.reshape(ORIGINS, 16, PACKED), x, dmiddle, gain_attn, g0, tables, qkv_split
+    )
 
     dgate, dup, dmiddle, db, dgain_mlp, datt = feed_forward_back(g_low)
     normed_two, mixed, attended, g_half, dgate, dup, db = pair_up(
         6, [normed_two, mixed, attended], [g_low, dgate, dup, db]
     )
     gate_g, up_g, o_g, down_g, key_g, value_g, query_g, gain_g, dx, _, _ = leave(
-        own_prefix,
+        prefix,
         kept,
         datt.reshape(ORIGINS, 16, PACKED),
         x,
@@ -1607,7 +1606,7 @@
         dgain_mlp,
         tables,
         qkv_split,
-        [outer(normed_two, dgate), outer(normed_two, dup), outer(attended, db), outer(mixed, g_half)],
+        outer_products(normed_two, attended, mixed, dgate, dup, db, g_half),
     )
     dx, query_g, key_g, value_g, o_g, gate_g, up_g, down_g = hand_over(
         [dx, query_g, key_g, value_g, o_g, gate_g, up_g, down_g]

time: 595 us -> 570 us (0.958)
  waiting for transfers between devices: 20.3 us -> 0 us
  Pallas kernels: 528 us -> 545 us
  matrix products: 15.7 us -> 0 us
    pallas_call x3, Pallas kernels: 95.9 us -> 124 us  [the longest x1 65.3 us: attend_back(): pl.pallas_call(attend_back_kernel, out_shape=jax.ShapeDtypeStruct(x.shape...]
    ppermute x2 -> x0, waiting for transfers between devices: 20.3 us -> none  [the longest x1 11.7 us: body(): received = lax.ppermute(dx0, 'section', [(1, 0)])]
    dot_general x4 -> x0, matrix products: 15.7 us -> none  [outer(): lax.dot_general(a, b, (((0,), (0,)), ((), ())), preferred_element_type=jn...]
    pallas_call x1, Pallas kernels: 164 us -> 152 us  [leave(): pl.pallas_call(leave_kernel, out_shape=scatter_shapes(MAIN_ARRAYS) + [jax...]
  transfers between devices with their start and end apart: 2 -> 0, of which waited for: 2 -> 0; matrix products, arithmetic and copies ran while one was open for 0% -> 0% of each run, Pallas kernels for 0% -> 0%
where the time goes in v5:
time: 570 us; the launch traced here: 564 us
  Pallas kernels  545 us (96%)
  local copies, waits for them, and re-layouts  15.2 us (3%)
    pallas_call x1, Pallas kernels, enter(): pl.pallas_call(enter_kernel, out_shape=[jax.ShapeDtypeStruct((2, 4, 4, 2...  169 us
    pallas_call x1, Pallas kernels, leave(): pl.pallas_call(leave_kernel, out_shape=scatter_shapes(MAIN_ARRAYS) + [jax...  152 us
    pallas_call x1, Pallas kernels, attend_back(): pl.pallas_call(attend_back_kernel, out_shape=jax.ShapeDtypeStruct(x.shape...  65.3 us
    pallas_call x1, Pallas kernels, attend(): pl.pallas_call(attend_kernel, out_shape=[jax.ShapeDtypeStruct(own.shape,...  49.8 us
    pallas_call x2, Pallas kernels, mlp_back(): pl.pallas_call(mlp_back_kernel, grid=(STEPS,), out_shape=[jax.ShapeDtypeS...  48.2 us
    pallas_call x2, Pallas kernels, mlp(): pl.pallas_call(mlp_kernel, grid=(STEPS,), out_shape=[jax.ShapeDtypeStruct...  42.1 us

profile of v5, /device:TPU:1, one launch (start us, length us, event | category | flops | bytes accessed | tf_op | source)
XLA Modules:
  0.0 564.0 jit_solution(2652807635632949664)
XLA Ops:
  2.8 0.9 reshape_squeeze.9
  3.7 0.9 reshape_squeeze.10
  4.6 1.0 reshape_squeeze.11
  6.5 1.5 fusion
  8.0 169.3 %enter.1 = (bf16[2,4,4,48,4096]{4,3,2,1,0:T(8,128)(2,1)}, bf16[2,4,4,48,4096]{4,3,2,1,0:T(8,128)(2,1)}, bf16[2,4,4,48,3072]{4,3,2,1,0:T(8,128)(2,1)}, bf16[2,4,4...) custom-call(s32[2]{0:T(128)} %prefix.7, ...), custom_call_target="tpu_custom_call" | custom-call | tf_op jit(solution)/shard_map/enter/pallas_call | solution.py:950
  177.3 1.5 slice_bitcast_fusion
  178.8 21.2 %mlp.2 = (bf16[128,1536]{1,0:T(8,128)(2,1)}, bf16[128,1536]{1,0:T(8,128)(2,1)}, f32[128,1536]{1,0:T(8,128)}, bf16[128,1536]{1,0:T(8,128)(2,1)}, f32[128,4096]{1,...) custom-call(bf16[2,8,2,16,384]{4,3,2,1,0:T(8,128)(2,1)} %bitcast.59, bf16[128,1536]{1,0:T(8,128)(2,1)} %bitcast.55, ...), custom_call_target="tpu_custom_call" | custom-call | tf_op jit(solution)/shard_map/mlp/pallas_call | solution.py:1388
  200.0 49.8 %attend.1 = (bf16[128,1536]{1,0:T(8,128)(2,1)}, bf16[128,1536]{1,0:T(8,128)(2,1)}, bf16[2048,128]{1,0:T(8,128)(2,1)}, bf16[2048,128]{1,0:T(8,128)(2,1)}, bf16[2,...) custom-call(s32[2]{0:T(128)} %prefix.7, bf16[128,1536]{1,0:T(8,128)(2,1)} %get-tuple-element.74.made, ...), custom_call_target="tpu_custom_call" | custom-call | tf_op jit(solution)/shard_map/attend/pallas_call | solution.py:863
  249.7 21.0 %mlp.3 = (bf16[128,1536]{1,0:T(8,128)(2,1)}, bf16[128,1536]{1,0:T(8,128)(2,1)}, f32[128,1536]{1,0:T(8,128)}, bf16[128,1536]{1,0:T(8,128)(2,1)}, f32[128,4096]{1,...) custom-call(bf16[2,8,2,16,384]{4,3,2,1,0:T(8,128)(2,1)} %bitcast.60, bf16[128,1536]{1,0:T(8,128)(2,1)} %get-tuple-element.77.x, ...), custom_call_target="tpu_custom_call" | custom-call | tf_op jit(solution)/shard_map/mlp/pallas_call | solution.py:1388
  270.7 1.1 copy-done.2
  271.9 24.8 %mlp_back.2 = (bf16[128,4096]{1,0:T(8,128)(2,1)}, bf16[128,4096]{1,0:T(8,128)(2,1)}, f32[128,1536]{1,0:T(8,128)S(1)}, bf16[128,1536]{1,0:T(8,128)(2,1)}, f32[8,1...) custom-call(bf16[128,1536]{1,0:T(8,128)(2,1)S(1)} %bitcast.32, f32[128,4096]{1,0:T(8,128)} %get-tuple-element.82.gate, ...), custom_call_target="tpu_custom_call" | custom-call | tf_op jit(solution)/shard_map/mlp_back/pallas_call | solution.py:1461
  296.7 0.9 copy-done.9
  297.5 0.7 copy-done.11
  298.3 65.3 %attend_back.1.g_low.refs_3_ = bf16[128,1536]{1,0:T(8,128)(2,1)} custom-call(s32[2]{0:T(128)} %prefix.7, bf16[2048,128]{1,0:T(8,128)(2,1)} %get-tuple-element.79.keys, bf16[2048,128]{1,0:T(8,128)(2,1)} %get-tuple-element.80.values, bf16[2,1024,128]{2,1,0:T(8,128)(2,1)} %get-tuple-element.81.queries, bf16[32,16,384]{2,1,0:T(8,128)(2,1)} %bitcast.34, ...), custom_call_target="tpu_custom_call" | custom-call | tf_op jit(solution)/shard_map/attend_back/pallas_call | solution.py:1121
  363.7 1.0 copy-done
  364.7 23.4 %mlp_back.3 = (bf16[128,4096]{1,0:T(8,128)(2,1)S(1)}, bf16[128,4096]{1,0:T(8,128)(2,1)S(1)}, f32[128,1536]{1,0:T(8,128)S(1)}, bf16[128,1536]{1,0:T(8,128)(2,1)S(...) custom-call(bf16[128,1536]{1,0:T(8,128)(2,1)S(1)} %copy-done, f32[128,4096]{1,0:T(8,128)} %get-tuple-element.82.gate, ...), custom_call_target="tpu_custom_call" | custom-call | tf_op jit(solution)/shard_map/mlp_back/pallas_call | solution.py:1461
  388.1 0.9 copy-done.8
  389.0 0.7 copy-done.10
  390.3 6.7 %pair_up.1 = (bf16[2,128,1536]{2,1,0:T(8,128)(2,1)S(1)}, bf16[2,128,4096]{2,1,0:T(8,128)(2,1)S(1)}, bf16[2,128,1536]{2,1,0:T(8,128)(2,1)S(1)}, bf16[2,128,768]{2...) custom-call(bf16[128,1536]{1,0:T(8,128)(2,1)S(1)} %copy-done.13, ...), custom_call_target="tpu_custom_call" | custom-call | tf_op jit(solution)/shard_map/pair_up/pallas_call | solution.py:1311
  397.1 8.7 %outer_products.1 = (bf16[1536,2048]{1,0:T(8,128)(2,1)}, bf16[1536,2048]{1,0:T(8,128)(2,1)}, bf16[1536,768]{1,0:T(8,128)(2,1)S(1)}, bf16[4096,768]{1,0:T(8,128)(2,1)}) custom-call(bf16[2,128,1536]{2,1,0:T(8,128)(2,1)S(1)} %get-tuple-element.97.normed_two, bf16[2,128,1536]{2,1,0:T(8,128)(2,1)S(1)} %get-tuple-element.98.attended, ...), custom_call_target="tpu_custom_call" | custom-call | tf_op jit(solution)/shard_map/outer_products/pallas_call | solution.py:1515
  405.8 1.5 copy-done.4
  407.2 152.2 %leave.1 = (f32[24,4096]{1,0:T(8,128)}, f32[24,4096]{1,0:T(8,128)}, f32[24,1536]{1,0:T(8,128)}, f32[64,1536]{1,0:T(8,128)}, f32[24,768]{1,0:T(8,128)}, /*index=5...) custom-call(s32[2]{0:T(128)} %prefix.7, ...), custom_call_target="tpu_custom_call" | custom-call | tf_op jit(solution)/shard_map/leave/pallas_call | solution.py:1252
  559.4 2.8 hand_over.1
  562.2 1.4 slice_reduce_fusion
  (33 shorter events, 3.7 us)
Async XLA Ops:
  249.7 21.0 %copy-start.5 = (bf16[2,64,1536]{2,1,0:T(8,128)(2,1)S(1)}, bf16[2,64,1536]{2,1,0:T(8,128)(2,1)}, u32[]{:S(2)}) copy-start(bf16[2,64,1536]{2,1,0:T(8,128)(2,1)} %param.14) | copy-start | bytes 1179652
  249.7 21.0 %copy-start.6 = (f32[8,1536]{1,0:T(8,128)S(1)}, f32[8,1536]{1,0:T(8,128)}, u32[]{:S(2)}) copy-start(f32[8,1536]{1,0:T(8,128)} %get-tuple-element.128.gain) | copy-start | bytes 147460
  270.7 1.1 copy-start.2
  296.6 0.9 copy-start.9
  297.5 0.7 copy-start.11
  298.3 65.4 %copy-start.3 = (f32[128,1536]{1,0:T(8,128)S(1)}, f32[128,1536]{1,0:T(8,128)}, u32[]{:S(2)}) copy-start(f32[128,1536]{1,0:T(8,128)} %get-tuple-element.84.middle) | copy-start | bytes 2359300
  363.6 1.0 copy-start
  364.6 25.7 %copy-start.1 = (bf16[128,1536]{1,0:T(8,128)(2,1)S(1)}, bf16[128,1536]{1,0:T(8,128)(2,1)}, u32[]{:S(2)}) copy-start(bf16[128,1536]{1,0:T(8,128)(2,1)} %attend_back.1.g_low.refs_3_) | copy-start | bytes 1179652
  364.6 25.7 %copy-start.7 = (bf16[128,4096]{1,0:T(8,128)(2,1)S(1)}, bf16[128,4096]{1,0:T(8,128)(2,1)}, u32[]{:S(2)}) copy-start(bf16[128,4096]{1,0:T(8,128)(2,1)} %get-tuple-element.92.refs_1_) | copy-start | bytes 3145732
  364.6 25.7 %copy-start.12 = (bf16[128,1536]{1,0:T(8,128)(2,1)S(1)}, bf16[128,1536]{1,0:T(8,128)(2,1)}, u32[]{:S(2)}) copy-start(bf16[128,1536]{1,0:T(8,128)(2,1)} %get-tuple-element.93.refs_2_) | copy-start | bytes 1179652
  364.6 25.7 %copy-start.13 = (bf16[128,1536]{1,0:T(8,128)(2,1)S(1)}, bf16[128,1536]{1,0:T(8,128)(2,1)}, u32[]{:S(2)}) copy-start(bf16[128,1536]{1,0:T(8,128)(2,1)} %get-tuple-element.91.refs_0_) | copy-start | bytes 1179652
  388.1 0.9 copy-start.8
  389.0 0.7 copy-start.10
  389.7 0.6 copy-start.14
  405.8 1.5 copy-start.4
